TPU v7x, 512 devices: a whole 4x4x16 slice. The times are simulated.
512 devices in a mesh: seg: 32 (over z, y_lo), trait: 16 (over y_hi, x, core).
Axes of the slice: x: 4, y: 4 (y_hi: 2, y_lo: 2; y = y_hi * 2 + y_lo), z: 16, core: 2. Of those that a mesh axis runs over, the one named last changes fastest.
Arguments:
- effects: bfloat16 [16, 192, 32768], P(None, 'trait', 'seg'), may hold values from -6 to 6
- precision: float32 [192, 192], replicated, may hold values from -0.4375 to 0.4375
- band: bfloat16 [32768, 2048], P('seg'), may hold values from -0.15625 to 0.15625
Outputs:
- rhs: bfloat16 [16, 192, 32768], P(None, 'trait', 'seg')
All inputs are finite; a program needn't handle non-finite values.
Results may differ from a plain program's by a relative error of at most 0.007.
Values may be sent and summed in bfloat16 or wider, within the bound.
No kernel may reach another device: no remote copies, remote signals or barrier semaphores. Data moves between devices by JAX's collectives and lax.ppermute only.
A program may use at most 64 MiB of HBM per device.

v0:
```python
import jax
import jax.numpy as jnp
from jax import lax
from jax.sharding import PartitionSpec as P


def passed_along(shard, axis, by):
    length = lax.axis_size(axis)
    pairs = [(i, i + by) for i in range(length) if 0 <= i + by < length]
    return lax.ppermute(shard, axis, pairs)


def skew_band(rows):
    seg_rows, width = rows.shape
    padded = jnp.pad(rows, ((0, 0), (1, seg_rows)))
    span = width + 1 + seg_rows
    flat_band = padded.reshape(-1)[: seg_rows * (span - 1)]
    return flat_band.reshape(seg_rows, span - 1)


def contract_rows(values, dense_block):
    return lax.dot_general(
        values, dense_block, (((1,), (1,)), ((), ())), preferred_element_type=jnp.float32
    )


def local(effects, precision, band):
    chains, local_traits, seg_rows = effects.shape
    width = band.shape[1]
    precision_cols = lax.dynamic_slice_in_dim(
        precision, lax.axis_index("trait") * local_traits, local_traits, 1
    )
    mixed = jnp.einsum(
        "kj,ckm->cjm",
        precision_cols,
        lax.all_gather(effects, "trait", axis=1, tiled=True).astype(jnp.float32),
        precision=lax.Precision.HIGHEST,
    ).astype(jnp.bfloat16)
    columns = chains * local_traits
    mixed_rows = mixed.reshape(columns, seg_rows)
    dense = skew_band(band)
    reach = min(width // seg_rows, lax.axis_size("seg") - 1)
    lower_part = jnp.dot(mixed_rows, dense, preferred_element_type=jnp.float32)
    total = mixed_rows.astype(jnp.float32) + lower_part[:, :seg_rows]
    total = total + contract_rows(mixed_rows, dense[:, :seg_rows])
    fetched = mixed_rows
    for step in range(1, reach + 1):
        fetched = passed_along(fetched, "seg", -1)
        total = total + contract_rows(fetched, dense[:, step * seg_rows : (step + 1) * seg_rows])
    carried = jnp.zeros((columns, seg_rows), jnp.float32)
    for step in range(reach, 0, -1):
        carried = passed_along(
            (carried + lower_part[:, step * seg_rows : (step + 1) * seg_rows]).astype(jnp.bfloat16),
            "seg",
            1,
        ).astype(jnp.float32)
    total = total + carried
    return total.astype(jnp.bfloat16).reshape(chains, local_traits, seg_rows)


def solution(mesh):
    in_specs = (P(None, "trait", "seg"), P(), P("seg", None))
    out_specs = P(None, "trait", "seg")
    return jax.shard_map(local, mesh=mesh, in_specs=in_specs, out_specs=out_specs, check_vma=False)
```

profile of v0, /device:TPU:8, one launch (start us, length us, event | category | flops | bytes accessed | tf_op | source)
XLA Modules:
  0.0 161.0 jit_solution(18022838221653044917)
XLA Ops:
  6.5 0.7 all-gather.2.cloned.1.call-update
  7.3 7.3 %pad.4 = bf16[1024,3073]{1,0:T(8,128)(2,1)} pad(bf16[1024,2048]{1,0:T(8,128)(2,1)} %param.5, bf16[]{:T(256)} %constant.11.clone.1), padding=0_0x1_1024 | pad | bytes 10487810 | tf_op jit(solution)/shard_map/jit(_pad)/pad | solution.py:15
  14.6 15.8 %reshape.13 = bf16[3146752]{0:T(1024)(128)(2,1)} reshape(bf16[1024,3073]{1,0:T(8,128)(2,1)} %pad.4) | data formatting | bytes 12587008 | tf_op jit(solution)/shard_map/reshape | solution.py:17
  30.4 6.5 %slice.29 = bf16[3145728]{0:T(1024)(128)(2,1)} slice(bf16[3146752]{0:T(1024)(128)(2,1)} %reshape.13), slice={[0:3145728]} | slice | bytes 12582912 | tf_op jit(solution)/shard_map/slice | solution.py:17
  36.9 10.3 %reshape.14 = bf16[1024,3072]{1,0:T(8,128)(2,1)} reshape(bf16[3145728]{0:T(1024)(128)(2,1)} %slice.29) | data formatting | bytes 12582912 | tf_op jit(solution)/shard_map/reshape | solution.py:18
  47.2 46.6 %all-gather.2.cloned.1.call-done = bf16[16,192,1024]{2,0,1:T(8,128)(2,1)} async-done(((bf16[16,12,1024]{2,0,1:T(8,128)(2,1)}), bf16[16,192,1024]{2,0,1:T(8,128)(2,1)}) %all-gather.2.cloned.1.call-update) | async-done | bytes 6291472 | tf_op jit(solution)/shard_map/all_gather | solution.py:36
  93.8 11.4 %fusion.26 = bf16[16,12,1024]{2,1,0:T(8,128)(2,1)S(1)} fusion(bf16[16,192,1024]{2,0,1:T(8,128)(2,1)} %all-gather.2.cloned.1.call-done, f32[192,192]{1,0:T(8,128)S(1)} %copy-done, s32[]{:T(128)S(6)} %select_n.3), kind=kOutput, calls=%fused_computation.14 | convolution fusion | flops 453181440 | bytes 6782980 | tf_op jit(solution)/shard_map/kj,ckm->cjm/dot_general | solution.py:33
  105.3 0.1 reshape.12
  105.4 0.0 slice-start.1
  105.4 4.3 %fusion.33 = f32[192,3072]{1,0:T(8,128)S(1)} fusion(bf16[192,1024]{1,0:T(8,128)(2,1)S(1)} %reshape.12, bf16[1024,3072]{1,0:T(8,128)(2,1)} %reshape.14), kind=kOutput, calls=%fused_computation.22 | convolution fusion | flops 1207959552 | bytes 9043968 | tf_op jit(solution)/shard_map/dot_general | solution.py:43
  109.8 4.3 %collective-permute-start.2 = (bf16[192,1024]{1,0:T(8,128)(2,1)S(1)}, bf16[192,1024]{1,0:T(8,128)(2,1)S(1)}, u32[]{:S(2)}, u32[]{:S(2)}) collective-permute-start(bf16[192,1024]{1,0:T(8,128)(2,1)S(1)} %slice.59), channel_id=1, source_target_pairs={{0,16},{16,32},{32,48},{48,64},{64,80},{80,96},{96,112},{112,128},... | collective-permute-start | bytes 1179656 | tf_op jit(solution)/shard_map/ppermute | solution.py:10
  114.1 1.9 %collective-permute-start = (bf16[192,1024]{1,0:T(8,128)(2,1)S(1)}, bf16[192,1024]{1,0:T(8,128)(2,1)S(1)}, u32[]{:S(2)}, u32[]{:S(2)}) collective-permute-start(bf16[192,1024]{1,0:T(8,128)(2,1)S(1)} %reshape.12), channel_id=1, source_target_pairs={{16,0},{32,16},{48,32},{64,48},{80,64},{96,80},{112,96},{128,112},... | collective-permute-start | bytes 1179656 | tf_op jit(solution)/shard_map/ppermute | solution.py:10
  116.0 15.3 %collective-permute-done.2 = bf16[192,1024]{1,0:T(8,128)(2,1)S(1)} collective-permute-done((bf16[192,1024]{1,0:T(8,128)(2,1)S(1)}, bf16[192,1024]{1,0:T(8,128)(2,1)S(1)}, u32[]{:S(2)}, u32[]{:S(2)}) %collective-permute-start.2) | collective-permute-done | bytes 393248 | tf_op jit(solution)/shard_map/ppermute | solution.py:10
  131.3 0.1 fusion.29
  131.5 2.4 %collective-permute-start.3 = (bf16[192,1024]{1,0:T(8,128)(2,1)S(1)}, bf16[192,1024]{1,0:T(8,128)(2,1)S(1)}, u32[]{:S(2)}, u32[]{:S(2)}) collective-permute-start(bf16[192,1024]{1,0:T(8,128)(2,1)S(1)} %fusion.29), channel_id=1, source_target_pairs={{0,16},{16,32},{32,48},{48,64},{64,80},{80,96},{96,112},{112,128},... | collective-permute-start | bytes 1179656 | tf_op jit(solution)/shard_map/ppermute | solution.py:10
  133.9 0.0 collective-permute-done
  133.9 3.4 %collective-permute-start.1 = (bf16[192,1024]{1,0:T(8,128)(2,1)S(1)}, bf16[192,1024]{1,0:T(8,128)(2,1)S(1)}, u32[]{:S(2)}, u32[]{:S(2)}) collective-permute-start(bf16[192,1024]{1,0:T(8,128)(2,1)S(1)} %collective-permute-done), channel_id=1, source_target_pairs={{16,0},{32,16},{48,32},{64,48},{80,64},{96,80},{112,96},{128,112},... | collective-permute-start | bytes 1179656 | tf_op jit(solution)/shard_map/ppermute | solution.py:10
  137.4 0.9 fusion.11
  138.2 0.9 fusion.14
  139.1 13.1 %collective-permute-done.3 = bf16[192,1024]{1,0:T(8,128)(2,1)S(1)} collective-permute-done((bf16[192,1024]{1,0:T(8,128)(2,1)S(1)}, bf16[192,1024]{1,0:T(8,128)(2,1)S(1)}, u32[]{:S(2)}, u32[]{:S(2)}) %collective-permute-start.3) | collective-permute-done | bytes 393248 | tf_op jit(solution)/shard_map/ppermute | solution.py:10
  152.2 0.0 collective-permute-done.1
  152.2 0.9 fusion.23
  153.1 0.1 reshape.15
  153.2 1.0 copy.12
  (8 shorter events, 0.1 us)
Async XLA Ops:
  6.5 87.3 %copy-start = (f32[192,192]{1,0:T(8,128)S(1)}, f32[192,192]{1,0:T(8,128)}, u32[]{:S(2)}) copy-start(f32[192,192]{1,0:T(8,128)} %param.4) | copy-start | bytes 442372
  6.5 87.3 %all-gather.2.cloned.1.call-start = ((), (), s32[]{:S(2)}) async-start(), calls=%async_computation | async-start | bytes 6684672 | tf_op jit(solution)/shard_map/all_gather | solution.py:36
  105.3 32.1 %slice-start = ((s8[6291456]{0:T(1024)(128)(4,1)}), s8[2097152]{0:T(1024)(128)(4,1)S(1)}, s32[]{:S(2)}) async-start(s8[6291456]{0:T(1024)(128)(4,1)} %bitcast.11), calls=%async_computation.1 | async-start | bytes 4194304
  105.4 32.0 %slice-start.1 = ((s8[6291456]{0:T(1024)(128)(4,1)}), s8[4194304]{0:T(1024)(128)(4,1)S(1)}, s32[]{:S(2)}) async-start(s8[6291456]{0:T(1024)(128)(4,1)} %bitcast.11), calls=%async_computation.2 | async-start | bytes 8388608
  109.8 21.6 %collective-permute-start.2 = (bf16[192,1024]{1,0:T(8,128)(2,1)S(1)}, bf16[192,1024]{1,0:T(8,128)(2,1)S(1)}, u32[]{:S(2)}, u32[]{:S(2)}) collective-permute-start(bf16[192,1024]{1,0:T(8,128)(2,1)S(1)} %slice.59), channel_id=1, source_target_pairs={{0,16},{16,32},{32,48},{48,64},{64,80},{80,96},{96,112},{112,128},... | collective-permute-start | bytes 1179656 | tf_op jit(solution)/shard_map/ppermute | solution.py:10
  114.1 19.8 %collective-permute-start = (bf16[192,1024]{1,0:T(8,128)(2,1)S(1)}, bf16[192,1024]{1,0:T(8,128)(2,1)S(1)}, u32[]{:S(2)}, u32[]{:S(2)}) collective-permute-start(bf16[192,1024]{1,0:T(8,128)(2,1)S(1)} %reshape.12), channel_id=1, source_target_pairs={{16,0},{32,16},{48,32},{64,48},{80,64},{96,80},{112,96},{128,112},... | collective-permute-start | bytes 1179656 | tf_op jit(solution)/shard_map/ppermute | solution.py:10
  131.5 20.8 %collective-permute-start.3 = (bf16[192,1024]{1,0:T(8,128)(2,1)S(1)}, bf16[192,1024]{1,0:T(8,128)(2,1)S(1)}, u32[]{:S(2)}, u32[]{:S(2)}) collective-permute-start(bf16[192,1024]{1,0:T(8,128)(2,1)S(1)} %fusion.29), channel_id=1, source_target_pairs={{0,16},{16,32},{32,48},{48,64},{64,80},{80,96},{96,112},{112,128},... | collective-permute-start | bytes 1179656 | tf_op jit(solution)/shard_map/ppermute | solution.py:10
  133.9 18.3 %collective-permute-start.1 = (bf16[192,1024]{1,0:T(8,128)(2,1)S(1)}, bf16[192,1024]{1,0:T(8,128)(2,1)S(1)}, u32[]{:S(2)}, u32[]{:S(2)}) collective-permute-start(bf16[192,1024]{1,0:T(8,128)(2,1)S(1)} %collective-permute-done), channel_id=1, source_target_pairs={{16,0},{32,16},{48,32},{64,48},{80,64},{96,80},{112,96},{128,112},... | collective-permute-start | bytes 1179656 | tf_op jit(solution)/shard_map/ppermute | solution.py:10
Sparse Core Ops, SparseCore 0:
  10.7 83.0 all-gather.1
where the time goes:
time: 162 us; the launch traced here: 161 us
  waiting for transfers between devices  75.8 us (47%)
  local copies, waits for them, and re-layouts  41.1 us (25%)
  matrix products  18.3 us (11%)
  between operations  13.5 us (8%)
  starting transfers between devices  12.1 us (7%)
    all_gather x1, waiting for transfers between devices, local(): lax.all_gather(effects, 'trait', axis=1, tiled=True).astype(jnp.float32)  46.6 us
    ppermute x4, waiting for transfers between devices, passed_along(): return lax.ppermute(shard, axis, pairs)  28.5 us
    reshape x1, local copies, waits for them, and re-layouts, skew_band(): flat_band = padded.reshape(-1)[:seg_rows * (span - 1)]  15.8 us
    ppermute x4, starting transfers between devices, passed_along(): return lax.ppermute(shard, axis, pairs)  12.1 us
    dot_general x1, matrix products, local(): jnp.einsum('kj,ckm->cjm', precision_cols, lax.all_gather(effects, 'trait'...  11.4 us
    reshape x1, local copies, waits for them, and re-layouts, skew_band(): return flat_band.reshape(seg_rows, span - 1)  10.3 us
    pad x1, local copies, waits for them, and re-layouts, skew_band(): padded = jnp.pad(rows, ((0, 0), (1, seg_rows)))  7.3 us
    slice x1, local copies, waits for them, and re-layouts, skew_band(): flat_band = padded.reshape(-1)[:seg_rows * (span - 1)]  6.48 us
  transfers between devices with their start and end apart: 5, of which 3 were waited for; matrix products, arithmetic and copies ran while one was open for 26% of the time, Pallas kernels for 0%

commit v1 on v0

v1 whole, which is shorter than its diff:
```python
import jax
import jax.numpy as jnp
from jax import lax
from jax.experimental import pallas as pl
from jax.experimental.pallas import tpu as pltpu
from jax.sharding import PartitionSpec as P

F32 = jnp.float32
BF16 = jnp.bfloat16
LANES = 128
MIB = 1 << 20


def vmem_specs(count):
    return [pl.BlockSpec(memory_space=pltpu.VMEM)] * count


def params(mib):
    return pltpu.CompilerParams(vmem_limit_bytes=mib * MIB)


def pack_kernel(x_ref, o_ref, wide):
    m = x_ref.shape[1]
    blocks = m // LANES
    for k in range(blocks):
        wide[k] = x_ref[:, k * LANES : (k + 1) * LANES].astype(F32)
    for c in range(0, 16, 2):
        rows = pl.ds(8 * c, 16)
        for k in range(blocks):
            parts = [wide[k, pl.ds(d, 8, stride=16), :] for d in (c, c + 1)]
            o_ref[rows, k * LANES : (k + 1) * LANES] = jnp.concatenate(parts, 0).astype(BF16)
        for k in range(blocks // 2):
            parts = [
                wide[k + h, pl.ds(128 + d, 4, stride=16), :] for d in (c, c + 1) for h in (0, blocks // 2)
            ]
            o_ref[rows, m + k * LANES : m + (k + 1) * LANES] = jnp.concatenate(parts, 0).astype(BF16)


def unpack_kernel(x_ref, o_ref, wide):
    m = o_ref.shape[1]
    blocks = m // LANES
    for k in range(wide.shape[0]):
        wide[k] = x_ref[:, k * LANES : (k + 1) * LANES].astype(F32)
    for k in range(blocks):
        lanes = pl.ds(k * LANES, LANES)
        for j in range(8):
            o_ref[16 * j : 16 * j + 16, lanes] = wide[k, pl.ds(j, 16, stride=8), :].astype(BF16)
        half, place = divmod(k, blocks // 2)
        for j in range(4):
            tail = wide[blocks + place, pl.ds(j + 4 * half, 16, stride=8), :]
            o_ref[128 + 16 * j : 144 + 16 * j, lanes] = tail.astype(BF16)


def mix_kernel(x_ref, p_ref, o_ref):
    m = o_ref.shape[1]
    half = m // 2
    blank = jnp.zeros((4, p_ref.shape[1]), F32)
    heads, lows, highs = [], [], []
    for t in range(16):
        heads.append(p_ref[12 * t : 12 * t + 8, :])
        tail = p_ref[12 * t + 8 : 12 * t + 12, :]
        lows += [tail, blank]
        highs += [blank, tail]
    head = jnp.concatenate(heads, 0)
    for first, tails in ((0, lows), (half, highs)):
        weights = jnp.concatenate([head, jnp.concatenate(tails, 0)], 0).T
        upper = weights.astype(BF16)
        lower = (weights - upper.astype(F32)).astype(BF16)
        values = jnp.concatenate([x_ref[:, first : first + half], x_ref[:, m:]], 0)
        total = jnp.dot(upper, values, preferred_element_type=F32)
        total += jnp.dot(lower, values, preferred_element_type=F32)
        o_ref[:, first : first + half] = total.astype(BF16)


def skew_rows(band_ref, dense_ref, first):
    rows = pl.ds(first, LANES)
    blocks = band_ref.shape[1] // LANES
    a = lax.broadcasted_iota(jnp.int32, (LANES, LANES), 0)
    b = lax.broadcasted_iota(jnp.int32, (LANES, LANES), 1)
    beyond = b > a
    before = jnp.zeros((LANES, LANES), F32)
    for d in range(blocks + 1):
        if d < blocks:
            tile = band_ref[rows, d * LANES : (d + 1) * LANES].astype(F32)
            now = pltpu.roll(tile, 1, 1, stride=1, stride_axis=0)
        else:
            now = jnp.zeros((LANES, LANES), F32)
        dense_ref[rows, pl.ds(first + d * LANES, LANES)] = jnp.where(beyond, now, before).astype(BF16)
        before = now


def lower_kernel(x_ref, band_ref, dense_ref, own_ref, near_ref, far_ref):
    m, width = band_ref.shape
    depth = 256
    for first in range(0, m, LANES):
        skew_rows(band_ref, dense_ref, first)
        zero = jnp.zeros((LANES, LANES), BF16)
        if first % depth:
            dense_ref[pl.ds(first, LANES), pl.ds(first - LANES, LANES)] = zero
        else:
            dense_ref[pl.ds(first, LANES), pl.ds(first + width + LANES, LANES)] = zero
    for col in range(0, m + width, depth):
        low = max(0, col - width)
        high = min(m, col + depth)
        part = jnp.dot(
            x_ref[:, low:high], dense_ref[low:high, col : col + depth], preferred_element_type=F32
        )
        if col < m:
            own_ref[:, col : col + depth] = part + x_ref[:, col : col + depth].astype(F32)
        elif col < 2 * m:
            near_ref[:, col - m : col - m + depth] = part.astype(BF16)
        else:
            far_ref[:, col - 2 * m : col - 2 * m + depth] = part.astype(BF16)


def contract(values, dense):
    return lax.dot_general(values, dense, (((1,), (1,)), ((), ())), preferred_element_type=F32)


def upper_kernel(x_ref, near_ref, far_ref, dense_ref, own_ref, o_ref):
    rows, m = x_ref.shape
    depth = 256
    for i in range(0, m, depth):
        d = dense_ref.at[i : i + depth, :]
        total = own_ref[:, i : i + depth]
        total += contract(x_ref[:, i:], d[:, i:m])
        total += contract(near_ref[...], d[:, m : 2 * m])
        total += contract(far_ref[:, : i + depth], d[:, 2 * m : 2 * m + i + depth])
        o_ref[:, i : i + depth] = total


def finish_kernel(total_ref, near_ref, far_ref, o_ref, wide):
    m = total_ref.shape[1]
    half = m // 2
    wide[...] = total_ref[...] + near_ref[...].astype(F32) + far_ref[...].astype(F32)
    for t in range(0, 16, 2):
        parts = []
        for u in (t, t + 1):
            head = wide[12 * u : 12 * u + 8, :]
            left = wide[12 * u + 8 : 12 * u + 12, :half]
            right = wide[12 * u + 8 : 12 * u + 12, half:]
            parts.append(jnp.concatenate([head, jnp.concatenate([left, right], 0)], 1))
        o_ref[8 * t : 8 * t + 16, :] = jnp.concatenate(parts, 0).astype(BF16)


def call(kernel, name, outs, mib, *args, scratch=(), flops=0):
    several = isinstance(outs, tuple)
    size = sum(a.size * a.dtype.itemsize for a in args)
    return pl.pallas_call(
        kernel,
        out_shape=outs,
        in_specs=vmem_specs(len(args)),
        out_specs=tuple(vmem_specs(len(outs))) if several else vmem_specs(1)[0],
        scratch_shapes=list(scratch),
        compiler_params=params(mib),
        cost_estimate=pl.CostEstimate(flops=flops, bytes_accessed=size, transcendentals=0),
        name=name,
    )(*args)


def passed_along(shard, by):
    length = lax.axis_size("seg")
    pairs = [(i, i + by) for i in range(length) if 0 <= i + by < length]
    return lax.ppermute(shard, "seg", pairs)


def exchange(packed):
    rows, lanes = packed.shape
    moved = lax.all_to_all(packed.reshape(16, rows // 16, lanes), "trait", 0, 0, tiled=True)
    return moved.reshape(rows, lanes)


def local(effects, precision, band):
    chains, traits, m = effects.shape
    width = band.shape[1]
    rows = chains * traits
    packed_shape = (8 * chains, m + m // 2)
    struct = jax.ShapeDtypeStruct

    flat = effects.transpose(1, 0, 2).reshape(rows, m)
    packed = call(
        pack_kernel, "pack", struct(packed_shape, BF16), 8, flat,
        scratch=[pltpu.VMEM((m // LANES, rows, LANES), F32)],
    )
    mixed = call(mix_kernel, "mix", struct((rows, m), BF16), 8, exchange(packed), precision)
    far = passed_along(mixed, -2)
    near = passed_along(mixed, -1)
    dense, own, low_near, low_far = call(
        lower_kernel,
        "lower",
        (
            struct((m, m + width), BF16),
            struct((rows, m), F32),
            struct((rows, m), BF16),
            struct((rows, m), BF16),
        ),
        16,
        mixed,
        band,
        flops=2 * rows * m * width,
    )
    low_far = passed_along(low_far, 2)
    low_near = passed_along(low_near, 1)
    total = call(
        upper_kernel, "upper", struct((rows, m), F32), 16, mixed, near, far, dense, own,
        flops=2 * rows * m * width,
    )
    packed = call(
        finish_kernel, "finish", struct(packed_shape, BF16), 8, total, low_near, low_far,
        scratch=[pltpu.VMEM((rows, m), F32)],
    )
    flat = call(
        unpack_kernel, "unpack", struct((rows, m), BF16), 8, exchange(packed),
        scratch=[pltpu.VMEM((packed_shape[1] // LANES, packed_shape[0], LANES), F32)],
    )
    return flat.reshape(traits, chains, m).transpose(1, 0, 2)


def solution(mesh):
    in_specs = (P(None, "trait", "seg"), P(), P("seg", None))
    out_specs = P(None, "trait", "seg")
    return jax.shard_map(local, mesh=mesh, in_specs=in_specs, out_specs=out_specs, check_vma=False)
```

time: 162 us -> 68.6 us (0.42)
  the two profiles are of different devices: /device:TPU:8 before, /device:TPU:392 now
where the time goes in v1:
time: 68.6 us; the launch traced here: 68.2 us
  blocking collectives  30.6 us (45%)
  waiting for transfers between devices  14.9 us (22%)
  starting transfers between devices  12.8 us (19%)
  Pallas kernels  5.74 us (8%)
  local copies, waits for them, and re-layouts  4.11 us (6%)
    all_to_all x2, blocking collectives, exchange(): lax.all_to_all(packed.reshape(16, rows // 16, lanes), 'trait', 0, 0, tile...  30.6 us
    ppermute x4, waiting for transfers between devices, passed_along(): return lax.ppermute(shard, 'seg', pairs)  14.9 us
    ppermute x4, starting transfers between devices, passed_along(): return lax.ppermute(shard, 'seg', pairs)  12.8 us
    pallas_call x6, Pallas kernels, call(): pl.pallas_call(kernel, out_shape=outs, in_specs=vmem_specs(len(args)), ou...  5.74 us
    unnamed x6, local copies, waits for them, and re-layouts  4.11 us
  transfers between devices with their start and end apart: 4, of which 3 were waited for; matrix products, arithmetic and copies ran while one was open for 0% of the time, Pallas kernels for 6%

profile of v1, /device:TPU:392, one launch (start us, length us, event | category | flops | bytes accessed | tf_op | source)
XLA Modules:
  0.0 68.2 jit_solution(14759936210084554110)
XLA Ops:
  0.0 0.0 copy-start.1
  0.0 1.0 %copy-done.1 = bf16[16,12,1024]{2,0,1:T(8,128)(2,1)S(1)} copy-done((bf16[16,12,1024]{2,0,1:T(8,128)(2,1)S(1)}, bf16[16,12,1024]{2,0,1:T(8,128)(2,1)}, u32[]{:S(2)}) %copy-start.1) | copy-done | bytes 393240
  1.0 0.3 pack.1
  1.3 16.7 %all_to_all.10 = bf16[16,8,1536]{2,1,0:T(8,128)(2,1)S(1)} all-to-all(bf16[16,8,1536]{2,1,0:T(8,128)(2,1)S(1)} %bitcast.11), channel_id=1, replica_groups=mesh['seg'=32,'trait'=16] {'trait'}, dimensions={0} | all-to-all | bytes 786432 | tf_op jit(solution)/shard_map/all_to_all | solution.py:169
  18.0 0.0 copy-start.2
  18.0 0.9 %copy-done.2 = f32[192,192]{1,0:T(8,128)S(1)} copy-done((f32[192,192]{1,0:T(8,128)S(1)}, f32[192,192]{1,0:T(8,128)}, u32[]{:S(2)}) %copy-start.2) | copy-done | bytes 147480
  18.9 0.4 mix.1.x_ref
  19.3 4.1 %collective-permute-start.1 = (bf16[192,1024]{1,0:T(8,128)(2,1)S(1)}, bf16[192,1024]{1,0:T(8,128)(2,1)S(1)}, u32[]{:S(2)}, u32[]{:S(2)}) collective-permute-start(bf16[192,1024]{1,0:T(8,128)(2,1)S(1)} %mix.1.x_ref), channel_id=1, source_target_pairs={{32,0},{48,16},{64,32},{80,48},{96,64},{112,80},{128,96},{144,112}... | collective-permute-start | bytes 1179656 | tf_op jit(solution)/shard_map/ppermute | solution.py:164
  23.5 3.2 %collective-permute-start = (bf16[192,1024]{1,0:T(8,128)(2,1)S(1)}, bf16[192,1024]{1,0:T(8,128)(2,1)S(1)}, u32[]{:S(2)}, u32[]{:S(2)}) collective-permute-start(bf16[192,1024]{1,0:T(8,128)(2,1)S(1)} %mix.1.x_ref), channel_id=1, source_target_pairs={{16,0},{32,16},{48,32},{64,48},{80,64},{96,80},{112,96},{128,112},... | collective-permute-start | bytes 1179656 | tf_op jit(solution)/shard_map/ppermute | solution.py:164
  26.7 0.0 copy-start
  26.7 2.2 %copy-done = bf16[1024,2048]{1,0:T(8,128)(2,1)S(1)} copy-done((bf16[1024,2048]{1,0:T(8,128)(2,1)S(1)}, bf16[1024,2048]{1,0:T(8,128)(2,1)}, u32[]{:S(2)}) %copy-start) | copy-done | bytes 4194328
  28.9 2.2 %lower.1 = (bf16[1024,3072]{1,0:T(8,128)(2,1)S(1)}, f32[192,1024]{1,0:T(8,128)S(1)}, bf16[192,1024]{1,0:T(8,128)(2,1)S(1)}, bf16[192,1024]{1,0:T(8,128)(2,1)S(1)}) custom-call(bf16[192,1024]{1,0:T(8,128)(2,1)S(1)} %mix.1.x_ref, bf16[1024,2048]{1,0:T(8,128)(2,1)S(1)} %copy-done), custom_call_target="tpu_custom_call" | custom-call | flops 805306368 | bytes 4587520 | tf_op jit(solution)/shard_map/lower/pallas_call | solution.py:149
  31.1 3.5 %collective-permute-start.2 = (bf16[192,1024]{1,0:T(8,128)(2,1)S(1)}, bf16[192,1024]{1,0:T(8,128)(2,1)S(1)}, u32[]{:S(2)}, u32[]{:S(2)}) collective-permute-start(bf16[192,1024]{1,0:T(8,128)(2,1)S(1)} %get-tuple-element.11), channel_id=1, source_target_pairs={{0,16},{16,32},{32,48},{48,64},{64,80},{80,96},{96,112},{112,128},... | collective-permute-start | bytes 1179656 | tf_op jit(solution)/shard_map/ppermute | solution.py:164
  34.6 1.9 %collective-permute-start.3 = (bf16[192,1024]{1,0:T(8,128)(2,1)S(1)}, bf16[192,1024]{1,0:T(8,128)(2,1)S(1)}, u32[]{:S(2)}, u32[]{:S(2)}) collective-permute-start(bf16[192,1024]{1,0:T(8,128)(2,1)S(1)} %get-tuple-element.12), channel_id=1, source_target_pairs={{0,32},{16,48},{32,64},{48,80},{64,96},{80,112},{96,128},{112,144}... | collective-permute-start | bytes 1179656 | tf_op jit(solution)/shard_map/ppermute | solution.py:164
  36.5 0.0 collective-permute-done.1.far_ref
  36.5 4.5 %collective-permute-done.near_ref = bf16[192,1024]{1,0:T(8,128)(2,1)S(1)} collective-permute-done((bf16[192,1024]{1,0:T(8,128)(2,1)S(1)}, bf16[192,1024]{1,0:T(8,128)(2,1)S(1)}, u32[]{:S(2)}, u32[]{:S(2)}) %collective-permute-start) | collective-permute-done | bytes 393248 | tf_op jit(solution)/shard_map/ppermute | solution.py:164
  41.0 1.7 %upper.1.total_ref = f32[192,1024]{1,0:T(8,128)S(1)} custom-call(bf16[192,1024]{1,0:T(8,128)(2,1)S(1)} %mix.1.x_ref, bf16[192,1024]{1,0:T(8,128)(2,1)S(1)} %collective-permute-done.near_ref, bf16[192,1024]{1,0:T(8,128)(2,1)S(1)} %collective-permute-done.1.far_ref, bf16[1024,3072]{1,0:T(8,128)(2,1)S(1)} %get-tuple-element.9.dense_ref, ...), custom_call_target="tpu_custom_call" | custom-call | flops 805306368 | bytes 8257536 | tf_op jit(solution)/shard_map/upper/pallas_call | solution.py:149
  42.7 6.7 %collective-permute-done.2.near_ref = bf16[192,1024]{1,0:T(8,128)(2,1)S(1)} collective-permute-done((bf16[192,1024]{1,0:T(8,128)(2,1)S(1)}, bf16[192,1024]{1,0:T(8,128)(2,1)S(1)}, u32[]{:S(2)}, u32[]{:S(2)}) %collective-permute-start.2) | collective-permute-done | bytes 393248 | tf_op jit(solution)/shard_map/ppermute | solution.py:164
  49.3 3.8 %collective-permute-done.3.far_ref = bf16[192,1024]{1,0:T(8,128)(2,1)S(1)} collective-permute-done((bf16[192,1024]{1,0:T(8,128)(2,1)S(1)}, bf16[192,1024]{1,0:T(8,128)(2,1)S(1)}, u32[]{:S(2)}, u32[]{:S(2)}) %collective-permute-start.3) | collective-permute-done | bytes 393248 | tf_op jit(solution)/shard_map/ppermute | solution.py:164
  53.1 0.2 finish.1
  53.3 14.0 %all_to_all.11 = bf16[16,8,1536]{2,1,0:T(8,128)(2,1)S(1)} all-to-all(bf16[16,8,1536]{2,1,0:T(8,128)(2,1)S(1)} %bitcast.13), channel_id=1, replica_groups=mesh['seg'=32,'trait'=16] {'trait'}, dimensions={0} | all-to-all | bytes 786432 | tf_op jit(solution)/shard_map/all_to_all | solution.py:169
  67.3 0.9 %unpack.1 = bf16[192,1024]{1,0:T(8,128)(2,1)} custom-call(bf16[128,1536]{1,0:T(8,128)(2,1)S(1)} %bitcast.10), custom_call_target="tpu_custom_call" | custom-call | bytes 393216 | tf_op jit(solution)/shard_map/unpack/pallas_call | solution.py:149
Async XLA Ops:
  0.0 1.0 %copy-start.1 = (bf16[16,12,1024]{2,0,1:T(8,128)(2,1)S(1)}, bf16[16,12,1024]{2,0,1:T(8,128)(2,1)}, u32[]{:S(2)}) copy-start(bf16[16,12,1024]{2,0,1:T(8,128)(2,1)} %param.3) | copy-start | bytes 1179652
  18.0 0.9 %copy-start.2 = (f32[192,192]{1,0:T(8,128)S(1)}, f32[192,192]{1,0:T(8,128)}, u32[]{:S(2)}) copy-start(f32[192,192]{1,0:T(8,128)} %p_ref.1) | copy-start | bytes 442372
  19.3 17.2 %collective-permute-start.1 = (bf16[192,1024]{1,0:T(8,128)(2,1)S(1)}, bf16[192,1024]{1,0:T(8,128)(2,1)S(1)}, u32[]{:S(2)}, u32[]{:S(2)}) collective-permute-start(bf16[192,1024]{1,0:T(8,128)(2,1)S(1)} %mix.1.x_ref), channel_id=1, source_target_pairs={{32,0},{48,16},{64,32},{80,48},{96,64},{112,80},{128,96},{144,112}... | collective-permute-start | bytes 1179656 | tf_op jit(solution)/shard_map/ppermute | solution.py:164
  23.5 17.6 %collective-permute-start = (bf16[192,1024]{1,0:T(8,128)(2,1)S(1)}, bf16[192,1024]{1,0:T(8,128)(2,1)S(1)}, u32[]{:S(2)}, u32[]{:S(2)}) collective-permute-start(bf16[192,1024]{1,0:T(8,128)(2,1)S(1)} %mix.1.x_ref), channel_id=1, source_target_pairs={{16,0},{32,16},{48,32},{64,48},{80,64},{96,80},{112,96},{128,112},... | collective-permute-start | bytes 1179656 | tf_op jit(solution)/shard_map/ppermute | solution.py:164
  26.7 2.2 %copy-start = (bf16[1024,2048]{1,0:T(8,128)(2,1)S(1)}, bf16[1024,2048]{1,0:T(8,128)(2,1)}, u32[]{:S(2)}) copy-start(bf16[1024,2048]{1,0:T(8,128)(2,1)} %band_ref.1) | copy-start | bytes 12582916
  31.1 18.3 %collective-permute-start.2 = (bf16[192,1024]{1,0:T(8,128)(2,1)S(1)}, bf16[192,1024]{1,0:T(8,128)(2,1)S(1)}, u32[]{:S(2)}, u32[]{:S(2)}) collective-permute-start(bf16[192,1024]{1,0:T(8,128)(2,1)S(1)} %get-tuple-element.11), channel_id=1, source_target_pairs={{0,16},{16,32},{32,48},{48,64},{64,80},{80,96},{96,112},{112,128},... | collective-permute-start | bytes 1179656 | tf_op jit(solution)/shard_map/ppermute | solution.py:164
  34.6 18.5 %collective-permute-start.3 = (bf16[192,1024]{1,0:T(8,128)(2,1)S(1)}, bf16[192,1024]{1,0:T(8,128)(2,1)S(1)}, u32[]{:S(2)}, u32[]{:S(2)}) collective-permute-start(bf16[192,1024]{1,0:T(8,128)(2,1)S(1)} %get-tuple-element.12), channel_id=1, source_target_pairs={{0,32},{16,48},{32,64},{48,80},{64,96},{80,112},{96,128},{112,144}... | collective-permute-start | bytes 1179656 | tf_op jit(solution)/shard_map/ppermute | solution.py:164

commit v2 on v1

--- a/solution.py
+++ b/solution.py
@@ -19,21 +19,28 @@
     return pltpu.CompilerParams(vmem_limit_bytes=mib * MIB)
 
 
-def pack_kernel(x_ref, o_ref, wide):
-    m = x_ref.shape[1]
+def pack_kernel(x_ref, o_ref, near, wide, sems):
+    rows, m = x_ref.shape
     blocks = m // LANES
-    for k in range(blocks):
-        wide[k] = x_ref[:, k * LANES : (k + 1) * LANES].astype(F32)
+    chunks = sems.shape[0]
+    copies = []
+    for q in range(chunks):
+        lanes = pl.ds(q * (m // chunks), m // chunks)
+        copies.append(pltpu.make_async_copy(x_ref.at[:, lanes], near.at[:, lanes], sems.at[q]))
+        copies[-1].start()
+    for q in range(chunks):
+        copies[q].wait()
+        for k in range(q * blocks // chunks, (q + 1) * blocks // chunks):
+            wide[k] = near[:, k * LANES : (k + 1) * LANES].astype(F32)
+            for c in range(0, 16, 2):
+                parts = [wide[k, pl.ds(d, 8, stride=16), :] for d in (c, c + 1)]
+                o_ref[8 * c : 8 * c + 16, k * LANES : (k + 1) * LANES] = jnp.concatenate(parts, 0).astype(BF16)
     for c in range(0, 16, 2):
-        rows = pl.ds(8 * c, 16)
-        for k in range(blocks):
-            parts = [wide[k, pl.ds(d, 8, stride=16), :] for d in (c, c + 1)]
-            o_ref[rows, k * LANES : (k + 1) * LANES] = jnp.concatenate(parts, 0).astype(BF16)
         for k in range(blocks // 2):
             parts = [
                 wide[k + h, pl.ds(128 + d, 4, stride=16), :] for d in (c, c + 1) for h in (0, blocks // 2)
             ]
-            o_ref[rows, m + k * LANES : m + (k + 1) * LANES] = jnp.concatenate(parts, 0).astype(BF16)
+            o_ref[8 * c : 8 * c + 16, m + k * LANES : m + (k + 1) * LANES] = jnp.concatenate(parts, 0).astype(BF16)
 
 
 def unpack_kernel(x_ref, o_ref, wide):
@@ -51,9 +58,21 @@
             o_ref[128 + 16 * j : 144 + 16 * j, lanes] = tail.astype(BF16)
 
 
-def mix_kernel(x_ref, p_ref, o_ref):
+def mix_kernel(x_ref, p_ref, dense_ref, o_ref, near_ref, far_ref, held, sems):
     m = o_ref.shape[1]
     half = m // 2
+    width = dense_ref.shape[1] - m
+    chunks = sems.shape[0]
+    depth = width // chunks
+    copies = []
+    for k in range(chunks):
+        low = max(0, m + k * depth - width)
+        lanes = pl.ds(m + k * depth, depth)
+        copy = pltpu.make_async_copy(
+            dense_ref.at[low:, lanes], held.at[low:, k * depth : (k + 1) * depth], sems.at[k]
+        )
+        copy.start()
+        copies.append((copy, low))
     blank = jnp.zeros((4, p_ref.shape[1]), F32)
     heads, lows, highs = [], [], []
     for t in range(16):
@@ -70,6 +89,17 @@
         total = jnp.dot(upper, values, preferred_element_type=F32)
         total += jnp.dot(lower, values, preferred_element_type=F32)
         o_ref[:, first : first + half] = total.astype(BF16)
+    for k, (copy, _) in enumerate(copies):
+        copy.wait()
+        for col in range(k * depth, (k + 1) * depth, 256):
+            low = max(0, m + col - width)
+            part = jnp.dot(
+                o_ref[:, low:], held[low:, col : col + 256], preferred_element_type=F32
+            ).astype(BF16)
+            if col < m:
+                near_ref[:, col : col + 256] = part
+            else:
+                far_ref[:, col - m : col - m + 256] = part
 
 
 def skew_rows(band_ref, dense_ref, first):
@@ -89,7 +119,7 @@
         before = now
 
 
-def lower_kernel(x_ref, band_ref, dense_ref, own_ref, near_ref, far_ref):
+def skew_kernel(band_ref, dense_ref):
     m, width = band_ref.shape
     depth = 256
     for first in range(0, m, LANES):
@@ -99,40 +129,37 @@
             dense_ref[pl.ds(first, LANES), pl.ds(first - LANES, LANES)] = zero
         else:
             dense_ref[pl.ds(first, LANES), pl.ds(first + width + LANES, LANES)] = zero
-    for col in range(0, m + width, depth):
-        low = max(0, col - width)
-        high = min(m, col + depth)
-        part = jnp.dot(
-            x_ref[:, low:high], dense_ref[low:high, col : col + depth], preferred_element_type=F32
-        )
-        if col < m:
-            own_ref[:, col : col + depth] = part + x_ref[:, col : col + depth].astype(F32)
-        elif col < 2 * m:
-            near_ref[:, col - m : col - m + depth] = part.astype(BF16)
-        else:
-            far_ref[:, col - 2 * m : col - 2 * m + depth] = part.astype(BF16)
 
 
 def contract(values, dense):
     return lax.dot_general(values, dense, (((1,), (1,)), ((), ())), preferred_element_type=F32)
 
 
-def upper_kernel(x_ref, near_ref, far_ref, dense_ref, own_ref, o_ref):
-    rows, m = x_ref.shape
+def own_kernel(x_ref, dense_ref, o_ref):
+    m = x_ref.shape[1]
     depth = 256
     for i in range(0, m, depth):
-        d = dense_ref.at[i : i + depth, :]
-        total = own_ref[:, i : i + depth]
-        total += contract(x_ref[:, i:], d[:, i:m])
-        total += contract(near_ref[...], d[:, m : 2 * m])
-        total += contract(far_ref[:, : i + depth], d[:, 2 * m : 2 * m + i + depth])
-        o_ref[:, i : i + depth] = total
-
-
-def finish_kernel(total_ref, near_ref, far_ref, o_ref, wide):
-    m = total_ref.shape[1]
+        high = i + depth
+        total = x_ref[:, i:high].astype(F32)
+        total += jnp.dot(x_ref[:, :high], dense_ref[:high, i:high], preferred_element_type=F32)
+        total += contract(x_ref[:, i:], dense_ref[i:high, i:m])
+        o_ref[:, i:high] = total
+
+
+def near_kernel(x_ref, low_ref, dense_ref, total_ref, o_ref):
+    m = x_ref.shape[1]
+    part = contract(x_ref[...], dense_ref[:, m : 2 * m])
+    o_ref[...] = total_ref[...] + low_ref[...].astype(F32) + part
+
+
+def far_kernel(x_ref, low_ref, dense_ref, total_ref, o_ref, wide):
+    m = x_ref.shape[1]
     half = m // 2
-    wide[...] = total_ref[...] + near_ref[...].astype(F32) + far_ref[...].astype(F32)
+    depth = 256
+    for i in range(0, m, depth):
+        high = i + depth
+        part = contract(x_ref[:, :high], dense_ref[i:high, 2 * m : 2 * m + high])
+        wide[:, i:high] = total_ref[:, i:high] + low_ref[:, i:high].astype(F32) + part
     for t in range(0, 16, 2):
         parts = []
         for u in (t, t + 1):
@@ -143,13 +170,16 @@
         o_ref[8 * t : 8 * t + 16, :] = jnp.concatenate(parts, 0).astype(BF16)
 
 
-def call(kernel, name, outs, mib, *args, scratch=(), flops=0):
+def call(kernel, name, outs, mib, *args, scratch=(), flops=0, far_off=()):
     several = isinstance(outs, tuple)
     size = sum(a.size * a.dtype.itemsize for a in args)
+    in_specs = vmem_specs(len(args))
+    for k in far_off:
+        in_specs[k] = pl.BlockSpec(memory_space=pltpu.HBM)
     return pl.pallas_call(
         kernel,
         out_shape=outs,
-        in_specs=vmem_specs(len(args)),
+        in_specs=in_specs,
         out_specs=tuple(vmem_specs(len(outs))) if several else vmem_specs(1)[0],
         scratch_shapes=list(scratch),
         compiler_params=params(mib),
@@ -179,35 +209,31 @@
 
     flat = effects.transpose(1, 0, 2).reshape(rows, m)
     packed = call(
-        pack_kernel, "pack", struct(packed_shape, BF16), 8, flat,
-        scratch=[pltpu.VMEM((m // LANES, rows, LANES), F32)],
-    )
-    mixed = call(mix_kernel, "mix", struct((rows, m), BF16), 8, exchange(packed), precision)
+        pack_kernel, "pack", struct(packed_shape, BF16), 63, flat,
+        far_off=(0,),
+        scratch=[
+            pltpu.VMEM((rows, m), BF16),
+            pltpu.VMEM((m // LANES, rows, LANES), F32),
+            pltpu.SemaphoreType.DMA((4,)),
+        ],
+    )
+    dense = call(skew_kernel, "skew", struct((m, m + width), BF16), 16, band, flops=m * width)
+    thin = struct((rows, m), BF16)
+    mixed, low_near, low_far = call(
+        mix_kernel, "mix", (thin, thin, thin), 52, exchange(packed), precision, dense,
+        flops=2 * rows * m * width, far_off=(2,),
+        scratch=[pltpu.VMEM((m, width), BF16), pltpu.SemaphoreType.DMA((4,))],
+    )
+    low_near = passed_along(low_near, 1)
+    near = passed_along(mixed, -1)
+    low_far = passed_along(low_far, 2)
     far = passed_along(mixed, -2)
-    near = passed_along(mixed, -1)
-    dense, own, low_near, low_far = call(
-        lower_kernel,
-        "lower",
-        (
-            struct((m, m + width), BF16),
-            struct((rows, m), F32),
-            struct((rows, m), BF16),
-            struct((rows, m), BF16),
-        ),
-        16,
-        mixed,
-        band,
-        flops=2 * rows * m * width,
-    )
-    low_far = passed_along(low_far, 2)
-    low_near = passed_along(low_near, 1)
-    total = call(
-        upper_kernel, "upper", struct((rows, m), F32), 16, mixed, near, far, dense, own,
-        flops=2 * rows * m * width,
-    )
+    wide = struct((rows, m), F32)
+    total = call(own_kernel, "own", wide, 16, mixed, dense, flops=4 * rows * m * m)
+    total = call(near_kernel, "near", wide, 16, near, low_near, dense, total, flops=2 * rows * m * m)
     packed = call(
-        finish_kernel, "finish", struct(packed_shape, BF16), 8, total, low_near, low_far,
-        scratch=[pltpu.VMEM((rows, m), F32)],
+        far_kernel, "far", struct(packed_shape, BF16), 16, far, low_far, dense, total,
+        flops=rows * m * m, scratch=[pltpu.VMEM((rows, m), F32)],
     )
     flat = call(
         unpack_kernel, "unpack", struct((rows, m), BF16), 8, exchange(packed),

time: 68.6 us -> 66.5 us (0.969)
  the two profiles are of different devices: /device:TPU:392 before, /device:TPU:96 now
where the time goes in v2:
time: 66.5 us; the launch traced here: 66.1 us
  starting transfers between devices  22.1 us (33%)
  waiting for transfers between devices  15.6 us (23%)
  blocking collectives  14 us (21%)
  Pallas kernels  9.54 us (14%)
  local copies, waits for them, and re-layouts  4.84 us (7%)
    ppermute x4, starting transfers between devices, passed_along(): return lax.ppermute(shard, 'seg', pairs)  15 us
    all_to_all x1, blocking collectives, exchange(): lax.all_to_all(packed.reshape(16, rows // 16, lanes), 'trait', 0, 0, tile...  14 us
    ppermute x4, waiting for transfers between devices, passed_along(): return lax.ppermute(shard, 'seg', pairs)  11.1 us
    pallas_call x7, Pallas kernels, call(): pl.pallas_call(kernel, out_shape=outs, in_specs=in_specs, out_specs=tuple...  9.54 us
    all_to_all x1, starting transfers between devices, exchange(): lax.all_to_all(packed.reshape(16, rows // 16, lanes), 'trait', 0, 0, tile...  7.05 us
    unnamed x8, local copies, waits for them, and re-layouts  4.84 us
    all_to_all x1, waiting for transfers between devices, exchange(): lax.all_to_all(packed.reshape(16, rows // 16, lanes), 'trait', 0, 0, tile...  4.44 us
  transfers between devices with their start and end apart: 5, of which 4 were waited for; matrix products, arithmetic and copies ran while one was open for 0% of the time, Pallas kernels for 5%

profile of v2, /device:TPU:96, one launch (start us, length us, event | category | flops | bytes accessed | tf_op | source)
XLA Modules:
  0.0 66.1 jit_solution(9456678480666250049)
XLA Ops:
  0.0 2.0 %pack.1 = bf16[128,1536]{1,0:T(8,128)(2,1)} custom-call(bf16[192,1024]{1,0:T(8,128)(2,1)} %bitcast.14), custom_call_target="tpu_custom_call" | custom-call | bytes 393216 | tf_op jit(solution)/shard_map/pack/pallas_call | solution.py:179
  2.1 7.0 %all-to-all-start = ((bf16[16,8,1536]{2,1,0:T(8,128)(2,1)}), bf16[16,8,1536]{2,1,0:T(8,128)(2,1)S(1)}, u32[]{:S(2)}, u32[]{:S(2)}) async-start(bf16[16,8,1536]{2,1,0:T(8,128)(2,1)} %bitcast.13), calls=%async_computation | async-start | bytes 786432 | tf_op jit(solution)/shard_map/all_to_all | solution.py:199
  9.1 0.0 copy-start.2
  9.1 2.2 %copy-done.2 = bf16[1024,2048]{1,0:T(8,128)(2,1)S(1)} copy-done((bf16[1024,2048]{1,0:T(8,128)(2,1)S(1)}, bf16[1024,2048]{1,0:T(8,128)(2,1)}, u32[]{:S(2)}) %copy-start.2) | copy-done | bytes 4194328
  11.3 1.4 %skew.1.dense_ref = bf16[1024,3072]{1,0:T(8,128)(2,1)S(1)} custom-call(bf16[1024,2048]{1,0:T(8,128)(2,1)S(1)} %copy-done.2), custom_call_target="tpu_custom_call" | custom-call | flops 2097152 | bytes 4194304 | tf_op jit(solution)/shard_map/skew/pallas_call | solution.py:179
  12.7 0.0 copy-start
  12.7 2.7 %copy-done = bf16[1024,3072]{1,0:T(8,128)(2,1)} copy-done((bf16[1024,3072]{1,0:T(8,128)(2,1)}, bf16[1024,3072]{1,0:T(8,128)(2,1)S(1)}, u32[]{:S(2)}) %copy-start) | copy-done | bytes 6291480
  15.4 4.4 %all-to-all-done = bf16[16,8,1536]{2,1,0:T(8,128)(2,1)S(1)} async-done(((bf16[16,8,1536]{2,1,0:T(8,128)(2,1)}), bf16[16,8,1536]{2,1,0:T(8,128)(2,1)S(1)}, u32[]{:S(2)}, u32[]{:S(2)}) %all-to-all-start) | async-done | bytes 393248 | tf_op jit(solution)/shard_map/all_to_all | solution.py:199
  19.8 0.0 copy-done.3
  19.8 2.9 %mix.1 = (bf16[192,1024]{1,0:T(8,128)(2,1)S(1)}, bf16[192,1024]{1,0:T(8,128)(2,1)S(1)}, bf16[192,1024]{1,0:T(8,128)(2,1)S(1)}) custom-call(bf16[128,1536]{1,0:T(8,128)(2,1)S(1)} %bitcast.12, f32[192,192]{1,0:T(8,128)S(1)} %copy-done.3, bf16[1024,3072]{1,0:T(8,128)(2,1)} %copy-done), custom_call_target="tpu_custom_call" | custom-call | flops 805306368 | bytes 6832128 | tf_op jit(solution)/shard_map/mix/pallas_call | solution.py:179
  22.7 2.7 %collective-permute-start.3 = (bf16[192,1024]{1,0:T(8,128)(2,1)S(1)}, bf16[192,1024]{1,0:T(8,128)(2,1)S(1)}, u32[]{:S(2)}, u32[]{:S(2)}) collective-permute-start(bf16[192,1024]{1,0:T(8,128)(2,1)S(1)} %get-tuple-element.10), channel_id=1, source_target_pairs={{0,16},{16,32},{32,48},{48,64},{64,80},{80,96},{96,112},{112,128},... | collective-permute-start | bytes 1179656 | tf_op jit(solution)/shard_map/ppermute | solution.py:194
  25.4 4.1 %collective-permute-start.2 = (bf16[192,1024]{1,0:T(8,128)(2,1)S(1)}, bf16[192,1024]{1,0:T(8,128)(2,1)S(1)}, u32[]{:S(2)}, u32[]{:S(2)}) collective-permute-start(bf16[192,1024]{1,0:T(8,128)(2,1)S(1)} %get-tuple-element.8.x_ref), channel_id=1, source_target_pairs={{16,0},{32,16},{48,32},{64,48},{80,64},{96,80},{112,96},{128,112},... | collective-permute-start | bytes 1179656 | tf_op jit(solution)/shard_map/ppermute | solution.py:194
  29.6 6.3 %collective-permute-start.1 = (bf16[192,1024]{1,0:T(8,128)(2,1)S(1)}, bf16[192,1024]{1,0:T(8,128)(2,1)S(1)}, u32[]{:S(2)}, u32[]{:S(2)}) collective-permute-start(bf16[192,1024]{1,0:T(8,128)(2,1)S(1)} %get-tuple-element.9), channel_id=1, source_target_pairs={{0,32},{16,48},{32,64},{48,80},{64,96},{80,112},{96,128},{112,144}... | collective-permute-start | bytes 1179656 | tf_op jit(solution)/shard_map/ppermute | solution.py:194
  35.9 1.9 %collective-permute-start = (bf16[192,1024]{1,0:T(8,128)(2,1)S(1)}, bf16[192,1024]{1,0:T(8,128)(2,1)S(1)}, u32[]{:S(2)}, u32[]{:S(2)}) collective-permute-start(bf16[192,1024]{1,0:T(8,128)(2,1)S(1)} %get-tuple-element.8.x_ref), channel_id=1, source_target_pairs={{32,0},{48,16},{64,32},{80,48},{96,64},{112,80},{128,96},{144,112}... | collective-permute-start | bytes 1179656 | tf_op jit(solution)/shard_map/ppermute | solution.py:194
  37.8 0.0 copy-done.1
  37.8 0.8 %own.1.total_ref = f32[192,1024]{1,0:T(8,128)S(1)} custom-call(bf16[192,1024]{1,0:T(8,128)(2,1)S(1)} %get-tuple-element.8.x_ref, bf16[1024,3072]{1,0:T(8,128)(2,1)S(1)} %copy-done.1), custom_call_target="tpu_custom_call" | custom-call | flops 805306368 | bytes 6684672 | tf_op jit(solution)/shard_map/own/pallas_call | solution.py:179
  38.6 2.0 %collective-permute-done.3.low_ref = bf16[192,1024]{1,0:T(8,128)(2,1)S(1)} collective-permute-done((bf16[192,1024]{1,0:T(8,128)(2,1)S(1)}, bf16[192,1024]{1,0:T(8,128)(2,1)S(1)}, u32[]{:S(2)}, u32[]{:S(2)}) %collective-permute-start.3) | collective-permute-done | bytes 393248 | tf_op jit(solution)/shard_map/ppermute | solution.py:194
  40.6 4.0 %collective-permute-done.2.x_ref = bf16[192,1024]{1,0:T(8,128)(2,1)S(1)} collective-permute-done((bf16[192,1024]{1,0:T(8,128)(2,1)S(1)}, bf16[192,1024]{1,0:T(8,128)(2,1)S(1)}, u32[]{:S(2)}, u32[]{:S(2)}) %collective-permute-start.2) | collective-permute-done | bytes 393248 | tf_op jit(solution)/shard_map/ppermute | solution.py:194
  44.5 0.8 %near.1.total_ref = f32[192,1024]{1,0:T(8,128)S(1)} custom-call(bf16[192,1024]{1,0:T(8,128)(2,1)S(1)} %collective-permute-done.2.x_ref, bf16[192,1024]{1,0:T(8,128)(2,1)S(1)} %collective-permute-done.3.low_ref, bf16[1024,3072]{1,0:T(8,128)(2,1)S(1)} %copy-done.1, f32[192,1024]{1,0:T(8,128)S(1)} %own.1.total_ref), custom_call_target="tpu_custom_call" | custom-call | flops 402653184 | bytes 7864320 | tf_op jit(solution)/shard_map/near/pallas_call | solution.py:179
  45.4 0.0 collective-permute-done.1.low_ref
  45.4 5.2 %collective-permute-done.x_ref = bf16[192,1024]{1,0:T(8,128)(2,1)S(1)} collective-permute-done((bf16[192,1024]{1,0:T(8,128)(2,1)S(1)}, bf16[192,1024]{1,0:T(8,128)(2,1)S(1)}, u32[]{:S(2)}, u32[]{:S(2)}) %collective-permute-start) | collective-permute-done | bytes 393248 | tf_op jit(solution)/shard_map/ppermute | solution.py:194
  50.6 0.6 far.1
  51.2 14.0 %all_to_all.10 = bf16[16,8,1536]{2,1,0:T(8,128)(2,1)S(1)} all-to-all(bf16[16,8,1536]{2,1,0:T(8,128)(2,1)S(1)} %bitcast.10), channel_id=1, replica_groups=mesh['seg'=32,'trait'=16] {'trait'}, dimensions={0} | all-to-all | bytes 786432 | tf_op jit(solution)/shard_map/all_to_all | solution.py:199
  65.2 0.9 %unpack.1 = bf16[192,1024]{1,0:T(8,128)(2,1)} custom-call(bf16[128,1536]{1,0:T(8,128)(2,1)S(1)} %bitcast.11), custom_call_target="tpu_custom_call" | custom-call | bytes 393216 | tf_op jit(solution)/shard_map/unpack/pallas_call | solution.py:179
  (2 shorter events, 0.0 us)
Async XLA Ops:
  0.0 19.8 %copy-start.3 = (f32[192,192]{1,0:T(8,128)S(1)}, f32[192,192]{1,0:T(8,128)}, u32[]{:S(2)}) copy-start(f32[192,192]{1,0:T(8,128)} %p_ref.1) | copy-start | bytes 442372
  2.1 17.8 %all-to-all-start = ((bf16[16,8,1536]{2,1,0:T(8,128)(2,1)}), bf16[16,8,1536]{2,1,0:T(8,128)(2,1)S(1)}, u32[]{:S(2)}, u32[]{:S(2)}) async-start(bf16[16,8,1536]{2,1,0:T(8,128)(2,1)} %bitcast.13), calls=%async_computation | async-start | bytes 786432 | tf_op jit(solution)/shard_map/all_to_all | solution.py:199
  9.1 2.2 %copy-start.2 = (bf16[1024,2048]{1,0:T(8,128)(2,1)S(1)}, bf16[1024,2048]{1,0:T(8,128)(2,1)}, u32[]{:S(2)}) copy-start(bf16[1024,2048]{1,0:T(8,128)(2,1)} %band_ref.1) | copy-start | bytes 12582916
  12.7 2.7 %copy-start = (bf16[1024,3072]{1,0:T(8,128)(2,1)}, bf16[1024,3072]{1,0:T(8,128)(2,1)S(1)}, u32[]{:S(2)}) copy-start(bf16[1024,3072]{1,0:T(8,128)(2,1)S(1)} %skew.1.dense_ref) | copy-start | bytes 18874372
  19.8 18.0 %copy-start.1 = (bf16[1024,3072]{1,0:T(8,128)(2,1)S(1)}, bf16[1024,3072]{1,0:T(8,128)(2,1)}, u32[]{:S(2)}) copy-start(bf16[1024,3072]{1,0:T(8,128)(2,1)} %copy-done) | copy-start | bytes 18874372
  22.7 17.9 %collective-permute-start.3 = (bf16[192,1024]{1,0:T(8,128)(2,1)S(1)}, bf16[192,1024]{1,0:T(8,128)(2,1)S(1)}, u32[]{:S(2)}, u32[]{:S(2)}) collective-permute-start(bf16[192,1024]{1,0:T(8,128)(2,1)S(1)} %get-tuple-element.10), channel_id=1, source_target_pairs={{0,16},{16,32},{32,48},{48,64},{64,80},{80,96},{96,112},{112,128},... | collective-permute-start | bytes 1179656 | tf_op jit(solution)/shard_map/ppermute | solution.py:194
  25.4 19.1 %collective-permute-start.2 = (bf16[192,1024]{1,0:T(8,128)(2,1)S(1)}, bf16[192,1024]{1,0:T(8,128)(2,1)S(1)}, u32[]{:S(2)}, u32[]{:S(2)}) collective-permute-start(bf16[192,1024]{1,0:T(8,128)(2,1)S(1)} %get-tuple-element.8.x_ref), channel_id=1, source_target_pairs={{16,0},{32,16},{48,32},{64,48},{80,64},{96,80},{112,96},{128,112},... | collective-permute-start | bytes 1179656 | tf_op jit(solution)/shard_map/ppermute | solution.py:194
  29.6 15.8 %collective-permute-start.1 = (bf16[192,1024]{1,0:T(8,128)(2,1)S(1)}, bf16[192,1024]{1,0:T(8,128)(2,1)S(1)}, u32[]{:S(2)}, u32[]{:S(2)}) collective-permute-start(bf16[192,1024]{1,0:T(8,128)(2,1)S(1)} %get-tuple-element.9), channel_id=1, source_target_pairs={{0,32},{16,48},{32,64},{48,80},{64,96},{80,112},{96,128},{112,144}... | collective-permute-start | bytes 1179656 | tf_op jit(solution)/shard_map/ppermute | solution.py:194
  35.9 14.7 %collective-permute-start = (bf16[192,1024]{1,0:T(8,128)(2,1)S(1)}, bf16[192,1024]{1,0:T(8,128)(2,1)S(1)}, u32[]{:S(2)}, u32[]{:S(2)}) collective-permute-start(bf16[192,1024]{1,0:T(8,128)(2,1)S(1)} %get-tuple-element.8.x_ref), channel_id=1, source_target_pairs={{32,0},{48,16},{64,32},{80,48},{96,64},{112,80},{128,96},{144,112}... | collective-permute-start | bytes 1179656 | tf_op jit(solution)/shard_map/ppermute | solution.py:194

commit v3 on v2

v3 whole, which is shorter than its diff:
```python
import jax
import jax.numpy as jnp
from jax import lax
from jax.experimental import pallas as pl
from jax.experimental.pallas import tpu as pltpu
from jax.sharding import PartitionSpec as P

F32 = jnp.float32
BF16 = jnp.bfloat16
LANES = 128
MIB = 1 << 20


def vmem_specs(count):
    return [pl.BlockSpec(memory_space=pltpu.VMEM)] * count


def params(mib):
    return pltpu.CompilerParams(vmem_limit_bytes=mib * MIB)


def swapped(place):
    return 8 * (place % 2) + 2 * (place // 2 % 4) + place // 8


def chain_places():
    odd = lax.rem(lax.axis_index("seg"), 2) == 1
    return [jnp.where(odd, swapped(p), p) for p in range(16)]


def pack_kernel(x_ref, o_ref, near, wide, packed, in_sems, out_sems):
    rows, m = x_ref.shape
    blocks = m // LANES
    chunks = in_sems.shape[0]
    part = m // chunks
    chains = chain_places()
    copies = []
    for q in range(chunks):
        lanes = pl.ds(q * part, part)
        copies.append(pltpu.make_async_copy(x_ref.at[:, lanes], near.at[:, lanes], in_sems.at[q]))
        copies[-1].start()
    out = []

    def send(first, size):
        lanes = pl.ds(first, size)
        out.append(pltpu.make_async_copy(packed.at[:, lanes], o_ref.at[:, lanes], out_sems.at[len(out)]))
        out[-1].start()

    for q in range(chunks):
        copies[q].wait()
        for k in range(q * blocks // chunks, (q + 1) * blocks // chunks):
            wide[k] = near[:, k * LANES : (k + 1) * LANES].astype(F32)
            for p in range(0, 16, 2):
                parts = [wide[k, pl.ds(d, 8, stride=16), :] for d in chains[p : p + 2]]
                packed[8 * p : 8 * p + 16, k * LANES : (k + 1) * LANES] = jnp.concatenate(parts, 0).astype(BF16)
        send(q * part, part)
    for p in range(0, 16, 2):
        for k in range(blocks // 2):
            parts = [
                wide[k + h, pl.ds(128 + d, 4, stride=16), :]
                for d in chains[p : p + 2]
                for h in (0, blocks // 2)
            ]
            packed[8 * p : 8 * p + 16, m + k * LANES : m + (k + 1) * LANES] = jnp.concatenate(parts, 0).astype(BF16)
    send(m, m // 2)
    for copy in out:
        copy.wait()


def unpack_kernel(x_ref, o_ref, wide):
    m = o_ref.shape[1]
    blocks = m // LANES
    chains = chain_places()
    for k in range(wide.shape[0]):
        for p in range(0, 16, 2):
            pair = x_ref[8 * p : 8 * p + 16, k * LANES : (k + 1) * LANES].astype(F32)
            for h in range(2):
                wide[k, pl.ds(pl.multiple_of(8 * chains[p + h], 8), 8), :] = pair[8 * h : 8 * h + 8]
    for k in range(blocks):
        lanes = pl.ds(k * LANES, LANES)
        for j in range(8):
            o_ref[16 * j : 16 * j + 16, lanes] = wide[k, pl.ds(j, 16, stride=8), :].astype(BF16)
        half, place = divmod(k, blocks // 2)
        for j in range(4):
            tail = wide[blocks + place, pl.ds(j + 4 * half, 16, stride=8), :]
            o_ref[128 + 16 * j : 144 + 16 * j, lanes] = tail.astype(BF16)


def mix_kernel(x_ref, p_ref, beyond_ref, o_ref, near_ref, far_ref, held, sems):
    m = o_ref.shape[1]
    half = m // 2
    width = beyond_ref.shape[1]
    chunks = sems.shape[0]
    depth = width // chunks
    copies = []
    for k in range(chunks):
        low = max(0, m + k * depth - width)
        lanes = pl.ds(k * depth, depth)
        copies.append(pltpu.make_async_copy(beyond_ref.at[low:, lanes], held.at[low:, lanes], sems.at[k]))
        copies[-1].start()
    blank = jnp.zeros((4, p_ref.shape[1]), F32)
    heads, lows, highs = [], [], []
    for t in range(16):
        heads.append(p_ref[12 * t : 12 * t + 8, :])
        tail = p_ref[12 * t + 8 : 12 * t + 12, :]
        lows += [tail, blank]
        highs += [blank, tail]
    head = jnp.concatenate(heads, 0)
    for first, tails in ((0, lows), (half, highs)):
        weights = jnp.concatenate([head, jnp.concatenate(tails, 0)], 0).T
        upper = weights.astype(BF16)
        lower = (weights - upper.astype(F32)).astype(BF16)
        values = jnp.concatenate([x_ref[:, first : first + half], x_ref[:, m:]], 0)
        total = jnp.dot(upper, values, preferred_element_type=F32)
        total += jnp.dot(lower, values, preferred_element_type=F32)
        o_ref[:, first : first + half] = total.astype(BF16)
    for k, copy in enumerate(copies):
        copy.wait()
        for col in range(k * depth, (k + 1) * depth, 256):
            low = max(0, m + col - width)
            part = jnp.dot(
                o_ref[:, low:], held[low:, col : col + 256], preferred_element_type=F32
            ).astype(BF16)
            if col < m:
                near_ref[:, col : col + 256] = part
            else:
                far_ref[:, col - m : col - m + 256] = part


def skew_rows(band_ref, own_ref, beyond_ref, first):
    m, width = band_ref.shape
    rows = pl.ds(first, LANES)

    def put(col, tile):
        if col < m:
            own_ref[rows, pl.ds(col, LANES)] = tile
        elif col < m + width:
            beyond_ref[rows, pl.ds(col - m, LANES)] = tile

    a = lax.broadcasted_iota(jnp.int32, (LANES, LANES), 0)
    b = lax.broadcasted_iota(jnp.int32, (LANES, LANES), 1)
    ahead = b > a
    zero = jnp.zeros((LANES, LANES), F32)
    before = zero
    for d in range(width // LANES + 1):
        if d < width // LANES:
            tile = band_ref[rows, d * LANES : (d + 1) * LANES].astype(F32)
            now = pltpu.roll(tile, 1, 1, stride=1, stride_axis=0)
        else:
            now = zero
        put(first + d * LANES, jnp.where(ahead, now, before).astype(BF16))
        before = now
    if first % 256:
        put(first - LANES, zero.astype(BF16))
    else:
        put(first + width + LANES, zero.astype(BF16))


def skew_kernel(band_ref, own_ref, beyond_ref):
    for first in range(0, band_ref.shape[0], LANES):
        skew_rows(band_ref, own_ref, beyond_ref, first)


def contract(values, dense):
    return lax.dot_general(values, dense, (((1,), (1,)), ((), ())), preferred_element_type=F32)


def own_kernel(x_ref, dense_ref, o_ref):
    m = x_ref.shape[1]
    depth = 256
    for i in range(0, m, depth):
        high = i + depth
        total = x_ref[:, i:high].astype(F32)
        total += jnp.dot(x_ref[:, :high], dense_ref[:high, i:high], preferred_element_type=F32)
        total += contract(x_ref[:, i:], dense_ref[i:high, i:m])
        o_ref[:, i:high] = total


def near_kernel(x_ref, low_ref, dense_ref, total_ref, o_ref):
    m = x_ref.shape[1]
    part = contract(x_ref[...], dense_ref[:, :m])
    o_ref[...] = total_ref[...] + low_ref[...].astype(F32) + part


def far_kernel(x_ref, low_ref, dense_ref, total_ref, o_ref, wide):
    m = x_ref.shape[1]
    half = m // 2
    depth = 256
    for i in range(0, m, depth):
        high = i + depth
        part = contract(x_ref[:, :high], dense_ref[i:high, m : m + high])
        wide[:, i:high] = total_ref[:, i:high] + low_ref[:, i:high].astype(F32) + part
    for t in range(0, 16, 2):
        parts = []
        for u in (t, t + 1):
            head = wide[12 * u : 12 * u + 8, :]
            left = wide[12 * u + 8 : 12 * u + 12, :half]
            right = wide[12 * u + 8 : 12 * u + 12, half:]
            parts.append(jnp.concatenate([head, jnp.concatenate([left, right], 0)], 1))
        o_ref[8 * t : 8 * t + 16, :] = jnp.concatenate(parts, 0).astype(BF16)


def call(kernel, name, outs, mib, *args, scratch=(), flops=0, far_off=(), far_out=False):
    several = isinstance(outs, tuple)
    size = sum(a.size * a.dtype.itemsize for a in args)
    in_specs = vmem_specs(len(args))
    for k in far_off:
        in_specs[k] = pl.BlockSpec(memory_space=pltpu.HBM)
    out_spec = pl.BlockSpec(memory_space=pltpu.HBM if far_out else pltpu.VMEM)
    return pl.pallas_call(
        kernel,
        out_shape=outs,
        in_specs=in_specs,
        out_specs=tuple(vmem_specs(len(outs))) if several else out_spec,
        scratch_shapes=list(scratch),
        compiler_params=params(mib),
        cost_estimate=pl.CostEstimate(flops=flops, bytes_accessed=size, transcendentals=0),
        name=name,
    )(*args)


def passed_along(shard, by):
    length, places = lax.axis_size("seg"), lax.axis_size("trait")
    pairs = []
    for s in range(length):
        for p in range(places):
            if 0 <= s + by < length:
                pairs.append((s * places + p, (s + by) * places + (swapped(p) if by % 2 else p)))
    return lax.ppermute(shard, ("seg", "trait"), pairs)


def exchange(packed):
    rows, lanes = packed.shape
    moved = lax.all_to_all(packed.reshape(16, rows // 16, lanes), "trait", 0, 0, tiled=True)
    return moved.reshape(rows, lanes)


def local(effects, precision, band):
    chains, traits, m = effects.shape
    width = band.shape[1]
    rows = chains * traits
    packed_shape = (8 * chains, m + m // 2)
    struct = jax.ShapeDtypeStruct

    flat = effects.transpose(1, 0, 2).reshape(rows, m)
    packed = call(
        pack_kernel, "pack", struct(packed_shape, BF16), 63, flat,
        far_off=(0,), far_out=True,
        scratch=[
            pltpu.VMEM((rows, m), BF16),
            pltpu.VMEM((m // LANES, rows, LANES), F32),
            pltpu.VMEM(packed_shape, BF16),
            pltpu.SemaphoreType.DMA((4,)),
            pltpu.SemaphoreType.DMA((5,)),
        ],
    )
    within, beyond = call(
        skew_kernel, "skew", (struct((m, m), BF16), struct((m, width), BF16)), 16, band, flops=m * width
    )
    thin = struct((rows, m), BF16)
    mixed, low_near, low_far, beyond = call(
        mix_kernel, "mix", (thin, thin, thin, struct((m, width), BF16)), 48,
        exchange(packed), precision, beyond,
        flops=2 * rows * m * width, far_off=(2,),
        scratch=[pltpu.SemaphoreType.DMA((4,))],
    )
    low_near = passed_along(low_near, 1)
    near = passed_along(mixed, -1)
    low_far = passed_along(low_far, 2)
    far = passed_along(mixed, -2)
    wide = struct((rows, m), F32)
    total = call(own_kernel, "own", wide, 16, mixed, within, flops=4 * rows * m * m)
    total = call(near_kernel, "near", wide, 16, near, low_near, beyond, total, flops=2 * rows * m * m)
    packed = call(
        far_kernel, "far", struct(packed_shape, BF16), 16, far, low_far, beyond, total,
        flops=rows * m * m, scratch=[pltpu.VMEM((rows, m), F32)],
    )
    flat = call(
        unpack_kernel, "unpack", struct((rows, m), BF16), 8, exchange(packed),
        scratch=[pltpu.VMEM((packed_shape[1] // LANES, packed_shape[0], LANES), F32)],
    )
    return flat.reshape(traits, chains, m).transpose(1, 0, 2)


def solution(mesh):
    in_specs = (P(None, "trait", "seg"), P(), P("seg", None))
    out_specs = P(None, "trait", "seg")
    return jax.shard_map(local, mesh=mesh, in_specs=in_specs, out_specs=out_specs, check_vma=False)
```

time: 66.5 us -> 67.2 us (1.011)
  waiting for transfers between devices: 15.6 us -> 17.7 us
  local copies, waits for them, and re-layouts: 4.84 us -> 4.13 us
  blocking collectives: 14 us -> 13.3 us
    ppermute x4, waiting for transfers between devices: 11.1 us -> 12.6 us  [passed_along(): return lax.ppermute(shard, ('seg', 'trait'), pairs)]
    unnamed x8 -> x6, local copies, waits for them, and re-layouts: 4.84 us -> 4.13 us
    all_to_all x1, waiting for transfers between devices: 4.44 us -> 5.15 us  [exchange(): lax.all_to_all(packed.reshape(16, rows // 16, lanes), 'trait', 0, 0, tile...]
where the time goes in v3:
time: 67.2 us; the launch traced here: 66.8 us
  starting transfers between devices  22 us (33%)
  waiting for transfers between devices  17.7 us (26%)
  blocking collectives  13.3 us (20%)
  Pallas kernels  9.51 us (14%)
  local copies, waits for them, and re-layouts  4.13 us (6%)
    ppermute x4, starting transfers between devices, passed_along(): return lax.ppermute(shard, ('seg', 'trait'), pairs)  14.9 us
    all_to_all x1, blocking collectives, exchange(): lax.all_to_all(packed.reshape(16, rows // 16, lanes), 'trait', 0, 0, tile...  13.3 us
    ppermute x4, waiting for transfers between devices, passed_along(): return lax.ppermute(shard, ('seg', 'trait'), pairs)  12.6 us
    pallas_call x7, Pallas kernels, call(): pl.pallas_call(kernel, out_shape=outs, in_specs=in_specs, out_specs=tuple...  9.51 us
    all_to_all x1, starting transfers between devices, exchange(): lax.all_to_all(packed.reshape(16, rows // 16, lanes), 'trait', 0, 0, tile...  7.05 us
    all_to_all x1, waiting for transfers between devices, exchange(): lax.all_to_all(packed.reshape(16, rows // 16, lanes), 'trait', 0, 0, tile...  5.15 us
    unnamed x6, local copies, waits for them, and re-layouts  4.13 us
  transfers between devices with their start and end apart: 5, of which 4 were waited for; matrix products, arithmetic and copies ran while one was open for 0% of the time, Pallas kernels for 5%

profile of v3, /device:TPU:96, one launch (start us, length us, event | category | flops | bytes accessed | tf_op | source)
XLA Modules:
  0.0 66.8 jit_solution(97975932518789025)
XLA Ops:
  0.0 0.0 copy-start.2
  0.0 2.0 %pack.1 = bf16[128,1536]{1,0:T(8,128)(2,1)} custom-call(bf16[192,1024]{1,0:T(8,128)(2,1)} %bitcast.14), custom_call_target="tpu_custom_call" | custom-call | bytes 393216 | tf_op jit(solution)/shard_map/pack/pallas_call | solution.py:210
  2.0 7.0 %all-to-all-start = ((bf16[16,8,1536]{2,1,0:T(8,128)(2,1)}), bf16[16,8,1536]{2,1,0:T(8,128)(2,1)S(1)}, u32[]{:S(2)}, u32[]{:S(2)}) async-start(bf16[16,8,1536]{2,1,0:T(8,128)(2,1)} %bitcast.13), calls=%async_computation | async-start | bytes 786432 | tf_op jit(solution)/shard_map/all_to_all | solution.py:234
  9.1 0.0 copy-start.1
  9.1 2.2 %copy-done.1 = bf16[1024,2048]{1,0:T(8,128)(2,1)S(1)} copy-done((bf16[1024,2048]{1,0:T(8,128)(2,1)S(1)}, bf16[1024,2048]{1,0:T(8,128)(2,1)}, u32[]{:S(2)}) %copy-start.1) | copy-done | bytes 4194328
  11.3 1.4 %skew.1 = (bf16[1024,1024]{1,0:T(8,128)(2,1)S(1)}, bf16[1024,2048]{1,0:T(8,128)(2,1)S(1)}) custom-call(bf16[1024,2048]{1,0:T(8,128)(2,1)S(1)} %copy-done.1), custom_call_target="tpu_custom_call" | custom-call | flops 2097152 | bytes 4194304 | tf_op jit(solution)/shard_map/skew/pallas_call | solution.py:210
  12.7 0.0 copy-start
  12.7 1.9 %copy-done = bf16[1024,2048]{1,0:T(8,128)(2,1)} copy-done((bf16[1024,2048]{1,0:T(8,128)(2,1)}, bf16[1024,2048]{1,0:T(8,128)(2,1)S(1)}, u32[]{:S(2)}) %copy-start) | copy-done | bytes 4194328
  14.7 5.2 %all-to-all-done = bf16[16,8,1536]{2,1,0:T(8,128)(2,1)S(1)} async-done(((bf16[16,8,1536]{2,1,0:T(8,128)(2,1)}), bf16[16,8,1536]{2,1,0:T(8,128)(2,1)S(1)}, u32[]{:S(2)}, u32[]{:S(2)}) %all-to-all-start) | async-done | bytes 393248 | tf_op jit(solution)/shard_map/all_to_all | solution.py:234
  19.8 0.0 copy-done.2
  19.8 2.8 %mix.1 = (bf16[192,1024]{1,0:T(8,128)(2,1)S(1)}, bf16[192,1024]{1,0:T(8,128)(2,1)S(1)}, bf16[192,1024]{1,0:T(8,128)(2,1)S(1)}, bf16[1024,2048]{1,0:T(8,128)(2,1)S(1)}) custom-call(bf16[128,1536]{1,0:T(8,128)(2,1)S(1)} %bitcast.10, f32[192,192]{1,0:T(8,128)S(1)} %copy-done.2, bf16[1024,2048]{1,0:T(8,128)(2,1)} %copy-done), custom_call_target="tpu_custom_call" | custom-call | flops 805306368 | bytes 4734976 | tf_op jit(solution)/shard_map/mix/pallas_call | solution.py:210
  22.6 2.6 %collective-permute-start.3 = (bf16[192,1024]{1,0:T(8,128)(2,1)S(1)}, bf16[192,1024]{1,0:T(8,128)(2,1)S(1)}, u32[]{:S(2)}, u32[]{:S(2)}) collective-permute-start(bf16[192,1024]{1,0:T(8,128)(2,1)S(1)} %get-tuple-element.15), channel_id=1, source_target_pairs={{0,16},{1,24},{2,18},{3,26},{4,20},{5,28},{6,22},{7,30},{8,17},{9,... | collective-permute-start | bytes 1179656 | tf_op jit(solution)/shard_map/ppermute | solution.py:229
  25.2 4.2 %collective-permute-start.2 = (bf16[192,1024]{1,0:T(8,128)(2,1)S(1)}, bf16[192,1024]{1,0:T(8,128)(2,1)S(1)}, u32[]{:S(2)}, u32[]{:S(2)}) collective-permute-start(bf16[192,1024]{1,0:T(8,128)(2,1)S(1)} %get-tuple-element.12.x_ref), channel_id=1, source_target_pairs={{16,0},{17,8},{18,2},{19,10},{20,4},{21,12},{22,6},{23,14},{24,1},... | collective-permute-start | bytes 1179656 | tf_op jit(solution)/shard_map/ppermute | solution.py:229
  29.4 6.2 %collective-permute-start.1 = (bf16[192,1024]{1,0:T(8,128)(2,1)S(1)}, bf16[192,1024]{1,0:T(8,128)(2,1)S(1)}, u32[]{:S(2)}, u32[]{:S(2)}) collective-permute-start(bf16[192,1024]{1,0:T(8,128)(2,1)S(1)} %get-tuple-element.13), channel_id=1, source_target_pairs={{0,32},{1,33},{2,34},{3,35},{4,36},{5,37},{6,38},{7,39},{8,40},{9,... | collective-permute-start | bytes 1179656 | tf_op jit(solution)/shard_map/ppermute | solution.py:229
  35.6 1.9 %collective-permute-start = (bf16[192,1024]{1,0:T(8,128)(2,1)S(1)}, bf16[192,1024]{1,0:T(8,128)(2,1)S(1)}, u32[]{:S(2)}, u32[]{:S(2)}) collective-permute-start(bf16[192,1024]{1,0:T(8,128)(2,1)S(1)} %get-tuple-element.12.x_ref), channel_id=1, source_target_pairs={{32,0},{33,1},{34,2},{35,3},{36,4},{37,5},{38,6},{39,7},{40,8},{41... | collective-permute-start | bytes 1179656 | tf_op jit(solution)/shard_map/ppermute | solution.py:229
  37.6 0.8 %own.1.total_ref = f32[192,1024]{1,0:T(8,128)S(1)} custom-call(bf16[192,1024]{1,0:T(8,128)(2,1)S(1)} %get-tuple-element.12.x_ref, bf16[1024,1024]{1,0:T(8,128)(2,1)S(1)} %get-tuple-element.16.dense_ref), custom_call_target="tpu_custom_call" | custom-call | flops 805306368 | bytes 2490368 | tf_op jit(solution)/shard_map/own/pallas_call | solution.py:210
  38.4 0.0 collective-permute-done.3.low_ref
  38.4 0.9 %collective-permute-done.2.x_ref = bf16[192,1024]{1,0:T(8,128)(2,1)S(1)} collective-permute-done((bf16[192,1024]{1,0:T(8,128)(2,1)S(1)}, bf16[192,1024]{1,0:T(8,128)(2,1)S(1)}, u32[]{:S(2)}, u32[]{:S(2)}) %collective-permute-start.2) | collective-permute-done | bytes 393248 | tf_op jit(solution)/shard_map/ppermute | solution.py:229
  39.3 0.8 %near.1.total_ref = f32[192,1024]{1,0:T(8,128)S(1)} custom-call(bf16[192,1024]{1,0:T(8,128)(2,1)S(1)} %collective-permute-done.2.x_ref, bf16[192,1024]{1,0:T(8,128)(2,1)S(1)} %collective-permute-done.3.low_ref, bf16[1024,2048]{1,0:T(8,128)(2,1)S(1)} %get-tuple-element.14.dense_ref, f32[192,1024]{1,0:T(8,128)S(1)} %own.1.total_ref), custom_call_target="tpu_custom_call" | custom-call | flops 402653184 | bytes 5767168 | tf_op jit(solution)/shard_map/near/pallas_call | solution.py:210
  40.1 4.5 %collective-permute-done.1.low_ref = bf16[192,1024]{1,0:T(8,128)(2,1)S(1)} collective-permute-done((bf16[192,1024]{1,0:T(8,128)(2,1)S(1)}, bf16[192,1024]{1,0:T(8,128)(2,1)S(1)}, u32[]{:S(2)}, u32[]{:S(2)}) %collective-permute-start.1) | collective-permute-done | bytes 393248 | tf_op jit(solution)/shard_map/ppermute | solution.py:229
  44.6 7.2 %collective-permute-done.x_ref = bf16[192,1024]{1,0:T(8,128)(2,1)S(1)} collective-permute-done((bf16[192,1024]{1,0:T(8,128)(2,1)S(1)}, bf16[192,1024]{1,0:T(8,128)(2,1)S(1)}, u32[]{:S(2)}, u32[]{:S(2)}) %collective-permute-start) | collective-permute-done | bytes 393248 | tf_op jit(solution)/shard_map/ppermute | solution.py:229
  51.8 0.6 far.1
  52.5 13.3 %all_to_all.10 = bf16[16,8,1536]{2,1,0:T(8,128)(2,1)S(1)} all-to-all(bf16[16,8,1536]{2,1,0:T(8,128)(2,1)S(1)} %bitcast.11), channel_id=1, replica_groups=mesh['seg'=32,'trait'=16] {'trait'}, dimensions={0} | all-to-all | bytes 786432 | tf_op jit(solution)/shard_map/all_to_all | solution.py:234
  65.8 1.0 %unpack.1 = bf16[192,1024]{1,0:T(8,128)(2,1)} custom-call(bf16[128,1536]{1,0:T(8,128)(2,1)S(1)} %bitcast.12), custom_call_target="tpu_custom_call" | custom-call | bytes 393216 | tf_op jit(solution)/shard_map/unpack/pallas_call | solution.py:210
Async XLA Ops:
  0.0 19.8 %copy-start.2 = (f32[192,192]{1,0:T(8,128)S(1)}, f32[192,192]{1,0:T(8,128)}, u32[]{:S(2)}) copy-start(f32[192,192]{1,0:T(8,128)} %p_ref.1) | copy-start | bytes 442372
  2.0 17.8 %all-to-all-start = ((bf16[16,8,1536]{2,1,0:T(8,128)(2,1)}), bf16[16,8,1536]{2,1,0:T(8,128)(2,1)S(1)}, u32[]{:S(2)}, u32[]{:S(2)}) async-start(bf16[16,8,1536]{2,1,0:T(8,128)(2,1)} %bitcast.13), calls=%async_computation | async-start | bytes 786432 | tf_op jit(solution)/shard_map/all_to_all | solution.py:234
  9.1 2.2 %copy-start.1 = (bf16[1024,2048]{1,0:T(8,128)(2,1)S(1)}, bf16[1024,2048]{1,0:T(8,128)(2,1)}, u32[]{:S(2)}) copy-start(bf16[1024,2048]{1,0:T(8,128)(2,1)} %band_ref.1) | copy-start | bytes 12582916
  12.7 1.9 %copy-start = (bf16[1024,2048]{1,0:T(8,128)(2,1)}, bf16[1024,2048]{1,0:T(8,128)(2,1)S(1)}, u32[]{:S(2)}) copy-start(bf16[1024,2048]{1,0:T(8,128)(2,1)S(1)} %get-tuple-element.11.beyond_ref) | copy-start | bytes 12582916
  22.6 15.7 %collective-permute-start.3 = (bf16[192,1024]{1,0:T(8,128)(2,1)S(1)}, bf16[192,1024]{1,0:T(8,128)(2,1)S(1)}, u32[]{:S(2)}, u32[]{:S(2)}) collective-permute-start(bf16[192,1024]{1,0:T(8,128)(2,1)S(1)} %get-tuple-element.15), channel_id=1, source_target_pairs={{0,16},{1,24},{2,18},{3,26},{4,20},{5,28},{6,22},{7,30},{8,17},{9,... | collective-permute-start | bytes 1179656 | tf_op jit(solution)/shard_map/ppermute | solution.py:229
  25.2 14.0 %collective-permute-start.2 = (bf16[192,1024]{1,0:T(8,128)(2,1)S(1)}, bf16[192,1024]{1,0:T(8,128)(2,1)S(1)}, u32[]{:S(2)}, u32[]{:S(2)}) collective-permute-start(bf16[192,1024]{1,0:T(8,128)(2,1)S(1)} %get-tuple-element.12.x_ref), channel_id=1, source_target_pairs={{16,0},{17,8},{18,2},{19,10},{20,4},{21,12},{22,6},{23,14},{24,1},... | collective-permute-start | bytes 1179656 | tf_op jit(solution)/shard_map/ppermute | solution.py:229
  29.4 15.2 %collective-permute-start.1 = (bf16[192,1024]{1,0:T(8,128)(2,1)S(1)}, bf16[192,1024]{1,0:T(8,128)(2,1)S(1)}, u32[]{:S(2)}, u32[]{:S(2)}) collective-permute-start(bf16[192,1024]{1,0:T(8,128)(2,1)S(1)} %get-tuple-element.13), channel_id=1, source_target_pairs={{0,32},{1,33},{2,34},{3,35},{4,36},{5,37},{6,38},{7,39},{8,40},{9,... | collective-permute-start | bytes 1179656 | tf_op jit(solution)/shard_map/ppermute | solution.py:229
  35.6 16.2 %collective-permute-start = (bf16[192,1024]{1,0:T(8,128)(2,1)S(1)}, bf16[192,1024]{1,0:T(8,128)(2,1)S(1)}, u32[]{:S(2)}, u32[]{:S(2)}) collective-permute-start(bf16[192,1024]{1,0:T(8,128)(2,1)S(1)} %get-tuple-element.12.x_ref), channel_id=1, source_target_pairs={{32,0},{33,1},{34,2},{35,3},{36,4},{37,5},{38,6},{39,7},{40,8},{41... | collective-permute-start | bytes 1179656 | tf_op jit(solution)/shard_map/ppermute | solution.py:229

commit v4 on v3

--- a/solution.py
+++ b/solution.py
@@ -86,18 +86,9 @@
             o_ref[128 + 16 * j : 144 + 16 * j, lanes] = tail.astype(BF16)
 
 
-def mix_kernel(x_ref, p_ref, beyond_ref, o_ref, near_ref, far_ref, held, sems):
+def mix_kernel(x_ref, p_ref, o_ref):
     m = o_ref.shape[1]
     half = m // 2
-    width = beyond_ref.shape[1]
-    chunks = sems.shape[0]
-    depth = width // chunks
-    copies = []
-    for k in range(chunks):
-        low = max(0, m + k * depth - width)
-        lanes = pl.ds(k * depth, depth)
-        copies.append(pltpu.make_async_copy(beyond_ref.at[low:, lanes], held.at[low:, lanes], sems.at[k]))
-        copies[-1].start()
     blank = jnp.zeros((4, p_ref.shape[1]), F32)
     heads, lows, highs = [], [], []
     for t in range(16):
@@ -114,28 +105,25 @@
         total = jnp.dot(upper, values, preferred_element_type=F32)
         total += jnp.dot(lower, values, preferred_element_type=F32)
         o_ref[:, first : first + half] = total.astype(BF16)
-    for k, copy in enumerate(copies):
-        copy.wait()
-        for col in range(k * depth, (k + 1) * depth, 256):
-            low = max(0, m + col - width)
-            part = jnp.dot(
-                o_ref[:, low:], held[low:, col : col + 256], preferred_element_type=F32
-            ).astype(BF16)
-            if col < m:
-                near_ref[:, col : col + 256] = part
-            else:
-                far_ref[:, col - m : col - m + 256] = part
-
-
-def skew_rows(band_ref, own_ref, beyond_ref, first):
+
+def lower_near_kernel(x_ref, dense_ref, o_ref):
+    o_ref[...] = jnp.dot(x_ref[...], dense_ref[...], preferred_element_type=F32).astype(BF16)
+
+
+def lower_far_kernel(x_ref, dense_ref, o_ref):
+    depth = 256
+    for i in range(0, x_ref.shape[1], depth):
+        part = jnp.dot(x_ref[:, i:], dense_ref[i:, i : i + depth], preferred_element_type=F32)
+        o_ref[:, i : i + depth] = part.astype(BF16)
+
+
+def skew_rows(band_ref, dense_refs, first):
     m, width = band_ref.shape
     rows = pl.ds(first, LANES)
 
     def put(col, tile):
-        if col < m:
-            own_ref[rows, pl.ds(col, LANES)] = tile
-        elif col < m + width:
-            beyond_ref[rows, pl.ds(col - m, LANES)] = tile
+        if col < m + width:
+            dense_refs[col // m][rows, pl.ds(col % m, LANES)] = tile
 
     a = lax.broadcasted_iota(jnp.int32, (LANES, LANES), 0)
     b = lax.broadcasted_iota(jnp.int32, (LANES, LANES), 1)
@@ -156,9 +144,9 @@
         put(first + width + LANES, zero.astype(BF16))
 
 
-def skew_kernel(band_ref, own_ref, beyond_ref):
+def skew_kernel(band_ref, *dense_refs):
     for first in range(0, band_ref.shape[0], LANES):
-        skew_rows(band_ref, own_ref, beyond_ref, first)
+        skew_rows(band_ref, dense_refs, first)
 
 
 def contract(values, dense):
@@ -176,20 +164,19 @@
         o_ref[:, i:high] = total
 
 
-def near_kernel(x_ref, low_ref, dense_ref, total_ref, o_ref):
+def far_kernel(x_ref, dense_ref, total_ref, o_ref):
     m = x_ref.shape[1]
-    part = contract(x_ref[...], dense_ref[:, :m])
-    o_ref[...] = total_ref[...] + low_ref[...].astype(F32) + part
-
-
-def far_kernel(x_ref, low_ref, dense_ref, total_ref, o_ref, wide):
-    m = x_ref.shape[1]
-    half = m // 2
     depth = 256
     for i in range(0, m, depth):
         high = i + depth
-        part = contract(x_ref[:, :high], dense_ref[i:high, m : m + high])
-        wide[:, i:high] = total_ref[:, i:high] + low_ref[:, i:high].astype(F32) + part
+        o_ref[:, i:high] = total_ref[:, i:high] + contract(x_ref[:, :high], dense_ref[i:high, :high])
+
+
+def near_kernel(x_ref, low_near_ref, low_far_ref, dense_ref, total_ref, o_ref, wide):
+    m = x_ref.shape[1]
+    half = m // 2
+    wide[...] = total_ref[...] + low_near_ref[...].astype(F32) + low_far_ref[...].astype(F32)
+    wide[...] += contract(x_ref[...], dense_ref[...])
     for t in range(0, 16, 2):
         parts = []
         for u in (t, t + 1):
@@ -229,6 +216,12 @@
     return lax.ppermute(shard, ("seg", "trait"), pairs)
 
 
+def traded(shard):
+    length, places = lax.axis_size("seg"), lax.axis_size("trait")
+    pairs = [(s * places + p, (s ^ 1) * places + swapped(p)) for s in range(length) for p in range(places)]
+    return lax.ppermute(shard, ("seg", "trait"), pairs)
+
+
 def exchange(packed):
     rows, lanes = packed.shape
     moved = lax.all_to_all(packed.reshape(16, rows // 16, lanes), "trait", 0, 0, tiled=True)
@@ -254,26 +247,26 @@
             pltpu.SemaphoreType.DMA((5,)),
         ],
     )
-    within, beyond = call(
-        skew_kernel, "skew", (struct((m, m), BF16), struct((m, width), BF16)), 16, band, flops=m * width
+    square = struct((m, m), BF16)
+    within, following, last = call(
+        skew_kernel, "skew", (square, square, square), 16, band, flops=m * width
     )
     thin = struct((rows, m), BF16)
-    mixed, low_near, low_far, beyond = call(
-        mix_kernel, "mix", (thin, thin, thin, struct((m, width), BF16)), 48,
-        exchange(packed), precision, beyond,
-        flops=2 * rows * m * width, far_off=(2,),
-        scratch=[pltpu.SemaphoreType.DMA((4,))],
-    )
+    gathered, following = lax.optimization_barrier((exchange(packed), following))
+    mixed = call(mix_kernel, "mix", thin, 16, gathered, precision, flops=4 * rows * rows * m)
+    far = passed_along(mixed, -2)
+    low_near = call(lower_near_kernel, "lower_near", thin, 16, mixed, following, flops=2 * rows * m * m)
     low_near = passed_along(low_near, 1)
-    near = passed_along(mixed, -1)
+    low_far = call(lower_far_kernel, "lower_far", thin, 16, mixed, last, flops=rows * m * m)
     low_far = passed_along(low_far, 2)
-    far = passed_along(mixed, -2)
+    odd = lax.axis_index("seg") % 2 == 1
+    near = traded(jnp.where(odd, mixed, far))
     wide = struct((rows, m), F32)
     total = call(own_kernel, "own", wide, 16, mixed, within, flops=4 * rows * m * m)
-    total = call(near_kernel, "near", wide, 16, near, low_near, beyond, total, flops=2 * rows * m * m)
+    total = call(far_kernel, "far", wide, 16, far, last, total, flops=rows * m * m)
     packed = call(
-        far_kernel, "far", struct(packed_shape, BF16), 16, far, low_far, beyond, total,
-        flops=rows * m * m, scratch=[pltpu.VMEM((rows, m), F32)],
+        near_kernel, "near", struct(packed_shape, BF16), 16, near, low_near, low_far, following, total,
+        flops=2 * rows * m * m, scratch=[pltpu.VMEM((rows, m), F32)],
     )
     flat = call(
         unpack_kernel, "unpack", struct((rows, m), BF16), 8, exchange(packed),

time: 67.2 us -> 62.3 us (0.927)
  the two profiles are of different devices: /device:TPU:96 before, /device:TPU:392 now
where the time goes in v4:
time: 62.3 us; the launch traced here: 61.9 us
  starting transfers between devices  19.1 us (31%)
  waiting for transfers between devices  16.1 us (26%)
  blocking collectives  13.6 us (22%)
  Pallas kernels  8.07 us (13%)
  local copies, waits for them, and re-layouts  4.83 us (8%)
    all_to_all x1, blocking collectives, exchange(): lax.all_to_all(packed.reshape(16, rows // 16, lanes), 'trait', 0, 0, tile...  13.6 us
    ppermute x3, waiting for transfers between devices, passed_along(): return lax.ppermute(shard, ('seg', 'trait'), pairs)  11.6 us
    ppermute x3, starting transfers between devices, passed_along(): return lax.ppermute(shard, ('seg', 'trait'), pairs)  9.67 us
    pallas_call x9, Pallas kernels, call(): pl.pallas_call(kernel, out_shape=outs, in_specs=in_specs, out_specs=tuple...  8.07 us
    all_to_all x1, starting transfers between devices, exchange(): lax.all_to_all(packed.reshape(16, rows // 16, lanes), 'trait', 0, 0, tile...  6.15 us
    unnamed x12, local copies, waits for them, and re-layouts  4.83 us
    all_to_all x1, waiting for transfers between devices, exchange(): lax.all_to_all(packed.reshape(16, rows // 16, lanes), 'trait', 0, 0, tile...  4.45 us
    ppermute x1, starting transfers between devices, traded(): return lax.ppermute(shard, ('seg', 'trait'), pairs)  3.26 us
  transfers between devices with their start and end apart: 5, of which 3 were waited for; matrix products, arithmetic and copies ran while one was open for 0% of the time, Pallas kernels for 6%

profile of v4, /device:TPU:392, one launch (start us, length us, event | category | flops | bytes accessed | tf_op | source)
XLA Modules:
  0.0 61.9 jit_solution(4284028771726176235)
XLA Ops:
  0.0 2.0 %pack.1 = bf16[128,1536]{1,0:T(8,128)(2,1)} custom-call(bf16[192,1024]{1,0:T(8,128)(2,1)} %bitcast.14), custom_call_target="tpu_custom_call" | custom-call | bytes 393216 | tf_op jit(solution)/shard_map/pack/pallas_call | solution.py:197
  2.0 6.1 %all-to-all-start = ((bf16[16,8,1536]{2,1,0:T(8,128)(2,1)}), bf16[16,8,1536]{2,1,0:T(8,128)(2,1)S(1)}, u32[]{:S(2)}, u32[]{:S(2)}) async-start(bf16[16,8,1536]{2,1,0:T(8,128)(2,1)} %bitcast.13), calls=%async_computation | async-start | bytes 786432 | tf_op jit(solution)/shard_map/all_to_all | solution.py:227
  8.1 0.0 copy-start.2
  8.2 2.2 %copy-done.2 = bf16[1024,2048]{1,0:T(8,128)(2,1)S(1)} copy-done((bf16[1024,2048]{1,0:T(8,128)(2,1)S(1)}, bf16[1024,2048]{1,0:T(8,128)(2,1)}, u32[]{:S(2)}) %copy-start.2) | copy-done | bytes 4194328
  10.3 1.4 %skew.1 = (bf16[1024,1024]{1,0:T(8,128)(2,1)S(1)}, bf16[1024,1024]{1,0:T(8,128)(2,1)S(1)}, bf16[1024,1024]{1,0:T(8,128)(2,1)S(1)}) custom-call(bf16[1024,2048]{1,0:T(8,128)(2,1)S(1)} %copy-done.2), custom_call_target="tpu_custom_call" | custom-call | flops 2097152 | bytes 4194304 | tf_op jit(solution)/shard_map/skew/pallas_call | solution.py:197
  11.8 1.3 %copy-done = bf16[1024,1024]{1,0:T(8,128)(2,1)} copy-done((bf16[1024,1024]{1,0:T(8,128)(2,1)}, bf16[1024,1024]{1,0:T(8,128)(2,1)S(1)}, u32[]{:S(2)}) %copy-start) | copy-done | bytes 2097176
  13.1 1.3 %copy-done.3 = bf16[1024,1024]{1,0:T(8,128)(2,1)} copy-done((bf16[1024,1024]{1,0:T(8,128)(2,1)}, bf16[1024,1024]{1,0:T(8,128)(2,1)S(1)}, u32[]{:S(2)}) %copy-start.3) | copy-done | bytes 2097176
  14.4 4.5 %all-to-all-done = bf16[16,8,1536]{2,1,0:T(8,128)(2,1)S(1)} async-done(((bf16[16,8,1536]{2,1,0:T(8,128)(2,1)}), bf16[16,8,1536]{2,1,0:T(8,128)(2,1)S(1)}, u32[]{:S(2)}, u32[]{:S(2)}) %all-to-all-start) | async-done | bytes 393248 | tf_op jit(solution)/shard_map/all_to_all | solution.py:227
  18.9 0.4 mix.1.x_ref
  19.3 4.1 %collective-permute-start = (bf16[192,1024]{1,0:T(8,128)(2,1)S(1)}, bf16[192,1024]{1,0:T(8,128)(2,1)S(1)}, u32[]{:S(2)}, u32[]{:S(2)}) collective-permute-start(bf16[192,1024]{1,0:T(8,128)(2,1)S(1)} %mix.1.x_ref), channel_id=1, source_target_pairs={{32,0},{33,1},{34,2},{35,3},{36,4},{37,5},{38,6},{39,7},{40,8},{41... | collective-permute-start | bytes 1179656 | tf_op jit(solution)/shard_map/ppermute | solution.py:216
  23.4 0.6 lower_near.1
  24.1 2.6 %collective-permute-start.2 = (bf16[192,1024]{1,0:T(8,128)(2,1)S(1)}, bf16[192,1024]{1,0:T(8,128)(2,1)S(1)}, u32[]{:S(2)}, u32[]{:S(2)}) collective-permute-start(bf16[192,1024]{1,0:T(8,128)(2,1)S(1)} %lower_near.1), channel_id=1, source_target_pairs={{0,16},{1,24},{2,18},{3,26},{4,20},{5,28},{6,22},{7,30},{8,17},{9,... | collective-permute-start | bytes 1179656 | tf_op jit(solution)/shard_map/ppermute | solution.py:216
  26.7 0.4 lower_far.1
  27.2 2.9 %collective-permute-start.3 = (bf16[192,1024]{1,0:T(8,128)(2,1)S(1)}, bf16[192,1024]{1,0:T(8,128)(2,1)S(1)}, u32[]{:S(2)}, u32[]{:S(2)}) collective-permute-start(bf16[192,1024]{1,0:T(8,128)(2,1)S(1)} %lower_far.1), channel_id=1, source_target_pairs={{0,32},{1,33},{2,34},{3,35},{4,36},{5,37},{6,38},{7,39},{8,40},{9,... | collective-permute-start | bytes 1179656 | tf_op jit(solution)/shard_map/ppermute | solution.py:216
  30.1 1.6 %collective-permute-done.x_ref = bf16[192,1024]{1,0:T(8,128)(2,1)S(1)} collective-permute-done((bf16[192,1024]{1,0:T(8,128)(2,1)S(1)}, bf16[192,1024]{1,0:T(8,128)(2,1)S(1)}, u32[]{:S(2)}, u32[]{:S(2)}) %collective-permute-start) | collective-permute-done | bytes 393248 | tf_op jit(solution)/shard_map/ppermute | solution.py:216
  31.7 3.3 %collective-permute-start.1 = (bf16[192,1024]{1,0:T(8,128)(2,1)S(1)}, bf16[192,1024]{1,0:T(8,128)(2,1)S(1)}, u32[]{:S(2)}, u32[]{:S(2)}) collective-permute-start(bf16[192,1024]{1,0:T(8,128)(2,1)S(1)} %broadcast_select_fusion), channel_id=1, source_target_pairs={{0,16},{1,24},{2,18},{3,26},{4,20},{5,28},{6,22},{7,30},{8,17},{9,... | collective-permute-start | bytes 1179656 | tf_op jit(solution)/shard_map/ppermute | solution.py:222
  35.0 0.8 %own.1.total_ref = f32[192,1024]{1,0:T(8,128)S(1)} custom-call(bf16[192,1024]{1,0:T(8,128)(2,1)S(1)} %mix.1.x_ref, bf16[1024,1024]{1,0:T(8,128)(2,1)S(1)} %copy-done.4), custom_call_target="tpu_custom_call" | custom-call | flops 805306368 | bytes 2490368 | tf_op jit(solution)/shard_map/own/pallas_call | solution.py:197
  35.8 0.6 far.1.total_ref
  36.4 0.0 collective-permute-done.2.low_near_ref
  36.4 10.0 %collective-permute-done.3.low_far_ref = bf16[192,1024]{1,0:T(8,128)(2,1)S(1)} collective-permute-done((bf16[192,1024]{1,0:T(8,128)(2,1)S(1)}, bf16[192,1024]{1,0:T(8,128)(2,1)S(1)}, u32[]{:S(2)}, u32[]{:S(2)}) %collective-permute-start.3) | collective-permute-done | bytes 393248 | tf_op jit(solution)/shard_map/ppermute | solution.py:216
  46.4 0.0 collective-permute-done.1.x_ref
  46.4 0.9 %near.1 = bf16[128,1536]{1,0:T(8,128)(2,1)S(1)} custom-call(bf16[192,1024]{1,0:T(8,128)(2,1)S(1)} %collective-permute-done.1.x_ref, bf16[192,1024]{1,0:T(8,128)(2,1)S(1)} %collective-permute-done.2.low_near_ref, bf16[192,1024]{1,0:T(8,128)(2,1)S(1)} %collective-permute-done.3.low_far_ref, bf16[1024,1024]{1,0:T(8,128)(2,1)S(1)} %get-tuple-element.12.dense_ref, ...), custom_call_target="tpu_custom_call" | custom-call | flops 402653184 | bytes 4063232 | tf_op jit(solution)/shard_map/near/pallas_call | solution.py:197
  47.3 13.6 %all_to_all.10 = bf16[16,8,1536]{2,1,0:T(8,128)(2,1)S(1)} all-to-all(bf16[16,8,1536]{2,1,0:T(8,128)(2,1)S(1)} %bitcast.10), channel_id=1, replica_groups=mesh['seg'=32,'trait'=16] {'trait'}, dimensions={0} | all-to-all | bytes 786432 | tf_op jit(solution)/shard_map/all_to_all | solution.py:227
  60.9 1.0 %unpack.1 = bf16[192,1024]{1,0:T(8,128)(2,1)} custom-call(bf16[128,1536]{1,0:T(8,128)(2,1)S(1)} %bitcast.11), custom_call_target="tpu_custom_call" | custom-call | bytes 393216 | tf_op jit(solution)/shard_map/unpack/pallas_call | solution.py:197
  (9 shorter events, 0.1 us)
Async XLA Ops:
  2.0 16.9 %all-to-all-start = ((bf16[16,8,1536]{2,1,0:T(8,128)(2,1)}), bf16[16,8,1536]{2,1,0:T(8,128)(2,1)S(1)}, u32[]{:S(2)}, u32[]{:S(2)}) async-start(bf16[16,8,1536]{2,1,0:T(8,128)(2,1)} %bitcast.13), calls=%async_computation | async-start | bytes 786432 | tf_op jit(solution)/shard_map/all_to_all | solution.py:227
  8.1 2.2 %copy-start.2 = (bf16[1024,2048]{1,0:T(8,128)(2,1)S(1)}, bf16[1024,2048]{1,0:T(8,128)(2,1)}, u32[]{:S(2)}) copy-start(bf16[1024,2048]{1,0:T(8,128)(2,1)} %band_ref.1) | copy-start | bytes 12582916
  10.3 8.5 %copy-start.5 = (f32[192,192]{1,0:T(8,128)S(1)}, f32[192,192]{1,0:T(8,128)}, u32[]{:S(2)}) copy-start(f32[192,192]{1,0:T(8,128)} %p_ref.1) | copy-start | bytes 442372
  11.8 1.3 %copy-start = (bf16[1024,1024]{1,0:T(8,128)(2,1)}, bf16[1024,1024]{1,0:T(8,128)(2,1)S(1)}, u32[]{:S(2)}) copy-start(bf16[1024,1024]{1,0:T(8,128)(2,1)S(1)} %get-tuple-element.13.dense_ref) | copy-start | bytes 6291460
  13.1 1.3 %copy-start.3 = (bf16[1024,1024]{1,0:T(8,128)(2,1)}, bf16[1024,1024]{1,0:T(8,128)(2,1)S(1)}, u32[]{:S(2)}) copy-start(bf16[1024,1024]{1,0:T(8,128)(2,1)S(1)} %get-tuple-element.14.dense_ref) | copy-start | bytes 6291460
  19.3 12.4 %collective-permute-start = (bf16[192,1024]{1,0:T(8,128)(2,1)S(1)}, bf16[192,1024]{1,0:T(8,128)(2,1)S(1)}, u32[]{:S(2)}, u32[]{:S(2)}) collective-permute-start(bf16[192,1024]{1,0:T(8,128)(2,1)S(1)} %mix.1.x_ref), channel_id=1, source_target_pairs={{32,0},{33,1},{34,2},{35,3},{36,4},{37,5},{38,6},{39,7},{40,8},{41... | collective-permute-start | bytes 1179656 | tf_op jit(solution)/shard_map/ppermute | solution.py:216
  23.4 3.3 %copy-start.1 = (bf16[1024,1024]{1,0:T(8,128)(2,1)S(1)}, bf16[1024,1024]{1,0:T(8,128)(2,1)}, u32[]{:S(2)}) copy-start(bf16[1024,1024]{1,0:T(8,128)(2,1)} %copy-done) | copy-start | bytes 6291460
  24.0 11.0 %copy-start.4 = (bf16[1024,1024]{1,0:T(8,128)(2,1)S(1)}, bf16[1024,1024]{1,0:T(8,128)(2,1)}, u32[]{:S(2)}) copy-start(bf16[1024,1024]{1,0:T(8,128)(2,1)} %copy-done.3) | copy-start | bytes 6291460
  24.1 12.3 %collective-permute-start.2 = (bf16[192,1024]{1,0:T(8,128)(2,1)S(1)}, bf16[192,1024]{1,0:T(8,128)(2,1)S(1)}, u32[]{:S(2)}, u32[]{:S(2)}) collective-permute-start(bf16[192,1024]{1,0:T(8,128)(2,1)S(1)} %lower_near.1), channel_id=1, source_target_pairs={{0,16},{1,24},{2,18},{3,26},{4,20},{5,28},{6,22},{7,30},{8,17},{9,... | collective-permute-start | bytes 1179656 | tf_op jit(solution)/shard_map/ppermute | solution.py:216
  27.2 19.3 %collective-permute-start.3 = (bf16[192,1024]{1,0:T(8,128)(2,1)S(1)}, bf16[192,1024]{1,0:T(8,128)(2,1)S(1)}, u32[]{:S(2)}, u32[]{:S(2)}) collective-permute-start(bf16[192,1024]{1,0:T(8,128)(2,1)S(1)} %lower_far.1), channel_id=1, source_target_pairs={{0,32},{1,33},{2,34},{3,35},{4,36},{5,37},{6,38},{7,39},{8,40},{9,... | collective-permute-start | bytes 1179656 | tf_op jit(solution)/shard_map/ppermute | solution.py:216
  31.7 14.7 %collective-permute-start.1 = (bf16[192,1024]{1,0:T(8,128)(2,1)S(1)}, bf16[192,1024]{1,0:T(8,128)(2,1)S(1)}, u32[]{:S(2)}, u32[]{:S(2)}) collective-permute-start(bf16[192,1024]{1,0:T(8,128)(2,1)S(1)} %broadcast_select_fusion), channel_id=1, source_target_pairs={{0,16},{1,24},{2,18},{3,26},{4,20},{5,28},{6,22},{7,30},{8,17},{9,... | collective-permute-start | bytes 1179656 | tf_op jit(solution)/shard_map/ppermute | solution.py:222

commit v5 on v4

--- a/solution.py
+++ b/solution.py
@@ -114,7 +114,7 @@
     depth = 256
     for i in range(0, x_ref.shape[1], depth):
         part = jnp.dot(x_ref[:, i:], dense_ref[i:, i : i + depth], preferred_element_type=F32)
-        o_ref[:, i : i + depth] = part.astype(BF16)
+        o_ref[:, i : i + depth] = part
 
 
 def skew_rows(band_ref, dense_refs, first):
@@ -149,6 +149,25 @@
         skew_rows(band_ref, dense_refs, first)
 
 
+def on_odd_segment():
+    return lax.rem(lax.axis_index("seg"), 2) == 1
+
+
+def join_kernel(far_ref, near_ref, o_ref):
+    near = near_ref[...].astype(F32)
+    o_ref[...] = (far_ref[...] + jnp.where(on_odd_segment(), jnp.zeros_like(near), near)).astype(BF16)
+
+
+def choose_kernel(own_ref, far_ref, o_ref):
+    @pl.when(on_odd_segment())
+    def _():
+        o_ref[...] = own_ref[...]
+
+    @pl.when(jnp.logical_not(on_odd_segment()))
+    def _():
+        o_ref[...] = far_ref[...]
+
+
 def contract(values, dense):
     return lax.dot_general(values, dense, (((1,), (1,)), ((), ())), preferred_element_type=F32)
 
@@ -172,10 +191,12 @@
         o_ref[:, i:high] = total_ref[:, i:high] + contract(x_ref[:, :high], dense_ref[i:high, :high])
 
 
-def near_kernel(x_ref, low_near_ref, low_far_ref, dense_ref, total_ref, o_ref, wide):
+def near_kernel(low_far_ref, low_near_ref, x_ref, dense_ref, total_ref, o_ref, wide):
     m = x_ref.shape[1]
     half = m // 2
-    wide[...] = total_ref[...] + low_near_ref[...].astype(F32) + low_far_ref[...].astype(F32)
+    low_near = low_near_ref[...].astype(F32)
+    low_near = jnp.where(on_odd_segment(), low_near, jnp.zeros_like(low_near))
+    wide[...] = total_ref[...] + low_near + low_far_ref[...].astype(F32)
     wide[...] += contract(x_ref[...], dense_ref[...])
     for t in range(0, 16, 2):
         parts = []
@@ -207,13 +228,9 @@
 
 
 def passed_along(shard, by):
-    length, places = lax.axis_size("seg"), lax.axis_size("trait")
-    pairs = []
-    for s in range(length):
-        for p in range(places):
-            if 0 <= s + by < length:
-                pairs.append((s * places + p, (s + by) * places + (swapped(p) if by % 2 else p)))
-    return lax.ppermute(shard, ("seg", "trait"), pairs)
+    length = lax.axis_size("seg")
+    pairs = [(s, s + by) for s in range(length) if 0 <= s + by < length]
+    return lax.ppermute(shard, "seg", pairs)
 
 
 def traded(shard):
@@ -252,20 +269,20 @@
         skew_kernel, "skew", (square, square, square), 16, band, flops=m * width
     )
     thin = struct((rows, m), BF16)
+    wide = struct((rows, m), F32)
     gathered, following = lax.optimization_barrier((exchange(packed), following))
     mixed = call(mix_kernel, "mix", thin, 16, gathered, precision, flops=4 * rows * rows * m)
     far = passed_along(mixed, -2)
     low_near = call(lower_near_kernel, "lower_near", thin, 16, mixed, following, flops=2 * rows * m * m)
-    low_near = passed_along(low_near, 1)
-    low_far = call(lower_far_kernel, "lower_far", thin, 16, mixed, last, flops=rows * m * m)
+    low_near = traded(low_near)
+    low_far = call(lower_far_kernel, "lower_far", wide, 16, mixed, last, flops=rows * m * m)
+    low_far = call(join_kernel, "join", thin, 8, low_far, low_near)
     low_far = passed_along(low_far, 2)
-    odd = lax.axis_index("seg") % 2 == 1
-    near = traded(jnp.where(odd, mixed, far))
-    wide = struct((rows, m), F32)
+    near = traded(call(choose_kernel, "choose", thin, 8, mixed, far))
     total = call(own_kernel, "own", wide, 16, mixed, within, flops=4 * rows * m * m)
     total = call(far_kernel, "far", wide, 16, far, last, total, flops=rows * m * m)
     packed = call(
-        near_kernel, "near", struct(packed_shape, BF16), 16, near, low_near, low_far, following, total,
+        near_kernel, "near", struct(packed_shape, BF16), 16, low_far, low_near, near, following, total,
         flops=2 * rows * m * m, scratch=[pltpu.VMEM((rows, m), F32)],
     )
     flat = call(

time: 62.3 us -> 63.1 us (1.013)
  the two profiles are of different devices: /device:TPU:392 before, /device:TPU:1 now
where the time goes in v5:
time: 63.1 us; the launch traced here: 62.7 us
  starting transfers between devices  20 us (32%)
  waiting for transfers between devices  15.6 us (25%)
  blocking collectives  13.9 us (22%)
  Pallas kernels  8.2 us (13%)
  local copies, waits for them, and re-layouts  4.83 us (8%)
    all_to_all x1, blocking collectives, exchange(): lax.all_to_all(packed.reshape(16, rows // 16, lanes), 'trait', 0, 0, tile...  13.9 us
    ppermute x2, waiting for transfers between devices, traded(): return lax.ppermute(shard, ('seg', 'trait'), pairs)  10.2 us
    all_to_all x1, starting transfers between devices, exchange(): lax.all_to_all(packed.reshape(16, rows // 16, lanes), 'trait', 0, 0, tile...  10.2 us
    pallas_call x11, Pallas kernels, call(): pl.pallas_call(kernel, out_shape=outs, in_specs=in_specs, out_specs=tuple...  8.2 us
    ppermute x2, starting transfers between devices, traded(): return lax.ppermute(shard, ('seg', 'trait'), pairs)  6.82 us
    unnamed x12, local copies, waits for them, and re-layouts  4.83 us
    all_to_all x1, waiting for transfers between devices, exchange(): lax.all_to_all(packed.reshape(16, rows // 16, lanes), 'trait', 0, 0, tile...  3.62 us
    ppermute x2, starting transfers between devices, passed_along(): return lax.ppermute(shard, 'seg', pairs)  2.98 us
  transfers between devices with their start and end apart: 5, of which 5 were waited for; matrix products, arithmetic and copies ran while one was open for 0% of the time, Pallas kernels for 5%

profile of v5, /device:TPU:1, one launch (start us, length us, event | category | flops | bytes accessed | tf_op | source)
XLA Modules:
  0.0 62.7 jit_solution(5359604430468142469)
XLA Ops:
  0.0 2.0 %pack.1 = bf16[128,1536]{1,0:T(8,128)(2,1)} custom-call(bf16[192,1024]{1,0:T(8,128)(2,1)} %bitcast.14), custom_call_target="tpu_custom_call" | custom-call | bytes 393216 | tf_op jit(solution)/shard_map/pack/pallas_call | solution.py:218
  2.0 10.2 %all-to-all-start = ((bf16[16,8,1536]{2,1,0:T(8,128)(2,1)}), bf16[16,8,1536]{2,1,0:T(8,128)(2,1)S(1)}, u32[]{:S(2)}, u32[]{:S(2)}) async-start(bf16[16,8,1536]{2,1,0:T(8,128)(2,1)} %bitcast.13), calls=%async_computation | async-start | bytes 786432 | tf_op jit(solution)/shard_map/all_to_all | solution.py:244
  12.2 2.2 %copy-done.2 = bf16[1024,2048]{1,0:T(8,128)(2,1)S(1)} copy-done((bf16[1024,2048]{1,0:T(8,128)(2,1)S(1)}, bf16[1024,2048]{1,0:T(8,128)(2,1)}, u32[]{:S(2)}) %copy-start.2) | copy-done | bytes 4194328
  14.4 1.4 %skew.1 = (bf16[1024,1024]{1,0:T(8,128)(2,1)S(1)}, bf16[1024,1024]{1,0:T(8,128)(2,1)S(1)}, bf16[1024,1024]{1,0:T(8,128)(2,1)S(1)}) custom-call(bf16[1024,2048]{1,0:T(8,128)(2,1)S(1)} %copy-done.2), custom_call_target="tpu_custom_call" | custom-call | flops 2097152 | bytes 4194304 | tf_op jit(solution)/shard_map/skew/pallas_call | solution.py:218
  15.8 1.3 %copy-done = bf16[1024,1024]{1,0:T(8,128)(2,1)} copy-done((bf16[1024,1024]{1,0:T(8,128)(2,1)}, bf16[1024,1024]{1,0:T(8,128)(2,1)S(1)}, u32[]{:S(2)}) %copy-start) | copy-done | bytes 2097176
  17.2 1.3 %copy-done.3 = bf16[1024,1024]{1,0:T(8,128)(2,1)} copy-done((bf16[1024,1024]{1,0:T(8,128)(2,1)}, bf16[1024,1024]{1,0:T(8,128)(2,1)S(1)}, u32[]{:S(2)}) %copy-start.3) | copy-done | bytes 2097176
  18.5 3.6 %all-to-all-done = bf16[16,8,1536]{2,1,0:T(8,128)(2,1)S(1)} async-done(((bf16[16,8,1536]{2,1,0:T(8,128)(2,1)}), bf16[16,8,1536]{2,1,0:T(8,128)(2,1)S(1)}, u32[]{:S(2)}, u32[]{:S(2)}) %all-to-all-start) | async-done | bytes 393248 | tf_op jit(solution)/shard_map/all_to_all | solution.py:244
  22.1 0.4 mix.1.x_ref.own_ref
  22.5 0.6 lower_near.1
  23.1 1.9 %collective-permute-start = (bf16[192,1024]{1,0:T(8,128)(2,1)S(1)}, bf16[192,1024]{1,0:T(8,128)(2,1)S(1)}, u32[]{:S(2)}, u32[]{:S(2)}) collective-permute-start(bf16[192,1024]{1,0:T(8,128)(2,1)S(1)} %lower_near.1), channel_id=1, source_target_pairs={{0,16},{1,24},{2,18},{3,26},{4,20},{5,28},{6,22},{7,30},{8,17},{9,... | collective-permute-start | bytes 1179656 | tf_op jit(solution)/shard_map/ppermute | solution.py:239
  25.1 1.3 %collective-permute-start.2 = (bf16[192,1024]{1,0:T(8,128)(2,1)S(1)}, bf16[192,1024]{1,0:T(8,128)(2,1)S(1)}, u32[]{:S(2)}, u32[]{:S(2)}) collective-permute-start(bf16[192,1024]{1,0:T(8,128)(2,1)S(1)} %mix.1.x_ref.own_ref), channel_id=1, source_target_pairs={{32,0},{48,16},{64,32},{80,48},{96,64},{112,80},{128,96},{144,112}... | collective-permute-start | bytes 1179656 | tf_op jit(solution)/shard_map/ppermute | solution.py:233
  26.4 0.4 lower_far.1.far_ref
  26.8 6.6 %collective-permute-done.near_ref.low_near_ref = bf16[192,1024]{1,0:T(8,128)(2,1)S(1)} collective-permute-done((bf16[192,1024]{1,0:T(8,128)(2,1)S(1)}, bf16[192,1024]{1,0:T(8,128)(2,1)S(1)}, u32[]{:S(2)}, u32[]{:S(2)}) %collective-permute-start) | collective-permute-done | bytes 393248 | tf_op jit(solution)/shard_map/ppermute | solution.py:239
  33.4 0.1 join.1
  33.5 1.7 %collective-permute-start.1 = (bf16[192,1024]{1,0:T(8,128)(2,1)S(1)}, bf16[192,1024]{1,0:T(8,128)(2,1)S(1)}, u32[]{:S(2)}, u32[]{:S(2)}) collective-permute-start(bf16[192,1024]{1,0:T(8,128)(2,1)S(1)} %join.1), channel_id=1, source_target_pairs={{0,32},{16,48},{32,64},{48,80},{64,96},{80,112},{96,128},{112,144}... | collective-permute-start | bytes 1179656 | tf_op jit(solution)/shard_map/ppermute | solution.py:233
  35.2 1.3 %collective-permute-done.2.far_ref.x_ref = bf16[192,1024]{1,0:T(8,128)(2,1)S(1)} collective-permute-done((bf16[192,1024]{1,0:T(8,128)(2,1)S(1)}, bf16[192,1024]{1,0:T(8,128)(2,1)S(1)}, u32[]{:S(2)}, u32[]{:S(2)}) %collective-permute-start.2) | collective-permute-done | bytes 393248 | tf_op jit(solution)/shard_map/ppermute | solution.py:233
  36.6 4.9 %collective-permute-start.3 = (bf16[192,1024]{1,0:T(8,128)(2,1)S(1)}, bf16[192,1024]{1,0:T(8,128)(2,1)S(1)}, u32[]{:S(2)}, u32[]{:S(2)}) collective-permute-start(bf16[192,1024]{1,0:T(8,128)(2,1)S(1)} %choose.1), channel_id=1, source_target_pairs={{0,16},{1,24},{2,18},{3,26},{4,20},{5,28},{6,22},{7,30},{8,17},{9,... | collective-permute-start | bytes 1179656 | tf_op jit(solution)/shard_map/ppermute | solution.py:239
  41.5 0.8 %own.1.total_ref = f32[192,1024]{1,0:T(8,128)S(1)} custom-call(bf16[192,1024]{1,0:T(8,128)(2,1)S(1)} %mix.1.x_ref.own_ref, bf16[1024,1024]{1,0:T(8,128)(2,1)S(1)} %copy-done.4), custom_call_target="tpu_custom_call" | custom-call | flops 805306368 | bytes 2490368 | tf_op jit(solution)/shard_map/own/pallas_call | solution.py:218
  42.3 0.6 far.1.total_ref
  42.9 0.4 collective-permute-done.1.low_far_ref
  43.3 3.6 %collective-permute-done.3.x_ref = bf16[192,1024]{1,0:T(8,128)(2,1)S(1)} collective-permute-done((bf16[192,1024]{1,0:T(8,128)(2,1)S(1)}, bf16[192,1024]{1,0:T(8,128)(2,1)S(1)}, u32[]{:S(2)}, u32[]{:S(2)}) %collective-permute-start.3) | collective-permute-done | bytes 393248 | tf_op jit(solution)/shard_map/ppermute | solution.py:239
  46.9 0.9 %near.1 = bf16[128,1536]{1,0:T(8,128)(2,1)S(1)} custom-call(bf16[192,1024]{1,0:T(8,128)(2,1)S(1)} %collective-permute-done.1.low_far_ref, bf16[192,1024]{1,0:T(8,128)(2,1)S(1)} %collective-permute-done.near_ref.low_near_ref, bf16[192,1024]{1,0:T(8,128)(2,1)S(1)} %collective-permute-done.3.x_ref, bf16[1024,1024]{1,0:T(8,128)(2,1)S(1)} %get-tuple-element.13.dense_ref, ...), custom_call_target="tpu_custom_call" | custom-call | flops 402653184 | bytes 4063232 | tf_op jit(solution)/shard_map/near/pallas_call | solution.py:218
  47.8 13.9 %all_to_all.10 = bf16[16,8,1536]{2,1,0:T(8,128)(2,1)S(1)} all-to-all(bf16[16,8,1536]{2,1,0:T(8,128)(2,1)S(1)} %bitcast.10), channel_id=1, replica_groups=mesh['seg'=32,'trait'=16] {'trait'}, dimensions={0} | all-to-all | bytes 786432 | tf_op jit(solution)/shard_map/all_to_all | solution.py:244
  61.7 1.0 %unpack.1 = bf16[192,1024]{1,0:T(8,128)(2,1)} custom-call(bf16[128,1536]{1,0:T(8,128)(2,1)S(1)} %bitcast.11), custom_call_target="tpu_custom_call" | custom-call | bytes 393216 | tf_op jit(solution)/shard_map/unpack/pallas_call | solution.py:218
  (10 shorter events, 0.0 us)
Async XLA Ops:
  2.0 20.1 %all-to-all-start = ((bf16[16,8,1536]{2,1,0:T(8,128)(2,1)}), bf16[16,8,1536]{2,1,0:T(8,128)(2,1)S(1)}, u32[]{:S(2)}, u32[]{:S(2)}) async-start(bf16[16,8,1536]{2,1,0:T(8,128)(2,1)} %bitcast.13), calls=%async_computation | async-start | bytes 786432 | tf_op jit(solution)/shard_map/all_to_all | solution.py:244
  12.2 2.2 %copy-start.2 = (bf16[1024,2048]{1,0:T(8,128)(2,1)S(1)}, bf16[1024,2048]{1,0:T(8,128)(2,1)}, u32[]{:S(2)}) copy-start(bf16[1024,2048]{1,0:T(8,128)(2,1)} %band_ref.1) | copy-start | bytes 12582916
  14.4 7.7 %copy-start.5 = (f32[192,192]{1,0:T(8,128)S(1)}, f32[192,192]{1,0:T(8,128)}, u32[]{:S(2)}) copy-start(f32[192,192]{1,0:T(8,128)} %p_ref.1) | copy-start | bytes 442372
  15.8 1.3 %copy-start = (bf16[1024,1024]{1,0:T(8,128)(2,1)}, bf16[1024,1024]{1,0:T(8,128)(2,1)S(1)}, u32[]{:S(2)}) copy-start(bf16[1024,1024]{1,0:T(8,128)(2,1)S(1)} %get-tuple-element.12.dense_ref) | copy-start | bytes 6291460
  17.2 1.3 %copy-start.3 = (bf16[1024,1024]{1,0:T(8,128)(2,1)}, bf16[1024,1024]{1,0:T(8,128)(2,1)S(1)}, u32[]{:S(2)}) copy-start(bf16[1024,1024]{1,0:T(8,128)(2,1)S(1)} %get-tuple-element.14.dense_ref) | copy-start | bytes 6291460
  22.1 4.3 %copy-start.1 = (bf16[1024,1024]{1,0:T(8,128)(2,1)S(1)}, bf16[1024,1024]{1,0:T(8,128)(2,1)}, u32[]{:S(2)}) copy-start(bf16[1024,1024]{1,0:T(8,128)(2,1)} %copy-done) | copy-start | bytes 6291460
  23.1 10.3 %collective-permute-start = (bf16[192,1024]{1,0:T(8,128)(2,1)S(1)}, bf16[192,1024]{1,0:T(8,128)(2,1)S(1)}, u32[]{:S(2)}, u32[]{:S(2)}) collective-permute-start(bf16[192,1024]{1,0:T(8,128)(2,1)S(1)} %lower_near.1), channel_id=1, source_target_pairs={{0,16},{1,24},{2,18},{3,26},{4,20},{5,28},{6,22},{7,30},{8,17},{9,... | collective-permute-start | bytes 1179656 | tf_op jit(solution)/shard_map/ppermute | solution.py:239
  25.1 11.5 %collective-permute-start.2 = (bf16[192,1024]{1,0:T(8,128)(2,1)S(1)}, bf16[192,1024]{1,0:T(8,128)(2,1)S(1)}, u32[]{:S(2)}, u32[]{:S(2)}) collective-permute-start(bf16[192,1024]{1,0:T(8,128)(2,1)S(1)} %mix.1.x_ref.own_ref), channel_id=1, source_target_pairs={{32,0},{48,16},{64,32},{80,48},{96,64},{112,80},{128,96},{144,112}... | collective-permute-start | bytes 1179656 | tf_op jit(solution)/shard_map/ppermute | solution.py:233
  26.8 14.7 %copy-start.4 = (bf16[1024,1024]{1,0:T(8,128)(2,1)S(1)}, bf16[1024,1024]{1,0:T(8,128)(2,1)}, u32[]{:S(2)}) copy-start(bf16[1024,1024]{1,0:T(8,128)(2,1)} %copy-done.3) | copy-start | bytes 6291460
  33.5 9.7 %collective-permute-start.1 = (bf16[192,1024]{1,0:T(8,128)(2,1)S(1)}, bf16[192,1024]{1,0:T(8,128)(2,1)S(1)}, u32[]{:S(2)}, u32[]{:S(2)}) collective-permute-start(bf16[192,1024]{1,0:T(8,128)(2,1)S(1)} %join.1), channel_id=1, source_target_pairs={{0,32},{16,48},{32,64},{48,80},{64,96},{80,112},{96,128},{112,144}... | collective-permute-start | bytes 1179656 | tf_op jit(solution)/shard_map/ppermute | solution.py:233
  36.6 10.4 %collective-permute-start.3 = (bf16[192,1024]{1,0:T(8,128)(2,1)S(1)}, bf16[192,1024]{1,0:T(8,128)(2,1)S(1)}, u32[]{:S(2)}, u32[]{:S(2)}) collective-permute-start(bf16[192,1024]{1,0:T(8,128)(2,1)S(1)} %choose.1), channel_id=1, source_target_pairs={{0,16},{1,24},{2,18},{3,26},{4,20},{5,28},{6,22},{7,30},{8,17},{9,... | collective-permute-start | bytes 1179656 | tf_op jit(solution)/shard_map/ppermute | solution.py:239

commit v6 on v4

--- a/solution.py
+++ b/solution.py
@@ -164,19 +164,23 @@
         o_ref[:, i:high] = total
 
 
-def far_kernel(x_ref, dense_ref, total_ref, o_ref):
+def far_kernel(low_ref, x_ref, dense_ref, total_ref, o_ref):
     m = x_ref.shape[1]
     depth = 256
     for i in range(0, m, depth):
         high = i + depth
-        o_ref[:, i:high] = total_ref[:, i:high] + contract(x_ref[:, :high], dense_ref[i:high, :high])
-
-
-def near_kernel(x_ref, low_near_ref, low_far_ref, dense_ref, total_ref, o_ref, wide):
-    m = x_ref.shape[1]
+        part = total_ref[:, i:high] + low_ref[:, i:high].astype(F32)
+        o_ref[:, i:high] = part + contract(x_ref[:, :high], dense_ref[i:high, :high])
+
+
+def near_kernel(x_ref, dense_ref, total_ref, o_ref):
+    o_ref[...] = total_ref[...] + contract(x_ref[...], dense_ref[...])
+
+
+def finish_kernel(total_ref, far_ref, o_ref, wide):
+    m = total_ref.shape[1]
     half = m // 2
-    wide[...] = total_ref[...] + low_near_ref[...].astype(F32) + low_far_ref[...].astype(F32)
-    wide[...] += contract(x_ref[...], dense_ref[...])
+    wide[...] = total_ref[...] + far_ref[...].astype(F32)
     for t in range(0, 16, 2):
         parts = []
         for u in (t, t + 1):
@@ -216,12 +220,6 @@
     return lax.ppermute(shard, ("seg", "trait"), pairs)
 
 
-def traded(shard):
-    length, places = lax.axis_size("seg"), lax.axis_size("trait")
-    pairs = [(s * places + p, (s ^ 1) * places + swapped(p)) for s in range(length) for p in range(places)]
-    return lax.ppermute(shard, ("seg", "trait"), pairs)
-
-
 def exchange(packed):
     rows, lanes = packed.shape
     moved = lax.all_to_all(packed.reshape(16, rows // 16, lanes), "trait", 0, 0, tiled=True)
@@ -252,21 +250,22 @@
         skew_kernel, "skew", (square, square, square), 16, band, flops=m * width
     )
     thin = struct((rows, m), BF16)
+    wide = struct((rows, m), F32)
     gathered, following = lax.optimization_barrier((exchange(packed), following))
     mixed = call(mix_kernel, "mix", thin, 16, gathered, precision, flops=4 * rows * rows * m)
-    far = passed_along(mixed, -2)
+    near = passed_along(mixed, -1)
     low_near = call(lower_near_kernel, "lower_near", thin, 16, mixed, following, flops=2 * rows * m * m)
+    later, low_near = lax.optimization_barrier((mixed, low_near))
     low_near = passed_along(low_near, 1)
+    far = passed_along(later, -2)
     low_far = call(lower_far_kernel, "lower_far", thin, 16, mixed, last, flops=rows * m * m)
     low_far = passed_along(low_far, 2)
-    odd = lax.axis_index("seg") % 2 == 1
-    near = traded(jnp.where(odd, mixed, far))
-    wide = struct((rows, m), F32)
     total = call(own_kernel, "own", wide, 16, mixed, within, flops=4 * rows * m * m)
-    total = call(far_kernel, "far", wide, 16, far, last, total, flops=rows * m * m)
+    total = call(near_kernel, "near", wide, 16, near, following, total, flops=2 * rows * m * m)
+    total = call(far_kernel, "far", wide, 16, low_near, far, last, total, flops=rows * m * m)
     packed = call(
-        near_kernel, "near", struct(packed_shape, BF16), 16, near, low_near, low_far, following, total,
-        flops=2 * rows * m * m, scratch=[pltpu.VMEM((rows, m), F32)],
+        finish_kernel, "finish", struct(packed_shape, BF16), 16, total, low_far,
+        scratch=[pltpu.VMEM((rows, m), F32)],
     )
     flat = call(
         unpack_kernel, "unpack", struct((rows, m), BF16), 8, exchange(packed),

time: 62.3 us -> 63.9 us (1.026)
  local copies, waits for them, and re-layouts: 4.83 us -> 6.41 us
  waiting for transfers between devices: 16.1 us -> 14.6 us
  starting transfers between devices: 19.1 us -> 20.4 us
    ppermute x3 -> x4, starting transfers between devices: 9.67 us -> 14.3 us  [passed_along(): return lax.ppermute(shard, ('seg', 'trait'), pairs)]
    ppermute x1 -> x0, starting transfers between devices: 3.26 us -> none  [traded(): return lax.ppermute(shard, ('seg', 'trait'), pairs)]
    unnamed x12 -> x14, local copies, waits for them, and re-layouts: 4.83 us -> 6.41 us
    ppermute x3 -> x4, waiting for transfers between devices: 11.6 us -> 10.2 us  [passed_along(): return lax.ppermute(shard, ('seg', 'trait'), pairs)]
    pallas_call x9 -> x10, Pallas kernels: 8.07 us -> 8.2 us  [call(): pl.pallas_call(kernel, out_shape=outs, in_specs=in_specs, out_specs=tuple...]
  transfers between devices with their start and end apart: 5 -> 5, of which waited for: 3 -> 3; matrix products, arithmetic and copies ran while one was open for 0% -> 0% of each run, Pallas kernels for 6% -> 7%
where the time goes in v6:
time: 63.9 us; the launch traced here: 63.5 us
  starting transfers between devices  20.4 us (32%)
  waiting for transfers between devices  14.6 us (23%)
  blocking collectives  13.7 us (21%)
  Pallas kernels  8.2 us (13%)
  local copies, waits for them, and re-layouts  6.41 us (10%)
    ppermute x4, starting transfers between devices, passed_along(): return lax.ppermute(shard, ('seg', 'trait'), pairs)  14.3 us
    all_to_all x1, blocking collectives, exchange(): lax.all_to_all(packed.reshape(16, rows // 16, lanes), 'trait', 0, 0, tile...  13.7 us
    ppermute x4, waiting for transfers between devices, passed_along(): return lax.ppermute(shard, ('seg', 'trait'), pairs)  10.2 us
    pallas_call x10, Pallas kernels, call(): pl.pallas_call(kernel, out_shape=outs, in_specs=in_specs, out_specs=tuple...  8.2 us
    unnamed x14, local copies, waits for them, and re-layouts  6.41 us
    all_to_all x1, starting transfers between devices, exchange(): lax.all_to_all(packed.reshape(16, rows // 16, lanes), 'trait', 0, 0, tile...  6.15 us
    all_to_all x1, waiting for transfers between devices, exchange(): lax.all_to_all(packed.reshape(16, rows // 16, lanes), 'trait', 0, 0, tile...  4.46 us
  transfers between devices with their start and end apart: 5, of which 3 were waited for; matrix products, arithmetic and copies ran while one was open for 0% of the time, Pallas kernels for 7%

profile of v6, /device:TPU:392, one launch (start us, length us, event | category | flops | bytes accessed | tf_op | source)
XLA Modules:
  0.0 63.5 jit_solution(12454427360875671349)
XLA Ops:
  0.0 2.0 %pack.1 = bf16[128,1536]{1,0:T(8,128)(2,1)} custom-call(bf16[192,1024]{1,0:T(8,128)(2,1)} %bitcast.14), custom_call_target="tpu_custom_call" | custom-call | bytes 393216 | tf_op jit(solution)/shard_map/pack/pallas_call | solution.py:201
  2.0 6.1 %all-to-all-start = ((bf16[16,8,1536]{2,1,0:T(8,128)(2,1)}), bf16[16,8,1536]{2,1,0:T(8,128)(2,1)S(1)}, u32[]{:S(2)}, u32[]{:S(2)}) async-start(bf16[16,8,1536]{2,1,0:T(8,128)(2,1)} %bitcast.13), calls=%async_computation | async-start | bytes 786432 | tf_op jit(solution)/shard_map/all_to_all | solution.py:225
  8.1 0.0 copy-start.3
  8.2 2.2 %copy-done.3 = bf16[1024,2048]{1,0:T(8,128)(2,1)S(1)} copy-done((bf16[1024,2048]{1,0:T(8,128)(2,1)S(1)}, bf16[1024,2048]{1,0:T(8,128)(2,1)}, u32[]{:S(2)}) %copy-start.3) | copy-done | bytes 4194328
  10.3 1.4 %skew.1 = (bf16[1024,1024]{1,0:T(8,128)(2,1)S(1)}, bf16[1024,1024]{1,0:T(8,128)(2,1)S(1)}, bf16[1024,1024]{1,0:T(8,128)(2,1)S(1)}) custom-call(bf16[1024,2048]{1,0:T(8,128)(2,1)S(1)} %copy-done.3), custom_call_target="tpu_custom_call" | custom-call | flops 2097152 | bytes 4194304 | tf_op jit(solution)/shard_map/skew/pallas_call | solution.py:201
  11.8 1.3 %copy-done = bf16[1024,1024]{1,0:T(8,128)(2,1)} copy-done((bf16[1024,1024]{1,0:T(8,128)(2,1)}, bf16[1024,1024]{1,0:T(8,128)(2,1)S(1)}, u32[]{:S(2)}) %copy-start) | copy-done | bytes 2097176
  13.1 1.3 %copy-done.4 = bf16[1024,1024]{1,0:T(8,128)(2,1)} copy-done((bf16[1024,1024]{1,0:T(8,128)(2,1)}, bf16[1024,1024]{1,0:T(8,128)(2,1)S(1)}, u32[]{:S(2)}) %copy-start.4) | copy-done | bytes 2097176
  14.4 4.5 %all-to-all-done = bf16[16,8,1536]{2,1,0:T(8,128)(2,1)S(1)} async-done(((bf16[16,8,1536]{2,1,0:T(8,128)(2,1)}), bf16[16,8,1536]{2,1,0:T(8,128)(2,1)S(1)}, u32[]{:S(2)}, u32[]{:S(2)}) %all-to-all-start) | async-done | bytes 393248 | tf_op jit(solution)/shard_map/all_to_all | solution.py:225
  18.9 0.4 mix.1.x_ref
  19.3 3.3 %collective-permute-start.2 = (bf16[192,1024]{1,0:T(8,128)(2,1)S(1)}, bf16[192,1024]{1,0:T(8,128)(2,1)S(1)}, u32[]{:S(2)}, u32[]{:S(2)}) collective-permute-start(bf16[192,1024]{1,0:T(8,128)(2,1)S(1)} %mix.1.x_ref), channel_id=1, source_target_pairs={{16,0},{17,8},{18,2},{19,10},{20,4},{21,12},{22,6},{23,14},{24,1},... | collective-permute-start | bytes 1179656 | tf_op jit(solution)/shard_map/ppermute | solution.py:220
  22.6 1.6 %copy-done.1 = bf16[1024,1024]{1,0:T(8,128)(2,1)S(1)} copy-done((bf16[1024,1024]{1,0:T(8,128)(2,1)S(1)}, bf16[1024,1024]{1,0:T(8,128)(2,1)}, u32[]{:S(2)}) %copy-start.1) | copy-done | bytes 2097176
  24.2 0.6 lower_near.1
  24.8 3.6 %collective-permute-start = (bf16[192,1024]{1,0:T(8,128)(2,1)S(1)}, bf16[192,1024]{1,0:T(8,128)(2,1)S(1)}, u32[]{:S(2)}, u32[]{:S(2)}) collective-permute-start(bf16[192,1024]{1,0:T(8,128)(2,1)S(1)} %lower_near.1), channel_id=1, source_target_pairs={{0,16},{1,24},{2,18},{3,26},{4,20},{5,28},{6,22},{7,30},{8,17},{9,... | collective-permute-start | bytes 1179656 | tf_op jit(solution)/shard_map/ppermute | solution.py:220
  28.4 5.3 %collective-permute-start.1 = (bf16[192,1024]{1,0:T(8,128)(2,1)S(1)}, bf16[192,1024]{1,0:T(8,128)(2,1)S(1)}, u32[]{:S(2)}, u32[]{:S(2)}) collective-permute-start(bf16[192,1024]{1,0:T(8,128)(2,1)S(1)} %mix.1.x_ref), channel_id=1, source_target_pairs={{32,0},{33,1},{34,2},{35,3},{36,4},{37,5},{38,6},{39,7},{40,8},{41... | collective-permute-start | bytes 1179656 | tf_op jit(solution)/shard_map/ppermute | solution.py:220
  33.7 0.4 lower_far.1
  34.2 2.1 %collective-permute-start.3 = (bf16[192,1024]{1,0:T(8,128)(2,1)S(1)}, bf16[192,1024]{1,0:T(8,128)(2,1)S(1)}, u32[]{:S(2)}, u32[]{:S(2)}) collective-permute-start(bf16[192,1024]{1,0:T(8,128)(2,1)S(1)} %lower_far.1), channel_id=1, source_target_pairs={{0,32},{1,33},{2,34},{3,35},{4,36},{5,37},{6,38},{7,39},{8,40},{9,... | collective-permute-start | bytes 1179656 | tf_op jit(solution)/shard_map/ppermute | solution.py:220
  36.2 0.8 %own.1.total_ref = f32[192,1024]{1,0:T(8,128)S(1)} custom-call(bf16[192,1024]{1,0:T(8,128)(2,1)S(1)} %mix.1.x_ref, bf16[1024,1024]{1,0:T(8,128)(2,1)S(1)} %copy-done.5), custom_call_target="tpu_custom_call" | custom-call | flops 805306368 | bytes 2490368 | tf_op jit(solution)/shard_map/own/pallas_call | solution.py:201
  37.1 0.8 %near.1.total_ref = f32[192,1024]{1,0:T(8,128)S(1)} custom-call(bf16[192,1024]{1,0:T(8,128)(2,1)S(1)} %collective-permute-done.2.x_ref, bf16[1024,1024]{1,0:T(8,128)(2,1)S(1)} %copy-done.2, f32[192,1024]{1,0:T(8,128)S(1)} %own.1.total_ref), custom_call_target="tpu_custom_call" | custom-call | flops 402653184 | bytes 3276800 | tf_op jit(solution)/shard_map/near/pallas_call | solution.py:201
  37.9 3.5 %collective-permute-done.1.x_ref = bf16[192,1024]{1,0:T(8,128)(2,1)S(1)} collective-permute-done((bf16[192,1024]{1,0:T(8,128)(2,1)S(1)}, bf16[192,1024]{1,0:T(8,128)(2,1)S(1)}, u32[]{:S(2)}, u32[]{:S(2)}) %collective-permute-start.1) | collective-permute-done | bytes 393248 | tf_op jit(solution)/shard_map/ppermute | solution.py:220
  41.4 0.6 far.1.total_ref
  42.0 6.7 %collective-permute-done.3.far_ref = bf16[192,1024]{1,0:T(8,128)(2,1)S(1)} collective-permute-done((bf16[192,1024]{1,0:T(8,128)(2,1)S(1)}, bf16[192,1024]{1,0:T(8,128)(2,1)S(1)}, u32[]{:S(2)}, u32[]{:S(2)}) %collective-permute-start.3) | collective-permute-done | bytes 393248 | tf_op jit(solution)/shard_map/ppermute | solution.py:220
  48.7 0.2 finish.1
  48.8 13.7 %all_to_all.10 = bf16[16,8,1536]{2,1,0:T(8,128)(2,1)S(1)} all-to-all(bf16[16,8,1536]{2,1,0:T(8,128)(2,1)S(1)} %bitcast.12), channel_id=1, replica_groups=mesh['seg'=32,'trait'=16] {'trait'}, dimensions={0} | all-to-all | bytes 786432 | tf_op jit(solution)/shard_map/all_to_all | solution.py:225
  62.5 1.0 %unpack.1 = bf16[192,1024]{1,0:T(8,128)(2,1)} custom-call(bf16[128,1536]{1,0:T(8,128)(2,1)S(1)} %bitcast.10), custom_call_target="tpu_custom_call" | custom-call | bytes 393216 | tf_op jit(solution)/shard_map/unpack/pallas_call | solution.py:201
  (11 shorter events, 0.0 us)
Async XLA Ops:
  2.0 16.9 %all-to-all-start = ((bf16[16,8,1536]{2,1,0:T(8,128)(2,1)}), bf16[16,8,1536]{2,1,0:T(8,128)(2,1)S(1)}, u32[]{:S(2)}, u32[]{:S(2)}) async-start(bf16[16,8,1536]{2,1,0:T(8,128)(2,1)} %bitcast.13), calls=%async_computation | async-start | bytes 786432 | tf_op jit(solution)/shard_map/all_to_all | solution.py:225
  8.1 2.2 %copy-start.3 = (bf16[1024,2048]{1,0:T(8,128)(2,1)S(1)}, bf16[1024,2048]{1,0:T(8,128)(2,1)}, u32[]{:S(2)}) copy-start(bf16[1024,2048]{1,0:T(8,128)(2,1)} %band_ref.1) | copy-start | bytes 12582916
  10.3 8.5 %copy-start.6 = (f32[192,192]{1,0:T(8,128)S(1)}, f32[192,192]{1,0:T(8,128)}, u32[]{:S(2)}) copy-start(f32[192,192]{1,0:T(8,128)} %p_ref.1) | copy-start | bytes 442372
  11.8 1.3 %copy-start = (bf16[1024,1024]{1,0:T(8,128)(2,1)}, bf16[1024,1024]{1,0:T(8,128)(2,1)S(1)}, u32[]{:S(2)}) copy-start(bf16[1024,1024]{1,0:T(8,128)(2,1)S(1)} %get-tuple-element.14.dense_ref) | copy-start | bytes 6291460
  13.1 1.3 %copy-start.4 = (bf16[1024,1024]{1,0:T(8,128)(2,1)}, bf16[1024,1024]{1,0:T(8,128)(2,1)S(1)}, u32[]{:S(2)}) copy-start(bf16[1024,1024]{1,0:T(8,128)(2,1)S(1)} %get-tuple-element.18.dense_ref) | copy-start | bytes 6291460
  19.3 17.7 %collective-permute-start.2 = (bf16[192,1024]{1,0:T(8,128)(2,1)S(1)}, bf16[192,1024]{1,0:T(8,128)(2,1)S(1)}, u32[]{:S(2)}, u32[]{:S(2)}) collective-permute-start(bf16[192,1024]{1,0:T(8,128)(2,1)S(1)} %mix.1.x_ref), channel_id=1, source_target_pairs={{16,0},{17,8},{18,2},{19,10},{20,4},{21,12},{22,6},{23,14},{24,1},... | collective-permute-start | bytes 1179656 | tf_op jit(solution)/shard_map/ppermute | solution.py:220
  22.6 1.6 %copy-start.1 = (bf16[1024,1024]{1,0:T(8,128)(2,1)S(1)}, bf16[1024,1024]{1,0:T(8,128)(2,1)}, u32[]{:S(2)}) copy-start(bf16[1024,1024]{1,0:T(8,128)(2,1)} %copy-done) | copy-start | bytes 6291460
  24.8 11.5 %copy-start.5 = (bf16[1024,1024]{1,0:T(8,128)(2,1)S(1)}, bf16[1024,1024]{1,0:T(8,128)(2,1)}, u32[]{:S(2)}) copy-start(bf16[1024,1024]{1,0:T(8,128)(2,1)} %copy-done.4) | copy-start | bytes 6291460
  24.8 13.1 %collective-permute-start = (bf16[192,1024]{1,0:T(8,128)(2,1)S(1)}, bf16[192,1024]{1,0:T(8,128)(2,1)S(1)}, u32[]{:S(2)}, u32[]{:S(2)}) collective-permute-start(bf16[192,1024]{1,0:T(8,128)(2,1)S(1)} %lower_near.1), channel_id=1, source_target_pairs={{0,16},{1,24},{2,18},{3,26},{4,20},{5,28},{6,22},{7,30},{8,17},{9,... | collective-permute-start | bytes 1179656 | tf_op jit(solution)/shard_map/ppermute | solution.py:220
  28.4 13.0 %collective-permute-start.1 = (bf16[192,1024]{1,0:T(8,128)(2,1)S(1)}, bf16[192,1024]{1,0:T(8,128)(2,1)S(1)}, u32[]{:S(2)}, u32[]{:S(2)}) collective-permute-start(bf16[192,1024]{1,0:T(8,128)(2,1)S(1)} %mix.1.x_ref), channel_id=1, source_target_pairs={{32,0},{33,1},{34,2},{35,3},{36,4},{37,5},{38,6},{39,7},{40,8},{41... | collective-permute-start | bytes 1179656 | tf_op jit(solution)/shard_map/ppermute | solution.py:220
  34.2 2.9 %copy-start.2 = (bf16[1024,1024]{1,0:T(8,128)(2,1)S(1)}, bf16[1024,1024]{1,0:T(8,128)(2,1)}, u32[]{:S(2)}) copy-start(bf16[1024,1024]{1,0:T(8,128)(2,1)} %copy-done) | copy-start | bytes 6291460
  34.2 14.5 %collective-permute-start.3 = (bf16[192,1024]{1,0:T(8,128)(2,1)S(1)}, bf16[192,1024]{1,0:T(8,128)(2,1)S(1)}, u32[]{:S(2)}, u32[]{:S(2)}) collective-permute-start(bf16[192,1024]{1,0:T(8,128)(2,1)S(1)} %lower_far.1), channel_id=1, source_target_pairs={{0,32},{1,33},{2,34},{3,35},{4,36},{5,37},{6,38},{7,39},{8,40},{9,... | collective-permute-start | bytes 1179656 | tf_op jit(solution)/shard_map/ppermute | solution.py:220

commit v7 on v6

--- a/solution.py
+++ b/solution.py
@@ -173,14 +173,15 @@
         o_ref[:, i:high] = part + contract(x_ref[:, :high], dense_ref[i:high, :high])
 
 
-def near_kernel(x_ref, dense_ref, total_ref, o_ref):
-    o_ref[...] = total_ref[...] + contract(x_ref[...], dense_ref[...])
-
-
-def finish_kernel(total_ref, far_ref, o_ref, wide):
+def near_kernel(cross_ref, pair_ref, dense_ref, total_ref, o_ref):
+    x = (cross_ref[...].astype(F32) + pair_ref[...].astype(F32)).astype(BF16)
+    o_ref[...] = total_ref[...] + contract(x, dense_ref[...])
+
+
+def finish_kernel(far_ref, pair_ref, total_ref, o_ref, wide):
     m = total_ref.shape[1]
     half = m // 2
-    wide[...] = total_ref[...] + far_ref[...].astype(F32)
+    wide[...] = total_ref[...] + far_ref[...].astype(F32) + pair_ref[...].astype(F32)
     for t in range(0, 16, 2):
         parts = []
         for u in (t, t + 1):
@@ -210,10 +211,10 @@
     )(*args)
 
 
-def passed_along(shard, by):
+def passed_along(shard, by, sources):
     length, places = lax.axis_size("seg"), lax.axis_size("trait")
     pairs = []
-    for s in range(length):
+    for s in sources:
         for p in range(places):
             if 0 <= s + by < length:
                 pairs.append((s * places + p, (s + by) * places + (swapped(p) if by % 2 else p)))
@@ -253,18 +254,23 @@
     wide = struct((rows, m), F32)
     gathered, following = lax.optimization_barrier((exchange(packed), following))
     mixed = call(mix_kernel, "mix", thin, 16, gathered, precision, flops=4 * rows * rows * m)
-    near = passed_along(mixed, -1)
+    every = range(lax.axis_size("seg"))
+    even, odd = every[::2], every[1::2]
+    cross = passed_along(mixed, -1, even)
     low_near = call(lower_near_kernel, "lower_near", thin, 16, mixed, following, flops=2 * rows * m * m)
-    later, low_near = lax.optimization_barrier((mixed, low_near))
-    low_near = passed_along(low_near, 1)
-    far = passed_along(later, -2)
-    low_far = call(lower_far_kernel, "lower_far", thin, 16, mixed, last, flops=rows * m * m)
-    low_far = passed_along(low_far, 2)
+    low_cross = passed_along(low_near, 1, odd)
+    later, after = lax.optimization_barrier((mixed, low_near))
+    far = passed_along(later, -2, every)
+    low_far = call(lower_far_kernel, "lower_far", thin, 16, later, last, flops=rows * m * m)
+    later, after, low_far = lax.optimization_barrier((later, after, low_far))
+    low_far = passed_along(low_far, 2, every)
+    pair = passed_along(later, -1, odd)
+    low_pair = passed_along(after, 1, even)
     total = call(own_kernel, "own", wide, 16, mixed, within, flops=4 * rows * m * m)
-    total = call(near_kernel, "near", wide, 16, near, following, total, flops=2 * rows * m * m)
-    total = call(far_kernel, "far", wide, 16, low_near, far, last, total, flops=rows * m * m)
+    total = call(far_kernel, "far", wide, 16, low_cross, far, last, total, flops=rows * m * m)
+    total = call(near_kernel, "near", wide, 16, cross, pair, following, total, flops=2 * rows * m * m)
     packed = call(
-        finish_kernel, "finish", struct(packed_shape, BF16), 16, total, low_far,
+        finish_kernel, "finish", struct(packed_shape, BF16), 16, low_far, low_pair, total,
         scratch=[pltpu.VMEM((rows, m), F32)],
     )
     flat = call(

time: 63.9 us -> 64.1 us (level)
  the two profiles are of different devices: /device:TPU:392 before, /device:TPU:384 now
where the time goes in v7:
time: 64.1 us; the launch traced here: 63.7 us
  starting transfers between devices  23.8 us (37%)
  blocking collectives  13.3 us (21%)
  waiting for transfers between devices  13.2 us (21%)
  Pallas kernels  8.29 us (13%)
  local copies, waits for them, and re-layouts  4.85 us (8%)
    ppermute x6, starting transfers between devices, passed_along(): return lax.ppermute(shard, ('seg', 'trait'), pairs)  16.8 us
    all_to_all x1, blocking collectives, exchange(): lax.all_to_all(packed.reshape(16, rows // 16, lanes), 'trait', 0, 0, tile...  13.3 us
    ppermute x6, waiting for transfers between devices, passed_along(): return lax.ppermute(shard, ('seg', 'trait'), pairs)  8.74 us
    pallas_call x10, Pallas kernels, call(): pl.pallas_call(kernel, out_shape=outs, in_specs=in_specs, out_specs=tuple...  8.29 us
    all_to_all x1, starting transfers between devices, exchange(): lax.all_to_all(packed.reshape(16, rows // 16, lanes), 'trait', 0, 0, tile...  7.05 us
    unnamed x12, local copies, waits for them, and re-layouts  4.85 us
    all_to_all x1, waiting for transfers between devices, exchange(): lax.all_to_all(packed.reshape(16, rows // 16, lanes), 'trait', 0, 0, tile...  4.44 us
  transfers between devices with their start and end apart: 7, of which 4 were waited for; matrix products, arithmetic and copies ran while one was open for 0% of the time, Pallas kernels for 6%

profile of v7, /device:TPU:384, one launch (start us, length us, event | category | flops | bytes accessed | tf_op | source)
XLA Modules:
  0.0 63.7 jit_solution(5539967130591308433)
XLA Ops:
  0.0 2.0 %pack.1 = bf16[128,1536]{1,0:T(8,128)(2,1)} custom-call(bf16[192,1024]{1,0:T(8,128)(2,1)} %bitcast.14), custom_call_target="tpu_custom_call" | custom-call | bytes 393216 | tf_op jit(solution)/shard_map/pack/pallas_call | solution.py:202
  2.0 7.0 %all-to-all-start = ((bf16[16,8,1536]{2,1,0:T(8,128)(2,1)}), bf16[16,8,1536]{2,1,0:T(8,128)(2,1)S(1)}, u32[]{:S(2)}, u32[]{:S(2)}) async-start(bf16[16,8,1536]{2,1,0:T(8,128)(2,1)} %bitcast.13), calls=%async_computation | async-start | bytes 786432 | tf_op jit(solution)/shard_map/all_to_all | solution.py:226
  9.1 2.2 %copy-done.2 = bf16[1024,2048]{1,0:T(8,128)(2,1)S(1)} copy-done((bf16[1024,2048]{1,0:T(8,128)(2,1)S(1)}, bf16[1024,2048]{1,0:T(8,128)(2,1)}, u32[]{:S(2)}) %copy-start.2) | copy-done | bytes 4194328
  11.2 1.4 %skew.1 = (bf16[1024,1024]{1,0:T(8,128)(2,1)S(1)}, bf16[1024,1024]{1,0:T(8,128)(2,1)S(1)}, bf16[1024,1024]{1,0:T(8,128)(2,1)S(1)}) custom-call(bf16[1024,2048]{1,0:T(8,128)(2,1)S(1)} %copy-done.2), custom_call_target="tpu_custom_call" | custom-call | flops 2097152 | bytes 4194304 | tf_op jit(solution)/shard_map/skew/pallas_call | solution.py:202
  12.7 1.3 %copy-done = bf16[1024,1024]{1,0:T(8,128)(2,1)} copy-done((bf16[1024,1024]{1,0:T(8,128)(2,1)}, bf16[1024,1024]{1,0:T(8,128)(2,1)S(1)}, u32[]{:S(2)}) %copy-start) | copy-done | bytes 2097176
  14.0 1.3 %copy-done.3 = bf16[1024,1024]{1,0:T(8,128)(2,1)} copy-done((bf16[1024,1024]{1,0:T(8,128)(2,1)}, bf16[1024,1024]{1,0:T(8,128)(2,1)S(1)}, u32[]{:S(2)}) %copy-start.3) | copy-done | bytes 2097176
  15.3 4.4 %all-to-all-done = bf16[16,8,1536]{2,1,0:T(8,128)(2,1)S(1)} async-done(((bf16[16,8,1536]{2,1,0:T(8,128)(2,1)}), bf16[16,8,1536]{2,1,0:T(8,128)(2,1)S(1)}, u32[]{:S(2)}, u32[]{:S(2)}) %all-to-all-start) | async-done | bytes 393248 | tf_op jit(solution)/shard_map/all_to_all | solution.py:226
  19.8 0.4 mix.1.x_ref
  20.2 0.6 lower_near.1
  20.8 4.3 %collective-permute-start.5 = (bf16[192,1024]{1,0:T(8,128)(2,1)S(1)}, bf16[192,1024]{1,0:T(8,128)(2,1)S(1)}, u32[]{:S(2)}, u32[]{:S(2)}) collective-permute-start(bf16[192,1024]{1,0:T(8,128)(2,1)S(1)} %mix.1.x_ref), channel_id=1, source_target_pairs={{32,0},{33,1},{34,2},{35,3},{36,4},{37,5},{38,6},{39,7},{40,8},{41... | collective-permute-start | bytes 1179656 | tf_op jit(solution)/shard_map/ppermute | solution.py:221
  25.1 1.3 %collective-permute-start.4 = (bf16[192,1024]{1,0:T(8,128)(2,1)S(1)}, bf16[192,1024]{1,0:T(8,128)(2,1)S(1)}, u32[]{:S(2)}, u32[]{:S(2)}) collective-permute-start(bf16[192,1024]{1,0:T(8,128)(2,1)S(1)} %lower_near.1), channel_id=1, source_target_pairs={{16,32},{17,40},{18,34},{19,42},{20,36},{21,44},{22,38},{23,46},{2... | collective-permute-start | bytes 1179656 | tf_op jit(solution)/shard_map/ppermute | solution.py:221
  26.4 0.4 lower_far.1
  26.8 1.3 %collective-permute-start.3 = (bf16[192,1024]{1,0:T(8,128)(2,1)S(1)}, bf16[192,1024]{1,0:T(8,128)(2,1)S(1)}, u32[]{:S(2)}, u32[]{:S(2)}) collective-permute-start(bf16[192,1024]{1,0:T(8,128)(2,1)S(1)} %mix.1.x_ref), channel_id=1, source_target_pairs={{16,0},{17,8},{18,2},{19,10},{20,4},{21,12},{22,6},{23,14},{24,1},... | collective-permute-start | bytes 1179656 | tf_op jit(solution)/shard_map/ppermute | solution.py:221
  28.1 6.7 %collective-permute-start.2 = (bf16[192,1024]{1,0:T(8,128)(2,1)S(1)}, bf16[192,1024]{1,0:T(8,128)(2,1)S(1)}, u32[]{:S(2)}, u32[]{:S(2)}) collective-permute-start(bf16[192,1024]{1,0:T(8,128)(2,1)S(1)} %mix.1.x_ref), channel_id=1, source_target_pairs={{32,16},{33,24},{34,18},{35,26},{36,20},{37,28},{38,22},{39,30},{4... | collective-permute-start | bytes 1179656 | tf_op jit(solution)/shard_map/ppermute | solution.py:221
  34.8 1.9 %collective-permute-start = (bf16[192,1024]{1,0:T(8,128)(2,1)S(1)}, bf16[192,1024]{1,0:T(8,128)(2,1)S(1)}, u32[]{:S(2)}, u32[]{:S(2)}) collective-permute-start(bf16[192,1024]{1,0:T(8,128)(2,1)S(1)} %lower_far.1), channel_id=1, source_target_pairs={{0,32},{1,33},{2,34},{3,35},{4,36},{5,37},{6,38},{7,39},{8,40},{9,... | collective-permute-start | bytes 1179656 | tf_op jit(solution)/shard_map/ppermute | solution.py:221
  36.8 1.3 %collective-permute-start.1 = (bf16[192,1024]{1,0:T(8,128)(2,1)S(1)}, bf16[192,1024]{1,0:T(8,128)(2,1)S(1)}, u32[]{:S(2)}, u32[]{:S(2)}) collective-permute-start(bf16[192,1024]{1,0:T(8,128)(2,1)S(1)} %lower_near.1), channel_id=1, source_target_pairs={{0,16},{1,24},{2,18},{3,26},{4,20},{5,28},{6,22},{7,30},{8,17},{9,... | collective-permute-start | bytes 1179656 | tf_op jit(solution)/shard_map/ppermute | solution.py:221
  38.1 0.8 %own.1.total_ref = f32[192,1024]{1,0:T(8,128)S(1)} custom-call(bf16[192,1024]{1,0:T(8,128)(2,1)S(1)} %mix.1.x_ref, bf16[1024,1024]{1,0:T(8,128)(2,1)S(1)} %copy-done.4), custom_call_target="tpu_custom_call" | custom-call | flops 805306368 | bytes 2490368 | tf_op jit(solution)/shard_map/own/pallas_call | solution.py:202
  38.9 2.2 %collective-permute-done.4.low_ref = bf16[192,1024]{1,0:T(8,128)(2,1)S(1)} collective-permute-done((bf16[192,1024]{1,0:T(8,128)(2,1)S(1)}, bf16[192,1024]{1,0:T(8,128)(2,1)S(1)}, u32[]{:S(2)}, u32[]{:S(2)}) %collective-permute-start.4) | collective-permute-done | bytes 393248 | tf_op jit(solution)/shard_map/ppermute | solution.py:221
  41.1 0.6 far.1.total_ref
  41.7 2.0 %collective-permute-done.2.cross_ref = bf16[192,1024]{1,0:T(8,128)(2,1)S(1)} collective-permute-done((bf16[192,1024]{1,0:T(8,128)(2,1)S(1)}, bf16[192,1024]{1,0:T(8,128)(2,1)S(1)}, u32[]{:S(2)}, u32[]{:S(2)}) %collective-permute-start.2) | collective-permute-done | bytes 393248 | tf_op jit(solution)/shard_map/ppermute | solution.py:221
  43.7 0.8 %near.1.total_ref = f32[192,1024]{1,0:T(8,128)S(1)} custom-call(bf16[192,1024]{1,0:T(8,128)(2,1)S(1)} %collective-permute-done.2.cross_ref, bf16[192,1024]{1,0:T(8,128)(2,1)S(1)} %collective-permute-done.3.pair_ref, bf16[1024,1024]{1,0:T(8,128)(2,1)S(1)} %get-tuple-element.17.dense_ref, f32[192,1024]{1,0:T(8,128)S(1)} %far.1.total_ref), custom_call_target="tpu_custom_call" | custom-call | flops 402653184 | bytes 3670016 | tf_op jit(solution)/shard_map/near/pallas_call | solution.py:202
  44.6 4.5 %collective-permute-done.far_ref = bf16[192,1024]{1,0:T(8,128)(2,1)S(1)} collective-permute-done((bf16[192,1024]{1,0:T(8,128)(2,1)S(1)}, bf16[192,1024]{1,0:T(8,128)(2,1)S(1)}, u32[]{:S(2)}, u32[]{:S(2)}) %collective-permute-start) | collective-permute-done | bytes 393248 | tf_op jit(solution)/shard_map/ppermute | solution.py:221
  49.3 13.3 %all_to_all.10 = bf16[16,8,1536]{2,1,0:T(8,128)(2,1)S(1)} all-to-all(bf16[16,8,1536]{2,1,0:T(8,128)(2,1)S(1)} %bitcast.12), channel_id=1, replica_groups=mesh['seg'=32,'trait'=16] {'trait'}, dimensions={0} | all-to-all | bytes 786432 | tf_op jit(solution)/shard_map/all_to_all | solution.py:226
  62.7 1.0 %unpack.1 = bf16[192,1024]{1,0:T(8,128)(2,1)} custom-call(bf16[128,1536]{1,0:T(8,128)(2,1)S(1)} %bitcast.10), custom_call_target="tpu_custom_call" | custom-call | bytes 393216 | tf_op jit(solution)/shard_map/unpack/pallas_call | solution.py:202
  (13 shorter events, 0.3 us)
Async XLA Ops:
  2.0 17.8 %all-to-all-start = ((bf16[16,8,1536]{2,1,0:T(8,128)(2,1)}), bf16[16,8,1536]{2,1,0:T(8,128)(2,1)S(1)}, u32[]{:S(2)}, u32[]{:S(2)}) async-start(bf16[16,8,1536]{2,1,0:T(8,128)(2,1)} %bitcast.13), calls=%async_computation | async-start | bytes 786432 | tf_op jit(solution)/shard_map/all_to_all | solution.py:226
  9.0 2.2 %copy-start.2 = (bf16[1024,2048]{1,0:T(8,128)(2,1)S(1)}, bf16[1024,2048]{1,0:T(8,128)(2,1)}, u32[]{:S(2)}) copy-start(bf16[1024,2048]{1,0:T(8,128)(2,1)} %band_ref.1) | copy-start | bytes 12582916
  11.2 8.5 %copy-start.5 = (f32[192,192]{1,0:T(8,128)S(1)}, f32[192,192]{1,0:T(8,128)}, u32[]{:S(2)}) copy-start(f32[192,192]{1,0:T(8,128)} %p_ref.1) | copy-start | bytes 442372
  12.7 1.3 %copy-start = (bf16[1024,1024]{1,0:T(8,128)(2,1)}, bf16[1024,1024]{1,0:T(8,128)(2,1)S(1)}, u32[]{:S(2)}) copy-start(bf16[1024,1024]{1,0:T(8,128)(2,1)S(1)} %get-tuple-element.20.dense_ref) | copy-start | bytes 6291460
  14.0 1.3 %copy-start.3 = (bf16[1024,1024]{1,0:T(8,128)(2,1)}, bf16[1024,1024]{1,0:T(8,128)(2,1)S(1)}, u32[]{:S(2)}) copy-start(bf16[1024,1024]{1,0:T(8,128)(2,1)S(1)} %get-tuple-element.24.dense_ref) | copy-start | bytes 6291460
  19.8 6.6 %copy-start.1 = (bf16[1024,1024]{1,0:T(8,128)(2,1)S(1)}, bf16[1024,1024]{1,0:T(8,128)(2,1)}, u32[]{:S(2)}) copy-start(bf16[1024,1024]{1,0:T(8,128)(2,1)} %copy-done) | copy-start | bytes 6291460
  20.8 17.3 %copy-start.4 = (bf16[1024,1024]{1,0:T(8,128)(2,1)S(1)}, bf16[1024,1024]{1,0:T(8,128)(2,1)}, u32[]{:S(2)}) copy-start(bf16[1024,1024]{1,0:T(8,128)(2,1)} %copy-done.3) | copy-start | bytes 6291460
  20.8 16.0 %collective-permute-start.5 = (bf16[192,1024]{1,0:T(8,128)(2,1)S(1)}, bf16[192,1024]{1,0:T(8,128)(2,1)S(1)}, u32[]{:S(2)}, u32[]{:S(2)}) collective-permute-start(bf16[192,1024]{1,0:T(8,128)(2,1)S(1)} %mix.1.x_ref), channel_id=1, source_target_pairs={{32,0},{33,1},{34,2},{35,3},{36,4},{37,5},{38,6},{39,7},{40,8},{41... | collective-permute-start | bytes 1179656 | tf_op jit(solution)/shard_map/ppermute | solution.py:221
  25.1 16.1 %collective-permute-start.4 = (bf16[192,1024]{1,0:T(8,128)(2,1)S(1)}, bf16[192,1024]{1,0:T(8,128)(2,1)S(1)}, u32[]{:S(2)}, u32[]{:S(2)}) collective-permute-start(bf16[192,1024]{1,0:T(8,128)(2,1)S(1)} %lower_near.1), channel_id=1, source_target_pairs={{16,32},{17,40},{18,34},{19,42},{20,36},{21,44},{22,38},{23,46},{2... | collective-permute-start | bytes 1179656 | tf_op jit(solution)/shard_map/ppermute | solution.py:221
  26.8 14.9 %collective-permute-start.3 = (bf16[192,1024]{1,0:T(8,128)(2,1)S(1)}, bf16[192,1024]{1,0:T(8,128)(2,1)S(1)}, u32[]{:S(2)}, u32[]{:S(2)}) collective-permute-start(bf16[192,1024]{1,0:T(8,128)(2,1)S(1)} %mix.1.x_ref), channel_id=1, source_target_pairs={{16,0},{17,8},{18,2},{19,10},{20,4},{21,12},{22,6},{23,14},{24,1},... | collective-permute-start | bytes 1179656 | tf_op jit(solution)/shard_map/ppermute | solution.py:221
  28.1 15.6 %collective-permute-start.2 = (bf16[192,1024]{1,0:T(8,128)(2,1)S(1)}, bf16[192,1024]{1,0:T(8,128)(2,1)S(1)}, u32[]{:S(2)}, u32[]{:S(2)}) collective-permute-start(bf16[192,1024]{1,0:T(8,128)(2,1)S(1)} %mix.1.x_ref), channel_id=1, source_target_pairs={{32,16},{33,24},{34,18},{35,26},{36,20},{37,28},{38,22},{39,30},{4... | collective-permute-start | bytes 1179656 | tf_op jit(solution)/shard_map/ppermute | solution.py:221
  34.8 14.2 %collective-permute-start = (bf16[192,1024]{1,0:T(8,128)(2,1)S(1)}, bf16[192,1024]{1,0:T(8,128)(2,1)S(1)}, u32[]{:S(2)}, u32[]{:S(2)}) collective-permute-start(bf16[192,1024]{1,0:T(8,128)(2,1)S(1)} %lower_far.1), channel_id=1, source_target_pairs={{0,32},{1,33},{2,34},{3,35},{4,36},{5,37},{6,38},{7,39},{8,40},{9,... | collective-permute-start | bytes 1179656 | tf_op jit(solution)/shard_map/ppermute | solution.py:221
  36.8 12.3 %collective-permute-start.1 = (bf16[192,1024]{1,0:T(8,128)(2,1)S(1)}, bf16[192,1024]{1,0:T(8,128)(2,1)S(1)}, u32[]{:S(2)}, u32[]{:S(2)}) collective-permute-start(bf16[192,1024]{1,0:T(8,128)(2,1)S(1)} %lower_near.1), channel_id=1, source_target_pairs={{0,16},{1,24},{2,18},{3,26},{4,20},{5,28},{6,22},{7,30},{8,17},{9,... | collective-permute-start | bytes 1179656 | tf_op jit(solution)/shard_map/ppermute | solution.py:221

commit v8 on v4

--- a/solution.py
+++ b/solution.py
@@ -67,23 +67,36 @@
         copy.wait()
 
 
-def unpack_kernel(x_ref, o_ref, wide):
+def unpack_kernel(x_ref, o_ref, wide, held, sems):
     m = o_ref.shape[1]
     blocks = m // LANES
+    chunks = sems.shape[0]
     chains = chain_places()
-    for k in range(wide.shape[0]):
+
+    def widen(k):
         for p in range(0, 16, 2):
             pair = x_ref[8 * p : 8 * p + 16, k * LANES : (k + 1) * LANES].astype(F32)
             for h in range(2):
                 wide[k, pl.ds(pl.multiple_of(8 * chains[p + h], 8), 8), :] = pair[8 * h : 8 * h + 8]
-    for k in range(blocks):
-        lanes = pl.ds(k * LANES, LANES)
-        for j in range(8):
-            o_ref[16 * j : 16 * j + 16, lanes] = wide[k, pl.ds(j, 16, stride=8), :].astype(BF16)
-        half, place = divmod(k, blocks // 2)
-        for j in range(4):
-            tail = wide[blocks + place, pl.ds(j + 4 * half, 16, stride=8), :]
-            o_ref[128 + 16 * j : 144 + 16 * j, lanes] = tail.astype(BF16)
+
+    for k in range(blocks, wide.shape[0]):
+        widen(k)
+    copies = []
+    for q in range(chunks):
+        for k in range(q * blocks // chunks, (q + 1) * blocks // chunks):
+            widen(k)
+            lanes = pl.ds(k * LANES, LANES)
+            for j in range(8):
+                held[16 * j : 16 * j + 16, lanes] = wide[k, pl.ds(j, 16, stride=8), :].astype(BF16)
+            half, place = divmod(k, blocks // 2)
+            for j in range(4):
+                tail = wide[blocks + place, pl.ds(j + 4 * half, 16, stride=8), :]
+                held[128 + 16 * j : 144 + 16 * j, lanes] = tail.astype(BF16)
+        lanes = pl.ds(q * (m // chunks), m // chunks)
+        copies.append(pltpu.make_async_copy(held.at[:, lanes], o_ref.at[:, lanes], sems.at[q]))
+        copies[-1].start()
+    for copy in copies:
+        copy.wait()
 
 
 def mix_kernel(x_ref, p_ref, o_ref):
@@ -172,19 +185,37 @@
         o_ref[:, i:high] = total_ref[:, i:high] + contract(x_ref[:, :high], dense_ref[i:high, :high])
 
 
+def on_odd_segment():
+    return lax.rem(lax.axis_index("seg"), 2) == 1
+
+
+def choose_kernel(own_ref, far_ref, o_ref):
+    @pl.when(on_odd_segment())
+    def _():
+        o_ref[...] = own_ref[...]
+
+    @pl.when(jnp.logical_not(on_odd_segment()))
+    def _():
+        o_ref[...] = far_ref[...]
+
+
 def near_kernel(x_ref, low_near_ref, low_far_ref, dense_ref, total_ref, o_ref, wide):
     m = x_ref.shape[1]
     half = m // 2
-    wide[...] = total_ref[...] + low_near_ref[...].astype(F32) + low_far_ref[...].astype(F32)
-    wide[...] += contract(x_ref[...], dense_ref[...])
-    for t in range(0, 16, 2):
-        parts = []
-        for u in (t, t + 1):
-            head = wide[12 * u : 12 * u + 8, :]
-            left = wide[12 * u + 8 : 12 * u + 12, :half]
-            right = wide[12 * u + 8 : 12 * u + 12, half:]
-            parts.append(jnp.concatenate([head, jnp.concatenate([left, right], 0)], 1))
-        o_ref[8 * t : 8 * t + 16, :] = jnp.concatenate(parts, 0).astype(BF16)
+    depth = 256
+    for i in range(0, m, depth):
+        lanes = pl.ds(i, depth)
+        total = total_ref[:, lanes] + low_near_ref[:, lanes].astype(F32) + low_far_ref[:, lanes].astype(F32)
+        wide[:, lanes] = total + contract(x_ref[...], dense_ref[lanes, :])
+        for t in range(0, 16, 2):
+            parts = [wide[12 * u : 12 * u + 8, lanes] for u in (t, t + 1)]
+            o_ref[8 * t : 8 * t + 16, lanes] = jnp.concatenate(parts, 0).astype(BF16)
+        if i >= half:
+            for t in range(0, 16, 2):
+                parts = [
+                    wide[12 * u + 8 : 12 * u + 12, pl.ds(k, depth)] for u in (t, t + 1) for k in (i - half, i)
+                ]
+                o_ref[8 * t : 8 * t + 16, pl.ds(half + i, depth)] = jnp.concatenate(parts, 0).astype(BF16)
 
 
 def call(kernel, name, outs, mib, *args, scratch=(), flops=0, far_off=(), far_out=False):
@@ -259,8 +290,7 @@
     low_near = passed_along(low_near, 1)
     low_far = call(lower_far_kernel, "lower_far", thin, 16, mixed, last, flops=rows * m * m)
     low_far = passed_along(low_far, 2)
-    odd = lax.axis_index("seg") % 2 == 1
-    near = traded(jnp.where(odd, mixed, far))
+    near = traded(call(choose_kernel, "choose", thin, 8, mixed, far))
     wide = struct((rows, m), F32)
     total = call(own_kernel, "own", wide, 16, mixed, within, flops=4 * rows * m * m)
     total = call(far_kernel, "far", wide, 16, far, last, total, flops=rows * m * m)
@@ -269,8 +299,12 @@
         flops=2 * rows * m * m, scratch=[pltpu.VMEM((rows, m), F32)],
     )
     flat = call(
-        unpack_kernel, "unpack", struct((rows, m), BF16), 8, exchange(packed),
-        scratch=[pltpu.VMEM((packed_shape[1] // LANES, packed_shape[0], LANES), F32)],
+        unpack_kernel, "unpack", thin, 8, exchange(packed), far_out=True,
+        scratch=[
+            pltpu.VMEM((packed_shape[1] // LANES, packed_shape[0], LANES), F32),
+            pltpu.VMEM((rows, m), BF16),
+            pltpu.SemaphoreType.DMA((4,)),
+        ],
     )
     return flat.reshape(traits, chains, m).transpose(1, 0, 2)
 

time: 62.3 us -> 62.4 us (level)
    pallas_call x9 -> x10, Pallas kernels: 8.07 us -> 8.04 us  [call(): pl.pallas_call(kernel, out_shape=outs, in_specs=in_specs, out_specs=tuple...]
where the time goes in v8:
time: 62.4 us; the launch traced here: 62 us
  starting transfers between devices  19.2 us (31%)
  waiting for transfers between devices  16.1 us (26%)
  blocking collectives  13.7 us (22%)
  Pallas kernels  8.04 us (13%)
  local copies, waits for them, and re-layouts  4.83 us (8%)
    all_to_all x1, blocking collectives, exchange(): lax.all_to_all(packed.reshape(16, rows // 16, lanes), 'trait', 0, 0, tile...  13.7 us
    ppermute x3, waiting for transfers between devices, passed_along(): return lax.ppermute(shard, ('seg', 'trait'), pairs)  11.6 us
    ppermute x3, starting transfers between devices, passed_along(): return lax.ppermute(shard, ('seg', 'trait'), pairs)  9.83 us
    pallas_call x10, Pallas kernels, call(): pl.pallas_call(kernel, out_shape=outs, in_specs=in_specs, out_specs=tuple...  8.04 us
    all_to_all x1, starting transfers between devices, exchange(): lax.all_to_all(packed.reshape(16, rows // 16, lanes), 'trait', 0, 0, tile...  6.15 us
    unnamed x12, local copies, waits for them, and re-layouts  4.83 us
    all_to_all x1, waiting for transfers between devices, exchange(): lax.all_to_all(packed.reshape(16, rows // 16, lanes), 'trait', 0, 0, tile...  4.45 us
    ppermute x1, starting transfers between devices, traded(): return lax.ppermute(shard, ('seg', 'trait'), pairs)  3.25 us
  transfers between devices with their start and end apart: 5, of which 3 were waited for; matrix products, arithmetic and copies ran while one was open for 0% of the time, Pallas kernels for 6%

profile of v8, /device:TPU:392, one launch (start us, length us, event | category | flops | bytes accessed | tf_op | source)
XLA Modules:
  0.0 62.0 jit_solution(9689033558703379869)
XLA Ops:
  0.0 2.0 %pack.1 = bf16[128,1536]{1,0:T(8,128)(2,1)} custom-call(bf16[192,1024]{1,0:T(8,128)(2,1)} %bitcast.14), custom_call_target="tpu_custom_call" | custom-call | bytes 393216 | tf_op jit(solution)/shard_map/pack/pallas_call | solution.py:228
  2.0 6.1 %all-to-all-start = ((bf16[16,8,1536]{2,1,0:T(8,128)(2,1)}), bf16[16,8,1536]{2,1,0:T(8,128)(2,1)S(1)}, u32[]{:S(2)}, u32[]{:S(2)}) async-start(bf16[16,8,1536]{2,1,0:T(8,128)(2,1)} %bitcast.13), calls=%async_computation | async-start | bytes 786432 | tf_op jit(solution)/shard_map/all_to_all | solution.py:258
  8.1 0.0 copy-start.2
  8.2 2.2 %copy-done.2 = bf16[1024,2048]{1,0:T(8,128)(2,1)S(1)} copy-done((bf16[1024,2048]{1,0:T(8,128)(2,1)S(1)}, bf16[1024,2048]{1,0:T(8,128)(2,1)}, u32[]{:S(2)}) %copy-start.2) | copy-done | bytes 4194328
  10.3 1.4 %skew.1 = (bf16[1024,1024]{1,0:T(8,128)(2,1)S(1)}, bf16[1024,1024]{1,0:T(8,128)(2,1)S(1)}, bf16[1024,1024]{1,0:T(8,128)(2,1)S(1)}) custom-call(bf16[1024,2048]{1,0:T(8,128)(2,1)S(1)} %copy-done.2), custom_call_target="tpu_custom_call" | custom-call | flops 2097152 | bytes 4194304 | tf_op jit(solution)/shard_map/skew/pallas_call | solution.py:228
  11.8 1.3 %copy-done = bf16[1024,1024]{1,0:T(8,128)(2,1)} copy-done((bf16[1024,1024]{1,0:T(8,128)(2,1)}, bf16[1024,1024]{1,0:T(8,128)(2,1)S(1)}, u32[]{:S(2)}) %copy-start) | copy-done | bytes 2097176
  13.1 1.3 %copy-done.3 = bf16[1024,1024]{1,0:T(8,128)(2,1)} copy-done((bf16[1024,1024]{1,0:T(8,128)(2,1)}, bf16[1024,1024]{1,0:T(8,128)(2,1)S(1)}, u32[]{:S(2)}) %copy-start.3) | copy-done | bytes 2097176
  14.4 4.5 %all-to-all-done = bf16[16,8,1536]{2,1,0:T(8,128)(2,1)S(1)} async-done(((bf16[16,8,1536]{2,1,0:T(8,128)(2,1)}), bf16[16,8,1536]{2,1,0:T(8,128)(2,1)S(1)}, u32[]{:S(2)}, u32[]{:S(2)}) %all-to-all-start) | async-done | bytes 393248 | tf_op jit(solution)/shard_map/all_to_all | solution.py:258
  18.9 0.4 mix.1.own_ref.x_ref
  19.3 4.3 %collective-permute-start = (bf16[192,1024]{1,0:T(8,128)(2,1)S(1)}, bf16[192,1024]{1,0:T(8,128)(2,1)S(1)}, u32[]{:S(2)}, u32[]{:S(2)}) collective-permute-start(bf16[192,1024]{1,0:T(8,128)(2,1)S(1)} %mix.1.own_ref.x_ref), channel_id=1, source_target_pairs={{32,0},{33,1},{34,2},{35,3},{36,4},{37,5},{38,6},{39,7},{40,8},{41... | collective-permute-start | bytes 1179656 | tf_op jit(solution)/shard_map/ppermute | solution.py:247
  23.6 0.6 lower_near.1
  24.2 2.6 %collective-permute-start.2 = (bf16[192,1024]{1,0:T(8,128)(2,1)S(1)}, bf16[192,1024]{1,0:T(8,128)(2,1)S(1)}, u32[]{:S(2)}, u32[]{:S(2)}) collective-permute-start(bf16[192,1024]{1,0:T(8,128)(2,1)S(1)} %lower_near.1), channel_id=1, source_target_pairs={{0,16},{1,24},{2,18},{3,26},{4,20},{5,28},{6,22},{7,30},{8,17},{9,... | collective-permute-start | bytes 1179656 | tf_op jit(solution)/shard_map/ppermute | solution.py:247
  26.8 0.4 lower_far.1
  27.3 2.9 %collective-permute-start.3 = (bf16[192,1024]{1,0:T(8,128)(2,1)S(1)}, bf16[192,1024]{1,0:T(8,128)(2,1)S(1)}, u32[]{:S(2)}, u32[]{:S(2)}) collective-permute-start(bf16[192,1024]{1,0:T(8,128)(2,1)S(1)} %lower_far.1), channel_id=1, source_target_pairs={{0,32},{1,33},{2,34},{3,35},{4,36},{5,37},{6,38},{7,39},{8,40},{9,... | collective-permute-start | bytes 1179656 | tf_op jit(solution)/shard_map/ppermute | solution.py:247
  30.2 1.6 %collective-permute-done.far_ref.x_ref = bf16[192,1024]{1,0:T(8,128)(2,1)S(1)} collective-permute-done((bf16[192,1024]{1,0:T(8,128)(2,1)S(1)}, bf16[192,1024]{1,0:T(8,128)(2,1)S(1)}, u32[]{:S(2)}, u32[]{:S(2)}) %collective-permute-start) | collective-permute-done | bytes 393248 | tf_op jit(solution)/shard_map/ppermute | solution.py:247
  31.8 3.3 %collective-permute-start.1 = (bf16[192,1024]{1,0:T(8,128)(2,1)S(1)}, bf16[192,1024]{1,0:T(8,128)(2,1)S(1)}, u32[]{:S(2)}, u32[]{:S(2)}) collective-permute-start(bf16[192,1024]{1,0:T(8,128)(2,1)S(1)} %choose.1), channel_id=1, source_target_pairs={{0,16},{1,24},{2,18},{3,26},{4,20},{5,28},{6,22},{7,30},{8,17},{9,... | collective-permute-start | bytes 1179656 | tf_op jit(solution)/shard_map/ppermute | solution.py:253
  35.1 0.8 %own.1.total_ref = f32[192,1024]{1,0:T(8,128)S(1)} custom-call(bf16[192,1024]{1,0:T(8,128)(2,1)S(1)} %mix.1.own_ref.x_ref, bf16[1024,1024]{1,0:T(8,128)(2,1)S(1)} %copy-done.4), custom_call_target="tpu_custom_call" | custom-call | flops 805306368 | bytes 2490368 | tf_op jit(solution)/shard_map/own/pallas_call | solution.py:228
  35.9 0.6 far.1.total_ref
  36.5 0.0 collective-permute-done.2.low_near_ref
  36.5 10.0 %collective-permute-done.3.low_far_ref = bf16[192,1024]{1,0:T(8,128)(2,1)S(1)} collective-permute-done((bf16[192,1024]{1,0:T(8,128)(2,1)S(1)}, bf16[192,1024]{1,0:T(8,128)(2,1)S(1)}, u32[]{:S(2)}, u32[]{:S(2)}) %collective-permute-start.3) | collective-permute-done | bytes 393248 | tf_op jit(solution)/shard_map/ppermute | solution.py:247
  46.5 0.0 collective-permute-done.1.x_ref
  46.5 0.9 %near.1 = bf16[128,1536]{1,0:T(8,128)(2,1)S(1)} custom-call(bf16[192,1024]{1,0:T(8,128)(2,1)S(1)} %collective-permute-done.1.x_ref, bf16[192,1024]{1,0:T(8,128)(2,1)S(1)} %collective-permute-done.2.low_near_ref, bf16[192,1024]{1,0:T(8,128)(2,1)S(1)} %collective-permute-done.3.low_far_ref, bf16[1024,1024]{1,0:T(8,128)(2,1)S(1)} %get-tuple-element.12.dense_ref, ...), custom_call_target="tpu_custom_call" | custom-call | flops 402653184 | bytes 4063232 | tf_op jit(solution)/shard_map/near/pallas_call | solution.py:228
  47.4 13.7 %all_to_all.10 = bf16[16,8,1536]{2,1,0:T(8,128)(2,1)S(1)} all-to-all(bf16[16,8,1536]{2,1,0:T(8,128)(2,1)S(1)} %bitcast.10), channel_id=1, replica_groups=mesh['seg'=32,'trait'=16] {'trait'}, dimensions={0} | all-to-all | bytes 786432 | tf_op jit(solution)/shard_map/all_to_all | solution.py:258
  61.1 0.9 %unpack.1 = bf16[192,1024]{1,0:T(8,128)(2,1)} custom-call(bf16[128,1536]{1,0:T(8,128)(2,1)S(1)} %bitcast.11), custom_call_target="tpu_custom_call" | custom-call | bytes 393216 | tf_op jit(solution)/shard_map/unpack/pallas_call | solution.py:228
  (9 shorter events, 0.0 us)
Async XLA Ops:
  2.0 16.9 %all-to-all-start = ((bf16[16,8,1536]{2,1,0:T(8,128)(2,1)}), bf16[16,8,1536]{2,1,0:T(8,128)(2,1)S(1)}, u32[]{:S(2)}, u32[]{:S(2)}) async-start(bf16[16,8,1536]{2,1,0:T(8,128)(2,1)} %bitcast.13), calls=%async_computation | async-start | bytes 786432 | tf_op jit(solution)/shard_map/all_to_all | solution.py:258
  8.1 2.2 %copy-start.2 = (bf16[1024,2048]{1,0:T(8,128)(2,1)S(1)}, bf16[1024,2048]{1,0:T(8,128)(2,1)}, u32[]{:S(2)}) copy-start(bf16[1024,2048]{1,0:T(8,128)(2,1)} %band_ref.1) | copy-start | bytes 12582916
  10.3 8.5 %copy-start.5 = (f32[192,192]{1,0:T(8,128)S(1)}, f32[192,192]{1,0:T(8,128)}, u32[]{:S(2)}) copy-start(f32[192,192]{1,0:T(8,128)} %p_ref.1) | copy-start | bytes 442372
  11.8 1.3 %copy-start = (bf16[1024,1024]{1,0:T(8,128)(2,1)}, bf16[1024,1024]{1,0:T(8,128)(2,1)S(1)}, u32[]{:S(2)}) copy-start(bf16[1024,1024]{1,0:T(8,128)(2,1)S(1)} %get-tuple-element.13.dense_ref) | copy-start | bytes 6291460
  13.1 1.3 %copy-start.3 = (bf16[1024,1024]{1,0:T(8,128)(2,1)}, bf16[1024,1024]{1,0:T(8,128)(2,1)S(1)}, u32[]{:S(2)}) copy-start(bf16[1024,1024]{1,0:T(8,128)(2,1)S(1)} %get-tuple-element.14.dense_ref) | copy-start | bytes 6291460
  18.9 7.9 %copy-start.1 = (bf16[1024,1024]{1,0:T(8,128)(2,1)S(1)}, bf16[1024,1024]{1,0:T(8,128)(2,1)}, u32[]{:S(2)}) copy-start(bf16[1024,1024]{1,0:T(8,128)(2,1)} %copy-done) | copy-start | bytes 6291460
  19.3 12.5 %collective-permute-start = (bf16[192,1024]{1,0:T(8,128)(2,1)S(1)}, bf16[192,1024]{1,0:T(8,128)(2,1)S(1)}, u32[]{:S(2)}, u32[]{:S(2)}) collective-permute-start(bf16[192,1024]{1,0:T(8,128)(2,1)S(1)} %mix.1.own_ref.x_ref), channel_id=1, source_target_pairs={{32,0},{33,1},{34,2},{35,3},{36,4},{37,5},{38,6},{39,7},{40,8},{41... | collective-permute-start | bytes 1179656 | tf_op jit(solution)/shard_map/ppermute | solution.py:247
  24.1 11.0 %copy-start.4 = (bf16[1024,1024]{1,0:T(8,128)(2,1)S(1)}, bf16[1024,1024]{1,0:T(8,128)(2,1)}, u32[]{:S(2)}) copy-start(bf16[1024,1024]{1,0:T(8,128)(2,1)} %copy-done.3) | copy-start | bytes 6291460
  24.2 12.4 %collective-permute-start.2 = (bf16[192,1024]{1,0:T(8,128)(2,1)S(1)}, bf16[192,1024]{1,0:T(8,128)(2,1)S(1)}, u32[]{:S(2)}, u32[]{:S(2)}) collective-permute-start(bf16[192,1024]{1,0:T(8,128)(2,1)S(1)} %lower_near.1), channel_id=1, source_target_pairs={{0,16},{1,24},{2,18},{3,26},{4,20},{5,28},{6,22},{7,30},{8,17},{9,... | collective-permute-start | bytes 1179656 | tf_op jit(solution)/shard_map/ppermute | solution.py:247
  27.3 19.3 %collective-permute-start.3 = (bf16[192,1024]{1,0:T(8,128)(2,1)S(1)}, bf16[192,1024]{1,0:T(8,128)(2,1)S(1)}, u32[]{:S(2)}, u32[]{:S(2)}) collective-permute-start(bf16[192,1024]{1,0:T(8,128)(2,1)S(1)} %lower_far.1), channel_id=1, source_target_pairs={{0,32},{1,33},{2,34},{3,35},{4,36},{5,37},{6,38},{7,39},{8,40},{9,... | collective-permute-start | bytes 1179656 | tf_op jit(solution)/shard_map/ppermute | solution.py:247
  31.8 14.7 %collective-permute-start.1 = (bf16[192,1024]{1,0:T(8,128)(2,1)S(1)}, bf16[192,1024]{1,0:T(8,128)(2,1)S(1)}, u32[]{:S(2)}, u32[]{:S(2)}) collective-permute-start(bf16[192,1024]{1,0:T(8,128)(2,1)S(1)} %choose.1), channel_id=1, source_target_pairs={{0,16},{1,24},{2,18},{3,26},{4,20},{5,28},{6,22},{7,30},{8,17},{9,... | collective-permute-start | bytes 1179656 | tf_op jit(solution)/shard_map/ppermute | solution.py:253

commit v9 on v8

--- a/solution.py
+++ b/solution.py
@@ -32,37 +32,33 @@
     rows, m = x_ref.shape
     blocks = m // LANES
     chunks = in_sems.shape[0]
-    part = m // chunks
+    part = rows // chunks
     chains = chain_places()
     copies = []
     for q in range(chunks):
-        lanes = pl.ds(q * part, part)
-        copies.append(pltpu.make_async_copy(x_ref.at[:, lanes], near.at[:, lanes], in_sems.at[q]))
+        some = pl.ds(q * part, part)
+        copies.append(pltpu.make_async_copy(x_ref.at[some], near.at[some], in_sems.at[q]))
         copies[-1].start()
-    out = []
-
-    def send(first, size):
-        lanes = pl.ds(first, size)
-        out.append(pltpu.make_async_copy(packed.at[:, lanes], o_ref.at[:, lanes], out_sems.at[len(out)]))
-        out[-1].start()
-
     for q in range(chunks):
         copies[q].wait()
-        for k in range(q * blocks // chunks, (q + 1) * blocks // chunks):
-            wide[k] = near[:, k * LANES : (k + 1) * LANES].astype(F32)
-            for p in range(0, 16, 2):
-                parts = [wide[k, pl.ds(d, 8, stride=16), :] for d in chains[p : p + 2]]
-                packed[8 * p : 8 * p + 16, k * LANES : (k + 1) * LANES] = jnp.concatenate(parts, 0).astype(BF16)
-        send(q * part, part)
-    for p in range(0, 16, 2):
+        for k in range(blocks):
+            some = pl.ds(q * part, part)
+            wide[k, some, :] = near[some, k * LANES : (k + 1) * LANES].astype(F32)
+    out = []
+    for q, p in enumerate(range(0, 16, 2)):
+        some = pl.ds(8 * p, 16)
+        for k in range(blocks):
+            parts = [wide[k, pl.ds(d, 8, stride=16), :] for d in chains[p : p + 2]]
+            packed[some, k * LANES : (k + 1) * LANES] = jnp.concatenate(parts, 0).astype(BF16)
         for k in range(blocks // 2):
             parts = [
                 wide[k + h, pl.ds(128 + d, 4, stride=16), :]
                 for d in chains[p : p + 2]
                 for h in (0, blocks // 2)
             ]
-            packed[8 * p : 8 * p + 16, m + k * LANES : m + (k + 1) * LANES] = jnp.concatenate(parts, 0).astype(BF16)
-    send(m, m // 2)
+            packed[some, m + k * LANES : m + (k + 1) * LANES] = jnp.concatenate(parts, 0).astype(BF16)
+        out.append(pltpu.make_async_copy(packed.at[some], o_ref.at[some], out_sems.at[q]))
+        out[-1].start()
     for copy in out:
         copy.wait()
 
@@ -99,9 +95,7 @@
         copy.wait()
 
 
-def mix_kernel(x_ref, p_ref, o_ref):
-    m = o_ref.shape[1]
-    half = m // 2
+def weights_kernel(p_ref, upper_ref, lower_ref):
     blank = jnp.zeros((4, p_ref.shape[1]), F32)
     heads, lows, highs = [], [], []
     for t in range(16):
@@ -110,14 +104,22 @@
         lows += [tail, blank]
         highs += [blank, tail]
     head = jnp.concatenate(heads, 0)
-    for first, tails in ((0, lows), (half, highs)):
+    for k, tails in enumerate((lows, highs)):
         weights = jnp.concatenate([head, jnp.concatenate(tails, 0)], 0).T
         upper = weights.astype(BF16)
-        lower = (weights - upper.astype(F32)).astype(BF16)
+        upper_ref[k] = upper
+        lower_ref[k] = (weights - upper.astype(F32)).astype(BF16)
+
+
+def mix_kernel(x_ref, upper_ref, lower_ref, o_ref):
+    m = o_ref.shape[1]
+    half = m // 2
+    for k, first in enumerate((0, half)):
         values = jnp.concatenate([x_ref[:, first : first + half], x_ref[:, m:]], 0)
-        total = jnp.dot(upper, values, preferred_element_type=F32)
-        total += jnp.dot(lower, values, preferred_element_type=F32)
+        total = jnp.dot(upper_ref[k], values, preferred_element_type=F32)
+        total += jnp.dot(lower_ref[k], values, preferred_element_type=F32)
         o_ref[:, first : first + half] = total.astype(BF16)
+
 
 def lower_near_kernel(x_ref, dense_ref, o_ref):
     o_ref[...] = jnp.dot(x_ref[...], dense_ref[...], preferred_element_type=F32).astype(BF16)
@@ -275,7 +277,7 @@
             pltpu.VMEM((m // LANES, rows, LANES), F32),
             pltpu.VMEM(packed_shape, BF16),
             pltpu.SemaphoreType.DMA((4,)),
-            pltpu.SemaphoreType.DMA((5,)),
+            pltpu.SemaphoreType.DMA((8,)),
         ],
     )
     square = struct((m, m), BF16)
@@ -283,8 +285,10 @@
         skew_kernel, "skew", (square, square, square), 16, band, flops=m * width
     )
     thin = struct((rows, m), BF16)
+    matrices = struct((2, rows, 256), BF16)
+    upper, lower = call(weights_kernel, "weights", (matrices, matrices), 16, precision, flops=rows * rows)
     gathered, following = lax.optimization_barrier((exchange(packed), following))
-    mixed = call(mix_kernel, "mix", thin, 16, gathered, precision, flops=4 * rows * rows * m)
+    mixed = call(mix_kernel, "mix", thin, 16, gathered, upper, lower, flops=4 * rows * rows * m)
     far = passed_along(mixed, -2)
     low_near = call(lower_near_kernel, "lower_near", thin, 16, mixed, following, flops=2 * rows * m * m)
     low_near = passed_along(low_near, 1)

time: 62.4 us -> 63.5 us (1.018)
  waiting for transfers between devices: 16.1 us -> 15 us
  blocking collectives: 13.7 us -> 14.7 us
  local copies, waits for them, and re-layouts: 4.83 us -> 5.74 us
    all_to_all x1, waiting for transfers between devices: 4.45 us -> 3.36 us  [exchange(): lax.all_to_all(packed.reshape(16, rows // 16, lanes), 'trait', 0, 0, tile...]
    all_to_all x1, blocking collectives: 13.7 us -> 14.7 us  [exchange(): lax.all_to_all(packed.reshape(16, rows // 16, lanes), 'trait', 0, 0, tile...]
    unnamed x12, local copies, waits for them, and re-layouts: 4.83 us -> 5.74 us
    pallas_call x10 -> x11, Pallas kernels: 8.04 us -> 8.22 us  [call(): pl.pallas_call(kernel, out_shape=outs, in_specs=in_specs, out_specs=tuple...]
where the time goes in v9:
time: 63.5 us; the launch traced here: 63.1 us
  starting transfers between devices  19.2 us (30%)
  waiting for transfers between devices  15 us (24%)
  blocking collectives  14.7 us (23%)
  Pallas kernels  8.22 us (13%)
  local copies, waits for them, and re-layouts  5.74 us (9%)
    all_to_all x1, blocking collectives, exchange(): lax.all_to_all(packed.reshape(16, rows // 16, lanes), 'trait', 0, 0, tile...  14.7 us
    ppermute x3, waiting for transfers between devices, passed_along(): return lax.ppermute(shard, ('seg', 'trait'), pairs)  11.6 us
    ppermute x3, starting transfers between devices, passed_along(): return lax.ppermute(shard, ('seg', 'trait'), pairs)  9.82 us
    pallas_call x11, Pallas kernels, call(): pl.pallas_call(kernel, out_shape=outs, in_specs=in_specs, out_specs=tuple...  8.22 us
    all_to_all x1, starting transfers between devices, exchange(): lax.all_to_all(packed.reshape(16, rows // 16, lanes), 'trait', 0, 0, tile...  6.15 us
    unnamed x12, local copies, waits for them, and re-layouts  5.74 us
    all_to_all x1, waiting for transfers between devices, exchange(): lax.all_to_all(packed.reshape(16, rows // 16, lanes), 'trait', 0, 0, tile...  3.36 us
    ppermute x1, starting transfers between devices, traded(): return lax.ppermute(shard, ('seg', 'trait'), pairs)  3.26 us
  transfers between devices with their start and end apart: 5, of which 3 were waited for; matrix products, arithmetic and copies ran while one was open for 0% of the time, Pallas kernels for 6%

profile of v9, /device:TPU:392, one launch (start us, length us, event | category | flops | bytes accessed | tf_op | source)
XLA Modules:
  0.0 63.1 jit_solution(1653553060999866400)
XLA Ops:
  0.0 2.0 %pack.1 = bf16[128,1536]{1,0:T(8,128)(2,1)} custom-call(bf16[192,1024]{1,0:T(8,128)(2,1)} %bitcast.14), custom_call_target="tpu_custom_call" | custom-call | bytes 393216 | tf_op jit(solution)/shard_map/pack/pallas_call | solution.py:230
  2.1 6.1 %all-to-all-start = ((bf16[16,8,1536]{2,1,0:T(8,128)(2,1)}), bf16[16,8,1536]{2,1,0:T(8,128)(2,1)S(1)}, u32[]{:S(2)}, u32[]{:S(2)}) async-start(bf16[16,8,1536]{2,1,0:T(8,128)(2,1)} %bitcast.13), calls=%async_computation | async-start | bytes 786432 | tf_op jit(solution)/shard_map/all_to_all | solution.py:260
  8.2 0.0 copy-start.5
  8.2 0.9 %copy-done.5 = f32[192,192]{1,0:T(8,128)S(1)} copy-done((f32[192,192]{1,0:T(8,128)S(1)}, f32[192,192]{1,0:T(8,128)}, u32[]{:S(2)}) %copy-start.5) | copy-done | bytes 147480
  9.1 0.2 weights.1
  9.3 2.2 %copy-done.2 = bf16[1024,2048]{1,0:T(8,128)(2,1)S(1)} copy-done((bf16[1024,2048]{1,0:T(8,128)(2,1)S(1)}, bf16[1024,2048]{1,0:T(8,128)(2,1)}, u32[]{:S(2)}) %copy-start.2) | copy-done | bytes 4194328
  11.5 1.4 %skew.1 = (bf16[1024,1024]{1,0:T(8,128)(2,1)S(1)}, bf16[1024,1024]{1,0:T(8,128)(2,1)S(1)}, bf16[1024,1024]{1,0:T(8,128)(2,1)S(1)}) custom-call(bf16[1024,2048]{1,0:T(8,128)(2,1)S(1)} %copy-done.2), custom_call_target="tpu_custom_call" | custom-call | flops 2097152 | bytes 4194304 | tf_op jit(solution)/shard_map/skew/pallas_call | solution.py:230
  12.9 1.3 %copy-done = bf16[1024,1024]{1,0:T(8,128)(2,1)} copy-done((bf16[1024,1024]{1,0:T(8,128)(2,1)}, bf16[1024,1024]{1,0:T(8,128)(2,1)S(1)}, u32[]{:S(2)}) %copy-start) | copy-done | bytes 2097176
  14.3 1.3 %copy-done.3 = bf16[1024,1024]{1,0:T(8,128)(2,1)} copy-done((bf16[1024,1024]{1,0:T(8,128)(2,1)}, bf16[1024,1024]{1,0:T(8,128)(2,1)S(1)}, u32[]{:S(2)}) %copy-start.3) | copy-done | bytes 2097176
  15.6 3.4 %all-to-all-done = bf16[16,8,1536]{2,1,0:T(8,128)(2,1)S(1)} async-done(((bf16[16,8,1536]{2,1,0:T(8,128)(2,1)}), bf16[16,8,1536]{2,1,0:T(8,128)(2,1)S(1)}, u32[]{:S(2)}, u32[]{:S(2)}) %all-to-all-start) | async-done | bytes 393248 | tf_op jit(solution)/shard_map/all_to_all | solution.py:260
  18.9 0.4 mix.1.own_ref.x_ref
  19.3 4.3 %collective-permute-start = (bf16[192,1024]{1,0:T(8,128)(2,1)S(1)}, bf16[192,1024]{1,0:T(8,128)(2,1)S(1)}, u32[]{:S(2)}, u32[]{:S(2)}) collective-permute-start(bf16[192,1024]{1,0:T(8,128)(2,1)S(1)} %mix.1.own_ref.x_ref), channel_id=1, source_target_pairs={{32,0},{33,1},{34,2},{35,3},{36,4},{37,5},{38,6},{39,7},{40,8},{41... | collective-permute-start | bytes 1179656 | tf_op jit(solution)/shard_map/ppermute | solution.py:249
  23.6 0.6 lower_near.1
  24.2 2.6 %collective-permute-start.2 = (bf16[192,1024]{1,0:T(8,128)(2,1)S(1)}, bf16[192,1024]{1,0:T(8,128)(2,1)S(1)}, u32[]{:S(2)}, u32[]{:S(2)}) collective-permute-start(bf16[192,1024]{1,0:T(8,128)(2,1)S(1)} %lower_near.1), channel_id=1, source_target_pairs={{0,16},{1,24},{2,18},{3,26},{4,20},{5,28},{6,22},{7,30},{8,17},{9,... | collective-permute-start | bytes 1179656 | tf_op jit(solution)/shard_map/ppermute | solution.py:249
  26.8 0.4 lower_far.1
  27.3 2.9 %collective-permute-start.3 = (bf16[192,1024]{1,0:T(8,128)(2,1)S(1)}, bf16[192,1024]{1,0:T(8,128)(2,1)S(1)}, u32[]{:S(2)}, u32[]{:S(2)}) collective-permute-start(bf16[192,1024]{1,0:T(8,128)(2,1)S(1)} %lower_far.1), channel_id=1, source_target_pairs={{0,32},{1,33},{2,34},{3,35},{4,36},{5,37},{6,38},{7,39},{8,40},{9,... | collective-permute-start | bytes 1179656 | tf_op jit(solution)/shard_map/ppermute | solution.py:249
  30.2 1.6 %collective-permute-done.far_ref.x_ref = bf16[192,1024]{1,0:T(8,128)(2,1)S(1)} collective-permute-done((bf16[192,1024]{1,0:T(8,128)(2,1)S(1)}, bf16[192,1024]{1,0:T(8,128)(2,1)S(1)}, u32[]{:S(2)}, u32[]{:S(2)}) %collective-permute-start) | collective-permute-done | bytes 393248 | tf_op jit(solution)/shard_map/ppermute | solution.py:249
  31.9 3.3 %collective-permute-start.1 = (bf16[192,1024]{1,0:T(8,128)(2,1)S(1)}, bf16[192,1024]{1,0:T(8,128)(2,1)S(1)}, u32[]{:S(2)}, u32[]{:S(2)}) collective-permute-start(bf16[192,1024]{1,0:T(8,128)(2,1)S(1)} %choose.1), channel_id=1, source_target_pairs={{0,16},{1,24},{2,18},{3,26},{4,20},{5,28},{6,22},{7,30},{8,17},{9,... | collective-permute-start | bytes 1179656 | tf_op jit(solution)/shard_map/ppermute | solution.py:255
  35.1 0.8 %own.1.total_ref = f32[192,1024]{1,0:T(8,128)S(1)} custom-call(bf16[192,1024]{1,0:T(8,128)(2,1)S(1)} %mix.1.own_ref.x_ref, bf16[1024,1024]{1,0:T(8,128)(2,1)S(1)} %copy-done.4), custom_call_target="tpu_custom_call" | custom-call | flops 805306368 | bytes 2490368 | tf_op jit(solution)/shard_map/own/pallas_call | solution.py:230
  35.9 0.6 far.1.total_ref
  36.5 10.0 %collective-permute-done.3.low_far_ref = bf16[192,1024]{1,0:T(8,128)(2,1)S(1)} collective-permute-done((bf16[192,1024]{1,0:T(8,128)(2,1)S(1)}, bf16[192,1024]{1,0:T(8,128)(2,1)S(1)}, u32[]{:S(2)}, u32[]{:S(2)}) %collective-permute-start.3) | collective-permute-done | bytes 393248 | tf_op jit(solution)/shard_map/ppermute | solution.py:249
  46.5 0.9 %near.1 = bf16[128,1536]{1,0:T(8,128)(2,1)S(1)} custom-call(bf16[192,1024]{1,0:T(8,128)(2,1)S(1)} %collective-permute-done.1.x_ref, bf16[192,1024]{1,0:T(8,128)(2,1)S(1)} %collective-permute-done.2.low_near_ref, bf16[192,1024]{1,0:T(8,128)(2,1)S(1)} %collective-permute-done.3.low_far_ref, bf16[1024,1024]{1,0:T(8,128)(2,1)S(1)} %get-tuple-element.16.dense_ref, ...), custom_call_target="tpu_custom_call" | custom-call | flops 402653184 | bytes 4063232 | tf_op jit(solution)/shard_map/near/pallas_call | solution.py:230
  47.4 14.7 %all_to_all.10 = bf16[16,8,1536]{2,1,0:T(8,128)(2,1)S(1)} all-to-all(bf16[16,8,1536]{2,1,0:T(8,128)(2,1)S(1)} %bitcast.10), channel_id=1, replica_groups=mesh['seg'=32,'trait'=16] {'trait'}, dimensions={0} | all-to-all | bytes 786432 | tf_op jit(solution)/shard_map/all_to_all | solution.py:260
  62.2 0.9 %unpack.1 = bf16[192,1024]{1,0:T(8,128)(2,1)} custom-call(bf16[128,1536]{1,0:T(8,128)(2,1)S(1)} %bitcast.11), custom_call_target="tpu_custom_call" | custom-call | bytes 393216 | tf_op jit(solution)/shard_map/unpack/pallas_call | solution.py:230
  (10 shorter events, 0.0 us)
Async XLA Ops:
  2.1 16.9 %all-to-all-start = ((bf16[16,8,1536]{2,1,0:T(8,128)(2,1)}), bf16[16,8,1536]{2,1,0:T(8,128)(2,1)S(1)}, u32[]{:S(2)}, u32[]{:S(2)}) async-start(bf16[16,8,1536]{2,1,0:T(8,128)(2,1)} %bitcast.13), calls=%async_computation | async-start | bytes 786432 | tf_op jit(solution)/shard_map/all_to_all | solution.py:260
  8.2 0.9 %copy-start.5 = (f32[192,192]{1,0:T(8,128)S(1)}, f32[192,192]{1,0:T(8,128)}, u32[]{:S(2)}) copy-start(f32[192,192]{1,0:T(8,128)} %p_ref.1) | copy-start | bytes 442372
  9.3 2.2 %copy-start.2 = (bf16[1024,2048]{1,0:T(8,128)(2,1)S(1)}, bf16[1024,2048]{1,0:T(8,128)(2,1)}, u32[]{:S(2)}) copy-start(bf16[1024,2048]{1,0:T(8,128)(2,1)} %band_ref.1) | copy-start | bytes 12582916
  12.9 1.3 %copy-start = (bf16[1024,1024]{1,0:T(8,128)(2,1)}, bf16[1024,1024]{1,0:T(8,128)(2,1)S(1)}, u32[]{:S(2)}) copy-start(bf16[1024,1024]{1,0:T(8,128)(2,1)S(1)} %get-tuple-element.17.dense_ref) | copy-start | bytes 6291460
  14.3 1.3 %copy-start.3 = (bf16[1024,1024]{1,0:T(8,128)(2,1)}, bf16[1024,1024]{1,0:T(8,128)(2,1)S(1)}, u32[]{:S(2)}) copy-start(bf16[1024,1024]{1,0:T(8,128)(2,1)S(1)} %get-tuple-element.18.dense_ref) | copy-start | bytes 6291460
  18.9 7.9 %copy-start.1 = (bf16[1024,1024]{1,0:T(8,128)(2,1)S(1)}, bf16[1024,1024]{1,0:T(8,128)(2,1)}, u32[]{:S(2)}) copy-start(bf16[1024,1024]{1,0:T(8,128)(2,1)} %copy-done) | copy-start | bytes 6291460
  19.3 12.5 %collective-permute-start = (bf16[192,1024]{1,0:T(8,128)(2,1)S(1)}, bf16[192,1024]{1,0:T(8,128)(2,1)S(1)}, u32[]{:S(2)}, u32[]{:S(2)}) collective-permute-start(bf16[192,1024]{1,0:T(8,128)(2,1)S(1)} %mix.1.own_ref.x_ref), channel_id=1, source_target_pairs={{32,0},{33,1},{34,2},{35,3},{36,4},{37,5},{38,6},{39,7},{40,8},{41... | collective-permute-start | bytes 1179656 | tf_op jit(solution)/shard_map/ppermute | solution.py:249
  24.2 11.0 %copy-start.4 = (bf16[1024,1024]{1,0:T(8,128)(2,1)S(1)}, bf16[1024,1024]{1,0:T(8,128)(2,1)}, u32[]{:S(2)}) copy-start(bf16[1024,1024]{1,0:T(8,128)(2,1)} %copy-done.3) | copy-start | bytes 6291460
  24.2 12.3 %collective-permute-start.2 = (bf16[192,1024]{1,0:T(8,128)(2,1)S(1)}, bf16[192,1024]{1,0:T(8,128)(2,1)S(1)}, u32[]{:S(2)}, u32[]{:S(2)}) collective-permute-start(bf16[192,1024]{1,0:T(8,128)(2,1)S(1)} %lower_near.1), channel_id=1, source_target_pairs={{0,16},{1,24},{2,18},{3,26},{4,20},{5,28},{6,22},{7,30},{8,17},{9,... | collective-permute-start | bytes 1179656 | tf_op jit(solution)/shard_map/ppermute | solution.py:249
  27.3 19.3 %collective-permute-start.3 = (bf16[192,1024]{1,0:T(8,128)(2,1)S(1)}, bf16[192,1024]{1,0:T(8,128)(2,1)S(1)}, u32[]{:S(2)}, u32[]{:S(2)}) collective-permute-start(bf16[192,1024]{1,0:T(8,128)(2,1)S(1)} %lower_far.1), channel_id=1, source_target_pairs={{0,32},{1,33},{2,34},{3,35},{4,36},{5,37},{6,38},{7,39},{8,40},{9,... | collective-permute-start | bytes 1179656 | tf_op jit(solution)/shard_map/ppermute | solution.py:249
  31.9 14.7 %collective-permute-start.1 = (bf16[192,1024]{1,0:T(8,128)(2,1)S(1)}, bf16[192,1024]{1,0:T(8,128)(2,1)S(1)}, u32[]{:S(2)}, u32[]{:S(2)}) collective-permute-start(bf16[192,1024]{1,0:T(8,128)(2,1)S(1)} %choose.1), channel_id=1, source_target_pairs={{0,16},{1,24},{2,18},{3,26},{4,20},{5,28},{6,22},{7,30},{8,17},{9,... | collective-permute-start | bytes 1179656 | tf_op jit(solution)/shard_map/ppermute | solution.py:255

commit v10 on v8

--- a/solution.py
+++ b/solution.py
@@ -157,9 +157,25 @@
         put(first + width + LANES, zero.astype(BF16))
 
 
-def skew_kernel(band_ref, *dense_refs):
-    for first in range(0, band_ref.shape[0], LANES):
-        skew_rows(band_ref, dense_refs, first)
+def skew_kernel(band_ref, within_ref, following_ref, last_ref, band, within, last, in_sems, out_sems):
+    chunks = in_sems.shape[0]
+    part = band_ref.shape[0] // chunks
+    fetches = []
+    for q in range(chunks):
+        some = pl.ds(q * part, part)
+        fetches.append(pltpu.make_async_copy(band_ref.at[some], band.at[some], in_sems.at[q]))
+        fetches[-1].start()
+    sends = []
+    for q in range(chunks):
+        fetches[q].wait()
+        some = pl.ds(q * part, part)
+        for first in range(q * part, (q + 1) * part, LANES):
+            skew_rows(band, (within, following_ref, last), first)
+        for k, (source, target) in enumerate(((within, within_ref), (last, last_ref))):
+            sends.append(pltpu.make_async_copy(source.at[some], target.at[some], out_sems.at[k, q]))
+            sends[-1].start()
+    for send in sends:
+        send.wait()
 
 
 def contract(values, dense):
@@ -218,18 +234,21 @@
                 o_ref[8 * t : 8 * t + 16, pl.ds(half + i, depth)] = jnp.concatenate(parts, 0).astype(BF16)
 
 
-def call(kernel, name, outs, mib, *args, scratch=(), flops=0, far_off=(), far_out=False):
+def call(kernel, name, outs, mib, *args, scratch=(), flops=0, far_off=(), far_out=False, far_outs=()):
     several = isinstance(outs, tuple)
     size = sum(a.size * a.dtype.itemsize for a in args)
     in_specs = vmem_specs(len(args))
     for k in far_off:
         in_specs[k] = pl.BlockSpec(memory_space=pltpu.HBM)
+    out_specs = vmem_specs(len(outs)) if several else []
+    for k in far_outs:
+        out_specs[k] = pl.BlockSpec(memory_space=pltpu.HBM)
     out_spec = pl.BlockSpec(memory_space=pltpu.HBM if far_out else pltpu.VMEM)
     return pl.pallas_call(
         kernel,
         out_shape=outs,
         in_specs=in_specs,
-        out_specs=tuple(vmem_specs(len(outs))) if several else out_spec,
+        out_specs=tuple(out_specs) if several else out_spec,
         scratch_shapes=list(scratch),
         compiler_params=params(mib),
         cost_estimate=pl.CostEstimate(flops=flops, bytes_accessed=size, transcendentals=0),
@@ -280,7 +299,15 @@
     )
     square = struct((m, m), BF16)
     within, following, last = call(
-        skew_kernel, "skew", (square, square, square), 16, band, flops=m * width
+        skew_kernel, "skew", (square, square, square), 49, band, flops=m * width,
+        far_off=(0,), far_outs=(0, 2),
+        scratch=[
+            pltpu.VMEM((m, width), BF16),
+            pltpu.VMEM((m, m), BF16),
+            pltpu.VMEM((m, m), BF16),
+            pltpu.SemaphoreType.DMA((4,)),
+            pltpu.SemaphoreType.DMA((2, 4)),
+        ],
     )
     thin = struct((rows, m), BF16)
     gathered, following = lax.optimization_barrier((exchange(packed), following))

time: 62.4 us -> 62.3 us (level)
  local copies, waits for them, and re-layouts: 4.83 us -> 1.33 us
  Pallas kernels: 8.04 us -> 10.5 us
  waiting for transfers between devices: 16.1 us -> 17.1 us
    unnamed x12 -> x8, local copies, waits for them, and re-layouts: 4.83 us -> 1.33 us
    pallas_call x10, Pallas kernels: 8.04 us -> 10.5 us  [call(): pl.pallas_call(kernel, out_shape=outs, in_specs=in_specs, out_specs=tuple...]
    all_to_all x1, waiting for transfers between devices: 4.45 us -> 5.5 us  [exchange(): lax.all_to_all(packed.reshape(16, rows // 16, lanes), 'trait', 0, 0, tile...]
  transfers between devices with their start and end apart: 5 -> 5, of which waited for: 3 -> 3; matrix products, arithmetic and copies ran while one was open for 0% -> 0% of each run, Pallas kernels for 6% -> 10%
where the time goes in v10:
time: 62.3 us; the launch traced here: 62 us
  starting transfers between devices  19.2 us (31%)
  waiting for transfers between devices  17.1 us (27%)
  blocking collectives  13.7 us (22%)
  Pallas kernels  10.5 us (17%)
  local copies, waits for them, and re-layouts  1.33 us (2%)
    all_to_all x1, blocking collectives, exchange(): lax.all_to_all(packed.reshape(16, rows // 16, lanes), 'trait', 0, 0, tile...  13.7 us
    ppermute x3, waiting for transfers between devices, passed_along(): return lax.ppermute(shard, ('seg', 'trait'), pairs)  11.6 us
    pallas_call x10, Pallas kernels, call(): pl.pallas_call(kernel, out_shape=outs, in_specs=in_specs, out_specs=tuple...  10.5 us
    ppermute x3, starting transfers between devices, passed_along(): return lax.ppermute(shard, ('seg', 'trait'), pairs)  9.83 us
    all_to_all x1, starting transfers between devices, exchange(): lax.all_to_all(packed.reshape(16, rows // 16, lanes), 'trait', 0, 0, tile...  6.15 us
    all_to_all x1, waiting for transfers between devices, exchange(): lax.all_to_all(packed.reshape(16, rows // 16, lanes), 'trait', 0, 0, tile...  5.5 us
    ppermute x1, starting transfers between devices, traded(): return lax.ppermute(shard, ('seg', 'trait'), pairs)  3.25 us
    unnamed x8, local copies, waits for them, and re-layouts  1.33 us
  transfers between devices with their start and end apart: 5, of which 3 were waited for; matrix products, arithmetic and copies ran while one was open for 0% of the time, Pallas kernels for 10%

profile of v10, /device:TPU:392, one launch (start us, length us, event | category | flops | bytes accessed | tf_op | source)
XLA Modules:
  0.0 62.0 jit_solution(9164486032874017722)
XLA Ops:
  0.0 2.0 %pack.1 = bf16[128,1536]{1,0:T(8,128)(2,1)} custom-call(bf16[192,1024]{1,0:T(8,128)(2,1)} %bitcast.14), custom_call_target="tpu_custom_call" | custom-call | bytes 393216 | tf_op jit(solution)/shard_map/pack/pallas_call | solution.py:247
  2.0 6.1 %all-to-all-start = ((bf16[16,8,1536]{2,1,0:T(8,128)(2,1)}), bf16[16,8,1536]{2,1,0:T(8,128)(2,1)S(1)}, u32[]{:S(2)}, u32[]{:S(2)}) async-start(bf16[16,8,1536]{2,1,0:T(8,128)(2,1)} %bitcast.13), calls=%async_computation | async-start | bytes 786432 | tf_op jit(solution)/shard_map/all_to_all | solution.py:277
  8.1 0.0 copy-start.3
  8.2 3.9 %skew.1 = (bf16[1024,1024]{1,0:T(8,128)(2,1)S(1)}, bf16[1024,1024]{1,0:T(8,128)(2,1)S(1)}, bf16[1024,1024]{1,0:T(8,128)(2,1)}) custom-call(bf16[1024,2048]{1,0:T(8,128)(2,1)} %band_ref.1), custom_call_target="tpu_custom_call" | custom-call | flops 2097152 | bytes 4194304 | tf_op jit(solution)/shard_map/skew/pallas_call | solution.py:247
  12.0 0.0 copy-start.1
  12.0 1.3 %copy-done.1 = bf16[1024,1024]{1,0:T(8,128)(2,1)} copy-done((bf16[1024,1024]{1,0:T(8,128)(2,1)}, bf16[1024,1024]{1,0:T(8,128)(2,1)S(1)}, u32[]{:S(2)}) %copy-start.1) | copy-done | bytes 2097176
  13.4 5.5 %all-to-all-done = bf16[16,8,1536]{2,1,0:T(8,128)(2,1)S(1)} async-done(((bf16[16,8,1536]{2,1,0:T(8,128)(2,1)}), bf16[16,8,1536]{2,1,0:T(8,128)(2,1)S(1)}, u32[]{:S(2)}, u32[]{:S(2)}) %all-to-all-start) | async-done | bytes 393248 | tf_op jit(solution)/shard_map/all_to_all | solution.py:277
  18.9 0.4 mix.1.own_ref.x_ref
  19.3 4.3 %collective-permute-start = (bf16[192,1024]{1,0:T(8,128)(2,1)S(1)}, bf16[192,1024]{1,0:T(8,128)(2,1)S(1)}, u32[]{:S(2)}, u32[]{:S(2)}) collective-permute-start(bf16[192,1024]{1,0:T(8,128)(2,1)S(1)} %mix.1.own_ref.x_ref), channel_id=1, source_target_pairs={{32,0},{33,1},{34,2},{35,3},{36,4},{37,5},{38,6},{39,7},{40,8},{41... | collective-permute-start | bytes 1179656 | tf_op jit(solution)/shard_map/ppermute | solution.py:266
  23.6 0.6 lower_near.1
  24.2 2.6 %collective-permute-start.2 = (bf16[192,1024]{1,0:T(8,128)(2,1)S(1)}, bf16[192,1024]{1,0:T(8,128)(2,1)S(1)}, u32[]{:S(2)}, u32[]{:S(2)}) collective-permute-start(bf16[192,1024]{1,0:T(8,128)(2,1)S(1)} %lower_near.1), channel_id=1, source_target_pairs={{0,16},{1,24},{2,18},{3,26},{4,20},{5,28},{6,22},{7,30},{8,17},{9,... | collective-permute-start | bytes 1179656 | tf_op jit(solution)/shard_map/ppermute | solution.py:266
  26.8 0.0 copy-done
  26.8 0.4 lower_far.1
  27.3 2.9 %collective-permute-start.3 = (bf16[192,1024]{1,0:T(8,128)(2,1)S(1)}, bf16[192,1024]{1,0:T(8,128)(2,1)S(1)}, u32[]{:S(2)}, u32[]{:S(2)}) collective-permute-start(bf16[192,1024]{1,0:T(8,128)(2,1)S(1)} %lower_far.1), channel_id=1, source_target_pairs={{0,32},{1,33},{2,34},{3,35},{4,36},{5,37},{6,38},{7,39},{8,40},{9,... | collective-permute-start | bytes 1179656 | tf_op jit(solution)/shard_map/ppermute | solution.py:266
  30.2 1.6 %collective-permute-done.far_ref.x_ref = bf16[192,1024]{1,0:T(8,128)(2,1)S(1)} collective-permute-done((bf16[192,1024]{1,0:T(8,128)(2,1)S(1)}, bf16[192,1024]{1,0:T(8,128)(2,1)S(1)}, u32[]{:S(2)}, u32[]{:S(2)}) %collective-permute-start) | collective-permute-done | bytes 393248 | tf_op jit(solution)/shard_map/ppermute | solution.py:266
  31.8 3.3 %collective-permute-start.1 = (bf16[192,1024]{1,0:T(8,128)(2,1)S(1)}, bf16[192,1024]{1,0:T(8,128)(2,1)S(1)}, u32[]{:S(2)}, u32[]{:S(2)}) collective-permute-start(bf16[192,1024]{1,0:T(8,128)(2,1)S(1)} %choose.1), channel_id=1, source_target_pairs={{0,16},{1,24},{2,18},{3,26},{4,20},{5,28},{6,22},{7,30},{8,17},{9,... | collective-permute-start | bytes 1179656 | tf_op jit(solution)/shard_map/ppermute | solution.py:272
  35.1 0.8 %own.1.total_ref = f32[192,1024]{1,0:T(8,128)S(1)} custom-call(bf16[192,1024]{1,0:T(8,128)(2,1)S(1)} %mix.1.own_ref.x_ref, bf16[1024,1024]{1,0:T(8,128)(2,1)S(1)} %copy-done.2), custom_call_target="tpu_custom_call" | custom-call | flops 805306368 | bytes 2490368 | tf_op jit(solution)/shard_map/own/pallas_call | solution.py:247
  35.9 0.6 far.1.total_ref
  36.5 0.0 collective-permute-done.2.low_near_ref
  36.5 10.0 %collective-permute-done.3.low_far_ref = bf16[192,1024]{1,0:T(8,128)(2,1)S(1)} collective-permute-done((bf16[192,1024]{1,0:T(8,128)(2,1)S(1)}, bf16[192,1024]{1,0:T(8,128)(2,1)S(1)}, u32[]{:S(2)}, u32[]{:S(2)}) %collective-permute-start.3) | collective-permute-done | bytes 393248 | tf_op jit(solution)/shard_map/ppermute | solution.py:266
  46.5 0.0 collective-permute-done.1.x_ref
  46.5 0.9 %near.1 = bf16[128,1536]{1,0:T(8,128)(2,1)S(1)} custom-call(bf16[192,1024]{1,0:T(8,128)(2,1)S(1)} %collective-permute-done.1.x_ref, bf16[192,1024]{1,0:T(8,128)(2,1)S(1)} %collective-permute-done.2.low_near_ref, bf16[192,1024]{1,0:T(8,128)(2,1)S(1)} %collective-permute-done.3.low_far_ref, bf16[1024,1024]{1,0:T(8,128)(2,1)S(1)} %get-tuple-element.12.dense_ref, ...), custom_call_target="tpu_custom_call" | custom-call | flops 402653184 | bytes 4063232 | tf_op jit(solution)/shard_map/near/pallas_call | solution.py:247
  47.4 13.7 %all_to_all.10 = bf16[16,8,1536]{2,1,0:T(8,128)(2,1)S(1)} all-to-all(bf16[16,8,1536]{2,1,0:T(8,128)(2,1)S(1)} %bitcast.10), channel_id=1, replica_groups=mesh['seg'=32,'trait'=16] {'trait'}, dimensions={0} | all-to-all | bytes 786432 | tf_op jit(solution)/shard_map/all_to_all | solution.py:277
  61.1 0.9 %unpack.1 = bf16[192,1024]{1,0:T(8,128)(2,1)} custom-call(bf16[128,1536]{1,0:T(8,128)(2,1)S(1)} %bitcast.11), custom_call_target="tpu_custom_call" | custom-call | bytes 393216 | tf_op jit(solution)/shard_map/unpack/pallas_call | solution.py:247
  (5 shorter events, 0.0 us)
Async XLA Ops:
  2.0 16.9 %all-to-all-start = ((bf16[16,8,1536]{2,1,0:T(8,128)(2,1)}), bf16[16,8,1536]{2,1,0:T(8,128)(2,1)S(1)}, u32[]{:S(2)}, u32[]{:S(2)}) async-start(bf16[16,8,1536]{2,1,0:T(8,128)(2,1)} %bitcast.13), calls=%async_computation | async-start | bytes 786432 | tf_op jit(solution)/shard_map/all_to_all | solution.py:277
  8.1 10.7 %copy-start.3 = (f32[192,192]{1,0:T(8,128)S(1)}, f32[192,192]{1,0:T(8,128)}, u32[]{:S(2)}) copy-start(f32[192,192]{1,0:T(8,128)} %p_ref.1) | copy-start | bytes 442372
  12.0 1.3 %copy-start.1 = (bf16[1024,1024]{1,0:T(8,128)(2,1)}, bf16[1024,1024]{1,0:T(8,128)(2,1)S(1)}, u32[]{:S(2)}) copy-start(bf16[1024,1024]{1,0:T(8,128)(2,1)S(1)} %get-tuple-element.14.dense_ref) | copy-start | bytes 6291460
  18.9 7.9 %copy-start = (bf16[1024,1024]{1,0:T(8,128)(2,1)S(1)}, bf16[1024,1024]{1,0:T(8,128)(2,1)}, u32[]{:S(2)}) copy-start(bf16[1024,1024]{1,0:T(8,128)(2,1)} %get-tuple-element.13.dense_ref) | copy-start | bytes 6291460
  19.3 12.5 %collective-permute-start = (bf16[192,1024]{1,0:T(8,128)(2,1)S(1)}, bf16[192,1024]{1,0:T(8,128)(2,1)S(1)}, u32[]{:S(2)}, u32[]{:S(2)}) collective-permute-start(bf16[192,1024]{1,0:T(8,128)(2,1)S(1)} %mix.1.own_ref.x_ref), channel_id=1, source_target_pairs={{32,0},{33,1},{34,2},{35,3},{36,4},{37,5},{38,6},{39,7},{40,8},{41... | collective-permute-start | bytes 1179656 | tf_op jit(solution)/shard_map/ppermute | solution.py:266
  24.1 11.0 %copy-start.2 = (bf16[1024,1024]{1,0:T(8,128)(2,1)S(1)}, bf16[1024,1024]{1,0:T(8,128)(2,1)}, u32[]{:S(2)}) copy-start(bf16[1024,1024]{1,0:T(8,128)(2,1)} %copy-done.1) | copy-start | bytes 6291460
  24.2 12.4 %collective-permute-start.2 = (bf16[192,1024]{1,0:T(8,128)(2,1)S(1)}, bf16[192,1024]{1,0:T(8,128)(2,1)S(1)}, u32[]{:S(2)}, u32[]{:S(2)}) collective-permute-start(bf16[192,1024]{1,0:T(8,128)(2,1)S(1)} %lower_near.1), channel_id=1, source_target_pairs={{0,16},{1,24},{2,18},{3,26},{4,20},{5,28},{6,22},{7,30},{8,17},{9,... | collective-permute-start | bytes 1179656 | tf_op jit(solution)/shard_map/ppermute | solution.py:266
  27.3 19.3 %collective-permute-start.3 = (bf16[192,1024]{1,0:T(8,128)(2,1)S(1)}, bf16[192,1024]{1,0:T(8,128)(2,1)S(1)}, u32[]{:S(2)}, u32[]{:S(2)}) collective-permute-start(bf16[192,1024]{1,0:T(8,128)(2,1)S(1)} %lower_far.1), channel_id=1, source_target_pairs={{0,32},{1,33},{2,34},{3,35},{4,36},{5,37},{6,38},{7,39},{8,40},{9,... | collective-permute-start | bytes 1179656 | tf_op jit(solution)/shard_map/ppermute | solution.py:266
  31.8 14.7 %collective-permute-start.1 = (bf16[192,1024]{1,0:T(8,128)(2,1)S(1)}, bf16[192,1024]{1,0:T(8,128)(2,1)S(1)}, u32[]{:S(2)}, u32[]{:S(2)}) collective-permute-start(bf16[192,1024]{1,0:T(8,128)(2,1)S(1)} %choose.1), channel_id=1, source_target_pairs={{0,16},{1,24},{2,18},{3,26},{4,20},{5,28},{6,22},{7,30},{8,17},{9,... | collective-permute-start | bytes 1179656 | tf_op jit(solution)/shard_map/ppermute | solution.py:272
